TPU v7x, 32 devices: a whole 2x2x4 slice. The times are simulated.
32 devices in a mesh: ctx: 16 (over z, x, core), tp: 2 (over y).
Axes of the slice: x: 2, y: 2, z: 4, core: 2. Of those that a mesh axis runs over, the one named last changes fastest.
Arguments:
- features: bfloat16 [8192, 3, 4096], P('ctx', None, 'tp'), may hold values from -6 to 6
- short_filter: float32 [3, 7, 4096], P(None, None, 'tp'), may hold values from -2 to 2
- decay_rate: float32 [16, 4096], P(None, 'tp'), may hold values from 0 to 1, as said below
- residue: float32 [16, 4096], P(None, 'tp'), may hold values from -2 to 2
- skip_gain: float32 [4096], P('tp'), may hold values from -4 to 4
- norm_gain: float32 [4096], replicated, may hold values from 0.1 to 1.9
- qkv_weight: bfloat16 [4096, 3, 2048], P('ctx', None, 'tp'), may hold values from -2 to 2
Outputs:
- mixer: bfloat16 [8192, 4096], P('ctx', 'tp')
- attended: bfloat16 [8192, 2048], P('ctx', 'tp')
Inputs may be any that keep to these rules, and one draw needn't show every extreme that they name: `decay_rate`: decay rates are positive.
All inputs are finite; a program needn't handle non-finite values.
Results may differ from a plain program's by a relative error of at most 0.01.
Values may be sent and summed in bfloat16 or wider, within the bound.
A program may use at most 192 MiB of HBM per device.

v0:
```python
from functools import reduce
import math

import jax
import jax.numpy as jnp
from jax import lax
from jax.sharding import PartitionSpec as P

HD = 128
TAPS = 7
WINDOW = 3


EPSILON = 1e-06
PRECISE = lax.Precision.HIGHEST


def from_behind(value, axis, steps):
    count = lax.axis_size(axis)
    leading, last = (max(0, -steps), min(count, count - steps))
    return lax.ppermute(value, axis, [(source, source + steps) for source in range(leading, last)])


def modal_toeplitz(mixing, decay, block_len):
    distance = jnp.arange(block_len)[:, None] - jnp.arange(block_len)[None, :]
    lag_float = jnp.maximum(distance, 0).astype(jnp.float32)
    channels = mixing.shape[1]
    start = jnp.zeros((channels, block_len, block_len), jnp.float32)

    def add_mode(mode, running):
        weight_row = lax.dynamic_index_in_dim(mixing, mode, 0, keepdims=False)
        rate_row = lax.dynamic_index_in_dim(decay, mode, 0, keepdims=False)
        term = weight_row[:, None, None] * jnp.exp(-rate_row[:, None, None] * lag_float[None])
        return running + term

    summed = lax.fori_loop(0, mixing.shape[0], add_mode, start)
    return jnp.where(distance[None] >= 0, summed, 0.0)


def channel_conv(signal, decay, residue, skip_gain):
    channels, length = signal.shape
    block_len = math.gcd(length, 256)
    block_count = length // block_len
    blocked = signal.reshape(channels, block_count, block_len)
    rate_cols = decay.T
    mode_weights = residue * jnp.sqrt(decay)
    mixing = mode_weights.T
    offsets = jnp.arange(block_len).astype(jnp.float32)
    trailing = jnp.exp(-rate_cols[:, :, None] * (block_len - 1.0 - offsets)[None, None, :])
    block_ends = jnp.einsum("cbs,cns->cnb", blocked, trailing, precision=PRECISE)
    block_ids = jnp.arange(block_count)
    spacing = block_ids[:, None] - 1 - block_ids[None, :]
    powers = (block_len * jnp.maximum(spacing, 0)).astype(jnp.float32)
    carry = jnp.where(
        spacing[None, None] >= 0, jnp.exp(-rate_cols[:, :, None, None] * powers[None, None]), 0.0
    )
    entering = jnp.einsum("cnkb,cnb->cnk", carry, block_ends, precision=PRECISE)
    leading = jnp.exp(-rate_cols[:, :, None] * (offsets + 1.0)[None, None, :])
    across = jnp.einsum("cnk,cns->cks", entering * mixing[:, :, None], leading, precision=PRECISE)
    toeplitz = modal_toeplitz(mode_weights, decay, block_len)
    within = jnp.einsum("cts,cbs->cbt", toeplitz, blocked, precision=PRECISE)
    return (within + across + skip_gain[:, None, None] * blocked).reshape(channels, length)


def on_device(features, short_filter, decay_rate, residue, skip_gain, norm_gain, qkv_weight):
    tok_dev, _, channels = features.shape
    rim_rows = features[tok_dev - (TAPS - 1) :]
    before = from_behind(rim_rows, "ctx", 1)
    extended = jnp.concatenate([before, features], axis=0).astype(jnp.float32)
    short_conv = jnp.zeros((tok_dev, 3, channels), jnp.float32)
    for offset in range(TAPS):
        first_row = TAPS - 1 - offset
        short_conv = (
            short_conv
            + short_filter[:, offset, :][None] * extended[first_row : first_row + tok_dev]
        )
    gated = (short_conv[:, 1] * short_conv[:, 2]).astype(jnp.bfloat16)
    per_device = channels // lax.axis_size("ctx")
    by_channel = lax.all_to_all(gated.T, "ctx", split_axis=0, concat_axis=1, tiled=True)
    first_channel = lax.axis_index("ctx") * per_device
    decay_part = lax.dynamic_slice_in_dim(decay_rate, first_channel, per_device, 1)
    residue_part = lax.dynamic_slice_in_dim(residue, first_channel, per_device, 1)
    skip_part = lax.dynamic_slice_in_dim(skip_gain, first_channel, per_device, 0)
    filtered = channel_conv(
        by_channel.astype(jnp.float32), decay_part, residue_part, skip_part
    ).astype(jnp.bfloat16)
    long_part = lax.all_to_all(filtered, "ctx", split_axis=1, concat_axis=0, tiled=True).T
    mixer = (short_conv[:, 0] * long_part.astype(jnp.float32)).astype(jnp.bfloat16)
    gathered = lax.all_gather(mixer, "tp", axis=1, tiled=True)
    as_float = gathered.astype(jnp.float32)
    inverse = lax.rsqrt(jnp.mean(as_float * as_float, axis=1, keepdims=True) + EPSILON)
    normed = (as_float * inverse * norm_gain[None]).astype(jnp.bfloat16)
    head_cols = qkv_weight.shape[2]
    shard_rows = lax.all_gather(qkv_weight, "ctx", axis=0, tiled=True)
    flat_rows = shard_rows.reshape(shard_rows.shape[0], 3 * head_cols)
    projected = jnp.dot(normed, flat_rows, preferred_element_type=jnp.float32).astype(jnp.bfloat16)
    heads = head_cols // HD
    query = projected[:, :head_cols].reshape(tok_dev, heads, HD)
    kv_pair = projected[:, head_cols:]
    blocks_kv = [kv_pair]
    for lag_step in range(WINDOW - 1):
        blocks_kv.append(from_behind(blocks_kv[-1], "ctx", 1))
    position = lax.axis_index("ctx")
    row_ids = jnp.arange(tok_dev)
    causal = row_ids[:, None] >= row_ids[None, :]
    score_list = []
    for lag_step in range(WINDOW):
        keys = blocks_kv[lag_step][:, :head_cols].reshape(tok_dev, heads, HD)
        scores = jnp.einsum(
            "thd,shd->hts", query, keys, preferred_element_type=jnp.float32
        ) / math.sqrt(HD)
        if lag_step == 0:
            allowed = causal
        else:
            allowed = jnp.broadcast_to(position >= lag_step, causal.shape)
        score_list.append(jnp.where(allowed[None], scores, -jnp.inf))
    peak = reduce(jnp.maximum, [jnp.max(entry, axis=2) for entry in score_list])
    total = jnp.zeros((heads, tok_dev), jnp.float32)
    output = jnp.zeros((tok_dev, heads, HD), jnp.float32)
    for lag_step in range(WINDOW):
        expo = jnp.exp(score_list[lag_step] - peak[:, :, None])
        total = total + jnp.sum(expo, axis=2)
        values = blocks_kv[lag_step][:, head_cols:].reshape(tok_dev, heads, HD)
        output = output + jnp.einsum(
            "hts,shd->thd", expo.astype(jnp.bfloat16), values, preferred_element_type=jnp.float32
        )
    attended = (output / total.T[:, :, None]).astype(jnp.bfloat16).reshape(tok_dev, head_cols)
    return (mixer, attended)


def solution(mesh):
    placed = (
        P("ctx", None, "tp"),
        P(None, None, "tp"),
        P(None, "tp"),
        P(None, "tp"),
        P("tp"),
        P(),
        P("ctx", None, "tp"),
    )
    return jax.shard_map(
        on_device,
        mesh=mesh,
        in_specs=placed,
        out_specs=(P("ctx", "tp"), P("ctx", "tp")),
        check_vma=False,
    )
```

profile of v0, /device:TPU:16, one launch (start us, length us, event | category | flops | bytes accessed | tf_op | source)
XLA Modules:
  0.0 951.8 jit_solution(4151889254535404088)
XLA Ops:
  7.2 0.9 slice.81
  8.1 1.9 collective-permute-start
  10.0 2.0 fusion.88
  13.6 1.4 collective-permute-done
  14.9 9.2 maximum_convert_fusion.1
  24.1 35.1 %fusion.6 = f32[512,3,2048]{2,0,1:T(8,128)} fusion(f32[518,3,2048]{2,0,1:T(8,128)} %maximum_convert_fusion.1, f32[3,2048]{1,0:T(4,128)S(1)} %get-tuple-element.157, f32[3,2048]{1,0:T(4,128)S(1)} %get-tuple-element.158, f32[3,2048]{1,0:T(4,128)S(1)} %get-tuple-element.159, f32[3,2048]{1,0:T(4,128)S(1)} %get-tuple-element.160, ...), kind=kLoop, calls=%fused_computation.10 | loop fusion | flops 40894464 | bytes 100835328 | tf_op jit(solution)/shard_map/add | solution.py:74
  59.2 4.1 fusion.48
  63.3 2.5 copy.67
  65.8 5.3 all-to-all-start
  71.6 380.7 %while.14 = (s32[]{:T(128)}, f32[128,256,256]{2,1,0:T(8,128)}, f32[16,128]{1,0:T(8,128)S(1)}, f32[16,128]{1,0:T(8,128)S(1)}, s32[]{:T(128)}, /*index=5*/s32[]{:T(128)}) while((s32[]{:T(128)}, f32[128,256,256]{2,1,0:T(8,128)}, f32[16,128]{1,0:T(8,128)S(1)}, f32[16,128]{1,0:T(8,128)S(1)}, s32[]{:T(128)}, /*index=5*/s32[]{:T(128)}) %tuple.62), condition=%wide.region_1.2_spmd.clone, body=%wide.region_0.1_spmd.clone.sunk | while | flops 33751168 | bytes 67636304 | solution.py:36
  71.6 12.7 %select_add_fusion.2 = f32[128,256,256]{2,1,0:T(8,128)} fusion(f32[128,256,256]{2,1,0:T(8,128)} %get-tuple-element.199, f32[256,256]{1,0:T(8,128)S(1)} %maximum_convert_fusion.3, f32[128]{0:T(128)S(1)} %get-tuple-element.190, f32[128]{0:T(128)S(1)} %get-tuple-element.191, pred[]{:T(512)S(6)} %compare.3), kind=kLoop, calls=%fused_computation.1.clone.1 | loop fusion | flops 33554432 | bytes 67372032 | tf_op jit(solution)/shard_map/while/body/eval_jaxpr/add | solution.py:34
  84.4 24.5 %select_add_fusion.2 = f32[128,256,256]{2,1,0:T(8,128)} fusion(f32[128,256,256]{2,1,0:T(8,128)} %get-tuple-element.199, f32[256,256]{1,0:T(8,128)S(1)} %maximum_convert_fusion.3, f32[128]{0:T(128)S(1)} %get-tuple-element.190, f32[128]{0:T(128)S(1)} %get-tuple-element.191, pred[]{:T(512)S(6)} %compare.3), kind=kLoop, calls=%fused_computation.1.clone.1 | loop fusion | flops 33554432 | bytes 67372032 | tf_op jit(solution)/shard_map/while/body/eval_jaxpr/add | solution.py:34
  108.9 24.5 %select_add_fusion.2 = f32[128,256,256]{2,1,0:T(8,128)} fusion(f32[128,256,256]{2,1,0:T(8,128)} %get-tuple-element.199, f32[256,256]{1,0:T(8,128)S(1)} %maximum_convert_fusion.3, f32[128]{0:T(128)S(1)} %get-tuple-element.190, f32[128]{0:T(128)S(1)} %get-tuple-element.191, pred[]{:T(512)S(6)} %compare.3), kind=kLoop, calls=%fused_computation.1.clone.1 | loop fusion | flops 33554432 | bytes 67372032 | tf_op jit(solution)/shard_map/while/body/eval_jaxpr/add | solution.py:34
  133.4 24.5 %select_add_fusion.2 = f32[128,256,256]{2,1,0:T(8,128)} fusion(f32[128,256,256]{2,1,0:T(8,128)} %get-tuple-element.199, f32[256,256]{1,0:T(8,128)S(1)} %maximum_convert_fusion.3, f32[128]{0:T(128)S(1)} %get-tuple-element.190, f32[128]{0:T(128)S(1)} %get-tuple-element.191, pred[]{:T(512)S(6)} %compare.3), kind=kLoop, calls=%fused_computation.1.clone.1 | loop fusion | flops 33554432 | bytes 67372032 | tf_op jit(solution)/shard_map/while/body/eval_jaxpr/add | solution.py:34
  158.0 24.5 %select_add_fusion.2 = f32[128,256,256]{2,1,0:T(8,128)} fusion(f32[128,256,256]{2,1,0:T(8,128)} %get-tuple-element.199, f32[256,256]{1,0:T(8,128)S(1)} %maximum_convert_fusion.3, f32[128]{0:T(128)S(1)} %get-tuple-element.190, f32[128]{0:T(128)S(1)} %get-tuple-element.191, pred[]{:T(512)S(6)} %compare.3), kind=kLoop, calls=%fused_computation.1.clone.1 | loop fusion | flops 33554432 | bytes 67372032 | tf_op jit(solution)/shard_map/while/body/eval_jaxpr/add | solution.py:34
  182.5 24.5 %select_add_fusion.2 = f32[128,256,256]{2,1,0:T(8,128)} fusion(f32[128,256,256]{2,1,0:T(8,128)} %get-tuple-element.199, f32[256,256]{1,0:T(8,128)S(1)} %maximum_convert_fusion.3, f32[128]{0:T(128)S(1)} %get-tuple-element.190, f32[128]{0:T(128)S(1)} %get-tuple-element.191, pred[]{:T(512)S(6)} %compare.3), kind=kLoop, calls=%fused_computation.1.clone.1 | loop fusion | flops 33554432 | bytes 67372032 | tf_op jit(solution)/shard_map/while/body/eval_jaxpr/add | solution.py:34
  207.0 24.5 %select_add_fusion.2 = f32[128,256,256]{2,1,0:T(8,128)} fusion(f32[128,256,256]{2,1,0:T(8,128)} %get-tuple-element.199, f32[256,256]{1,0:T(8,128)S(1)} %maximum_convert_fusion.3, f32[128]{0:T(128)S(1)} %get-tuple-element.190, f32[128]{0:T(128)S(1)} %get-tuple-element.191, pred[]{:T(512)S(6)} %compare.3), kind=kLoop, calls=%fused_computation.1.clone.1 | loop fusion | flops 33554432 | bytes 67372032 | tf_op jit(solution)/shard_map/while/body/eval_jaxpr/add | solution.py:34
  231.6 24.5 %select_add_fusion.2 = f32[128,256,256]{2,1,0:T(8,128)} fusion(f32[128,256,256]{2,1,0:T(8,128)} %get-tuple-element.199, f32[256,256]{1,0:T(8,128)S(1)} %maximum_convert_fusion.3, f32[128]{0:T(128)S(1)} %get-tuple-element.190, f32[128]{0:T(128)S(1)} %get-tuple-element.191, pred[]{:T(512)S(6)} %compare.3), kind=kLoop, calls=%fused_computation.1.clone.1 | loop fusion | flops 33554432 | bytes 67372032 | tf_op jit(solution)/shard_map/while/body/eval_jaxpr/add | solution.py:34
  256.1 24.5 %select_add_fusion.2 = f32[128,256,256]{2,1,0:T(8,128)} fusion(f32[128,256,256]{2,1,0:T(8,128)} %get-tuple-element.199, f32[256,256]{1,0:T(8,128)S(1)} %maximum_convert_fusion.3, f32[128]{0:T(128)S(1)} %get-tuple-element.190, f32[128]{0:T(128)S(1)} %get-tuple-element.191, pred[]{:T(512)S(6)} %compare.3), kind=kLoop, calls=%fused_computation.1.clone.1 | loop fusion | flops 33554432 | bytes 67372032 | tf_op jit(solution)/shard_map/while/body/eval_jaxpr/add | solution.py:34
  280.6 24.5 %select_add_fusion.2 = f32[128,256,256]{2,1,0:T(8,128)} fusion(f32[128,256,256]{2,1,0:T(8,128)} %get-tuple-element.199, f32[256,256]{1,0:T(8,128)S(1)} %maximum_convert_fusion.3, f32[128]{0:T(128)S(1)} %get-tuple-element.190, f32[128]{0:T(128)S(1)} %get-tuple-element.191, pred[]{:T(512)S(6)} %compare.3), kind=kLoop, calls=%fused_computation.1.clone.1 | loop fusion | flops 33554432 | bytes 67372032 | tf_op jit(solution)/shard_map/while/body/eval_jaxpr/add | solution.py:34
  305.1 24.5 %select_add_fusion.2 = f32[128,256,256]{2,1,0:T(8,128)} fusion(f32[128,256,256]{2,1,0:T(8,128)} %get-tuple-element.199, f32[256,256]{1,0:T(8,128)S(1)} %maximum_convert_fusion.3, f32[128]{0:T(128)S(1)} %get-tuple-element.190, f32[128]{0:T(128)S(1)} %get-tuple-element.191, pred[]{:T(512)S(6)} %compare.3), kind=kLoop, calls=%fused_computation.1.clone.1 | loop fusion | flops 33554432 | bytes 67372032 | tf_op jit(solution)/shard_map/while/body/eval_jaxpr/add | solution.py:34
  329.7 24.5 %select_add_fusion.2 = f32[128,256,256]{2,1,0:T(8,128)} fusion(f32[128,256,256]{2,1,0:T(8,128)} %get-tuple-element.199, f32[256,256]{1,0:T(8,128)S(1)} %maximum_convert_fusion.3, f32[128]{0:T(128)S(1)} %get-tuple-element.190, f32[128]{0:T(128)S(1)} %get-tuple-element.191, pred[]{:T(512)S(6)} %compare.3), kind=kLoop, calls=%fused_computation.1.clone.1 | loop fusion | flops 33554432 | bytes 67372032 | tf_op jit(solution)/shard_map/while/body/eval_jaxpr/add | solution.py:34
  354.2 24.5 %select_add_fusion.2 = f32[128,256,256]{2,1,0:T(8,128)} fusion(f32[128,256,256]{2,1,0:T(8,128)} %get-tuple-element.199, f32[256,256]{1,0:T(8,128)S(1)} %maximum_convert_fusion.3, f32[128]{0:T(128)S(1)} %get-tuple-element.190, f32[128]{0:T(128)S(1)} %get-tuple-element.191, pred[]{:T(512)S(6)} %compare.3), kind=kLoop, calls=%fused_computation.1.clone.1 | loop fusion | flops 33554432 | bytes 67372032 | tf_op jit(solution)/shard_map/while/body/eval_jaxpr/add | solution.py:34
  378.7 24.5 %select_add_fusion.2 = f32[128,256,256]{2,1,0:T(8,128)} fusion(f32[128,256,256]{2,1,0:T(8,128)} %get-tuple-element.199, f32[256,256]{1,0:T(8,128)S(1)} %maximum_convert_fusion.3, f32[128]{0:T(128)S(1)} %get-tuple-element.190, f32[128]{0:T(128)S(1)} %get-tuple-element.191, pred[]{:T(512)S(6)} %compare.3), kind=kLoop, calls=%fused_computation.1.clone.1 | loop fusion | flops 33554432 | bytes 67372032 | tf_op jit(solution)/shard_map/while/body/eval_jaxpr/add | solution.py:34
  403.2 24.5 %select_add_fusion.2 = f32[128,256,256]{2,1,0:T(8,128)} fusion(f32[128,256,256]{2,1,0:T(8,128)} %get-tuple-element.199, f32[256,256]{1,0:T(8,128)S(1)} %maximum_convert_fusion.3, f32[128]{0:T(128)S(1)} %get-tuple-element.190, f32[128]{0:T(128)S(1)} %get-tuple-element.191, pred[]{:T(512)S(6)} %compare.3), kind=kLoop, calls=%fused_computation.1.clone.1 | loop fusion | flops 33554432 | bytes 67372032 | tf_op jit(solution)/shard_map/while/body/eval_jaxpr/add | solution.py:34
  427.8 24.5 %select_add_fusion.2 = f32[128,256,256]{2,1,0:T(8,128)} fusion(f32[128,256,256]{2,1,0:T(8,128)} %get-tuple-element.199, f32[256,256]{1,0:T(8,128)S(1)} %maximum_convert_fusion.3, f32[128]{0:T(128)S(1)} %get-tuple-element.190, f32[128]{0:T(128)S(1)} %get-tuple-element.191, pred[]{:T(512)S(6)} %compare.3), kind=kLoop, calls=%fused_computation.1.clone.1 | loop fusion | flops 33554432 | bytes 67372032 | tf_op jit(solution)/shard_map/while/body/eval_jaxpr/add | solution.py:34
  452.5 4.1 exponential_select_fusion
  456.6 26.3 %copy.87 = f32[128,16,32,32]{3,2,1,0:T(8,128)} copy(f32[128,16,32,32]{0,3,2,1:T(8,128)} %exponential_select_fusion) | data formatting | bytes 16777216 | tf_op jit(solution)/shard_map/jit(_where)/select_n | solution.py:54
  483.0 0.8 dynamic_slice.26
  483.8 2.5 copy.68
  486.3 2.7 reshape.174
  489.0 23.2 %fusion.2 = f32[128,32,256]{2,1,0:T(8,128)} fusion(bf16[128,32,256]{2,1,0:T(8,128)(2,1)S(1)} %reshape.174, f32[128,256,256]{2,1,0:T(8,128)} %get-tuple-element.96, pred[256,256]{1,0:T(8,128)(4,1)S(1)} %subtract_compare_fusion), kind=kOutput, calls=%fused_computation.5 | convolution fusion | flops 3229614080 | bytes 39911424 | tf_op jit(solution)/shard_map/cts,cbs->cbt/dot_general | solution.py:61
  512.2 1.8 fusion.52
  514.0 56.1 %fusion.89 = f32[128,16,1,32]{3,2,1,0:T(1,128)S(1)} fusion(f32[128,16,32,32]{3,2,1,0:T(8,128)} %copy.87, f32[128,16,32,1]{2,3,1,0:T(1,128)S(1)} %bitcast.107), kind=kOutput, calls=%fused_computation.132 | convolution fusion | flops 25165824 | bytes 8912896 | tf_op jit(solution)/shard_map/cnkb,cnb->cnk/dot_general | solution.py:57
  570.1 6.6 add_convert_fusion
  576.7 2.7 convert_element_type.86
  579.4 1.2 copy.71
  580.5 53.4 %all_to_all.26 = bf16[128,16,512]{2,0,1:T(8,128)(2,1)S(1)} all-to-all(bf16[128,16,512]{2,0,1:T(8,128)(2,1)S(1)} %copy.71), channel_id=1, replica_groups=mesh['ctx'=16,'tp'=2] {'ctx'}, dimensions={1} | all-to-all | bytes 4194304 | tf_op jit(solution)/shard_map/all_to_all | solution.py:87
  634.0 2.5 convert_element_type.101
  636.5 5.4 copy.72
  641.9 5.5 fusion.33
  647.5 1.6 copy.73
  649.1 55.0 %all-gather.3.cloned.1.call-done = bf16[512,4096]{1,0:T(8,128)(2,1)} async-done(((bf16[512,2048]{1,0:T(8,128)(2,1)}), bf16[512,4096]{1,0:T(8,128)(2,1)}) %all-gather.3.cloned.1.call-update) | async-done | bytes 4194320 | tf_op jit(solution)/shard_map/all_gather | solution.py:89
  704.1 3.1 fusion.12
  707.1 134.0 %all-gather.5.cloned.1.call-done = bf16[4096,3,1024]{0,2,1:T(8,128)(2,1)} async-done(((bf16[256,3,1024]{0,2,1:T(8,128)(2,1)}), bf16[4096,3,1024]{0,2,1:T(8,128)(2,1)}) %all-gather.5.cloned.1.call-update) | async-done | bytes 25165840 | tf_op jit(solution)/shard_map/all_gather | solution.py:94
  841.2 18.3 %convolution_convert_fusion = bf16[512,3072]{1,0:T(8,128)(2,1)S(1)} fusion(bf16[4096,3072]{0,1:T(8,128)(2,1)} %bitcast.114, bf16[512,4096]{1,0:T(8,128)(2,1)} %all-gather.3.cloned.1.call-done, f32[4096]{0:T(1024)S(1)} %copy-done.6, f32[512]{0:T(512)S(1)} %add_rsqrt_fusion), kind=kOutput, calls=%fused_computation.44 | convolution fusion | flops 12894863360 | bytes 32524288 | tf_op jit(solution)/shard_map/dot_general | solution.py:96
  859.6 2.2 collective-permute-start.1
  861.8 26.2 %collective-permute-done.1 = bf16[512,2048]{1,0:T(8,128)(2,1)} collective-permute-done((bf16[512,2048]{1,0:T(8,128)(2,1)S(1)}, bf16[512,2048]{1,0:T(8,128)(2,1)}, u32[]{:S(2)}, u32[]{:S(2)}) %collective-permute-start.1) | collective-permute-done | bytes 2097184 | tf_op jit(solution)/shard_map/ppermute | solution.py:21
  888.0 1.9 collective-permute-start.2
  890.0 1.7 slice_bitcast_fusion.4
  891.7 2.5 copy.93
  894.2 6.2 fusion.15
  900.5 2.8 fusion.87
  903.2 1.3 copy.94
  904.5 2.9 fusion.16
  907.5 9.1 collective-permute-done.2
  916.5 2.8 fusion.86
  919.3 1.3 fusion.17
  920.6 3.3 fusion.26
  923.9 2.1 slice-done.1
  925.9 5.0 fusion.20
  931.0 4.9 fusion.28
  936.5 6.7 fusion.49
  943.2 1.3 copy.86
  (76 shorter events, 3.9 us)
Async XLA Ops:
  8.1 6.8 collective-permute-start
  65.8 418.0 %all-to-all-start = ((bf16[16,128,512]{2,1,0:T(8,128)(2,1)}), bf16[16,128,512]{2,1,0:T(8,128)(2,1)S(1)}, u32[]{:S(2)}, u32[]{:S(2)}) async-start(bf16[16,128,512]{2,1,0:T(8,128)(2,1)} %bitcast.105), calls=%async_computation | async-start | bytes 4194304 | tf_op jit(solution)/shard_map/all_to_all | solution.py:79
  71.0 633.0 %all-gather.3.cloned.1.call-start = ((), (), s32[]{:S(2)}) async-start(), calls=%async_computation.2 | async-start | bytes 6291456 | tf_op jit(solution)/shard_map/all_gather | solution.py:89
  514.0 56.1 %copy-start = (f32[128,32,256]{2,1,0:T(8,128)S(1)}, f32[128,32,256]{2,1,0:T(8,128)}, u32[]{:S(2)}) copy-start(f32[128,32,256]{2,1,0:T(8,128)} %fusion.2) | copy-start | bytes 12582916
  641.9 5.6 copy-start.3
  641.9 199.3 %copy-start.6 = (f32[4096]{0:T(1024)S(1)}, f32[4096]{0:T(1024)}, u32[]{:S(2)}) copy-start(f32[4096]{0:T(1024)} %param.14) | copy-start | bytes 49156
  647.4 193.8 %all-gather.5.cloned.1.call-start = ((), (), s32[]{:S(2)}) async-start(), calls=%async_computation.3 | async-start | bytes 26738688 | tf_op jit(solution)/shard_map/all_gather | solution.py:94
  859.6 28.4 %collective-permute-start.1 = (bf16[512,2048]{1,0:T(8,128)(2,1)S(1)}, bf16[512,2048]{1,0:T(8,128)(2,1)}, u32[]{:S(2)}, u32[]{:S(2)}) collective-permute-start(bf16[512,2048]{1,0:T(8,128)(2,1)S(1)} %slice.119), channel_id=1, source_target_pairs={{0,2},{2,4},{4,6},{6,8},{8,10},{10,12},{12,14},{14,16},{16,18},{18... | collective-permute-start | bytes 6291464 | tf_op jit(solution)/shard_map/ppermute | solution.py:21
  888.0 28.6 %collective-permute-start.2 = (bf16[512,2048]{1,0:T(8,128)(2,1)}, bf16[512,2048]{1,0:T(8,128)(2,1)}, u32[]{:S(2)}, u32[]{:S(2)}) collective-permute-start(bf16[512,2048]{1,0:T(8,128)(2,1)} %collective-permute-done.1), channel_id=1, source_target_pairs={{0,2},{2,4},{4,6},{6,8},{8,10},{10,12},{12,14},{14,16},{16,18},{18... | collective-permute-start | bytes 6291464 | tf_op jit(solution)/shard_map/ppermute | solution.py:21
  904.5 14.7 %copy-start.5 = (bf16[64,8,8,128]{3,2,1,0:T(8,128)(2,1)S(1)}, bf16[64,8,8,128]{3,2,1,0:T(8,128)(2,1)}, u32[]{:S(2)}) copy-start(bf16[64,8,8,128]{3,2,1,0:T(8,128)(2,1)} %get-tuple-element.137) | copy-start | bytes 3145732
  907.4 13.1 %copy-start.4 = (bf16[512,1024]{0,1:T(8,128)(2,1)S(1)}, bf16[512,1024]{0,1:T(8,128)(2,1)}, u32[]{:S(2)}) copy-start(bf16[512,1024]{0,1:T(8,128)(2,1)} %copy.94) | copy-start | bytes 3145732
  919.3 4.6 slice-start
  920.6 10.4 %copy-start.1 = (f32[8,512,512]{1,2,0:T(8,128)}, f32[8,512,512]{1,2,0:T(8,128)S(1)}, u32[]{:S(2)}) copy-start(f32[8,512,512]{1,2,0:T(8,128)S(1)} %get-tuple-element.152) | copy-start | bytes 25165828
  920.6 5.3 slice-start.1
  931.0 4.9 copy-start.2
Sparse Core Ops, SparseCore 0:
  647.5 56.4 all-gather.2
  705.6 135.5 all-gather.4
where the time goes:
time: 960 us; the launch traced here: 952 us
  other arithmetic  451 us (47%)
  waiting for transfers between devices  226 us (24%)
  matrix products  131 us (14%)
  local copies, waits for them, and re-layouts  63.9 us (7%)
  blocking collectives  53.4 us (6%)
  between operations  14.8 us (2%)
  starting transfers between devices  11.8 us (1%)
    add x16, other arithmetic, add_mode(): return running + term  380 us
    all_gather x1, waiting for transfers between devices, on_device(): shard_rows = lax.all_gather(qkv_weight, 'ctx', axis=0, tiled=True)  134 us
    dot_general x1, matrix products, channel_conv(): entering = jnp.einsum('cnkb,cnb->cnk', carry, block_ends, precision=PRECISE)  56.1 us
    all_gather x1, waiting for transfers between devices, on_device(): gathered = lax.all_gather(mixer, 'tp', axis=1, tiled=True)  55 us
    all_to_all x1, blocking collectives, on_device(): lax.all_to_all(filtered, 'ctx', split_axis=1, concat_axis=0, tiled=True)  53.4 us
    ppermute x3, waiting for transfers between devices, from_behind(): lax.ppermute(value, axis, [(source, source + steps) for source in range(l...  36.6 us
    add x1, other arithmetic, on_device(): short_conv + short_filter[:, offset, :][None] * extended[first_row:first_...  35.1 us
    select_n x1, local copies, waits for them, and re-layouts, channel_conv(): jnp.where(spacing[None, None] >= 0, jnp.exp(-rate_cols[:, :, None, None]...  26.3 us
  transfers between devices with their start and end apart: 6, of which 5 were waited for; matrix products, arithmetic and copies ran while one was open for 46% of the time, Pallas kernels for 0%

commit v1 on v0

v1 whole, which is shorter than its diff:
```python
import functools
import math

import jax
import jax.numpy as jnp
from jax import lax
from jax.experimental import pallas as pl
from jax.experimental.pallas import tpu as pltpu
from jax.sharding import PartitionSpec as P

HD = 128
TAPS = 7
WINDOW = 3
EPSILON = 1e-06
LANES = 128
SEGMENTS = 8
HALO = 16
RADIX = 4
MIB = 1 << 20


def shifted(value, axis, steps):
    count = lax.axis_size(axis)
    return lax.ppermute(value, axis, [(source, source + steps) for source in range(count - steps)])


def mode_rows(values, modes):
    return [jnp.broadcast_to(values[n : n + 1], (SEGMENTS, LANES)) for n in range(modes)]


def short_kernel(feat_ref, halo_ref, taps_ref, decay_ref, gated_ref, first_ref, enter_ref, end_ref, ext, gs, ends):
    tokens = feat_ref.shape[1]
    seg = tokens // SEGMENTS
    modes = decay_ref.shape[0]
    streams = []
    for j in range(3):
        ext[j, :HALO] = halo_ref[j].astype(jnp.float32)
        ext[j, HALO:] = feat_ref[j].astype(jnp.float32)
        total = taps_ref[j, 0:1] * ext[j, HALO:]
        for i in range(1, TAPS):
            total = total + taps_ref[j, i : i + 1] * ext[j, HALO - i : HALO - i + tokens]
        if j == 0:
            first_ref[...] = total
        elif j == 1:
            gs[...] = total
        else:
            gated = (gs[...] * total).astype(jnp.bfloat16)
    gated_ref[...] = gated
    gs[...] = gated.astype(jnp.float32)
    rate = decay_ref[...]
    decays = mode_rows(jnp.exp(-rate), modes)

    def step(t, states):
        g = gs[pl.ds(t, SEGMENTS, stride=seg), :]
        return tuple(a * s + g for a, s in zip(decays, states))

    zero = jnp.zeros((SEGMENTS, LANES), jnp.float32)
    states = lax.fori_loop(0, seg, step, (zero,) * modes, unroll=8)
    for n in range(modes):
        ends[n * SEGMENTS : (n + 1) * SEGMENTS] = states[n]
    across = jnp.exp(-float(seg) * rate)
    entering = jnp.zeros((modes, LANES), jnp.float32)
    for j in range(SEGMENTS):
        enter_ref[j] = entering
        entering = across * entering + ends[pl.ds(j, modes, stride=SEGMENTS), :]
    end_ref[...] = entering


def long_kernel(gated_ref, first_ref, enter_ref, state_ref, decay_ref, residue_ref, skip_ref, mixer_ref, gs, ys, starts):
    tokens = gated_ref.shape[0]
    seg = tokens // SEGMENTS
    modes = decay_ref.shape[0]
    rate = decay_ref[...]
    gs[...] = gated_ref[...].astype(jnp.float32)
    for j in range(SEGMENTS):
        starts[j * modes : (j + 1) * modes] = enter_ref[j] + jnp.exp(-float(j * seg) * rate) * state_ref[...]
    decays = mode_rows(jnp.exp(-rate), modes)
    weights = mode_rows(residue_ref[...] * jnp.sqrt(rate), modes)
    skip = jnp.broadcast_to(skip_ref[...], (SEGMENTS, LANES))

    def step(t, states):
        g = gs[pl.ds(t, SEGMENTS, stride=seg), :]
        states = tuple(a * s + g for a, s in zip(decays, states))
        terms = [w * s for w, s in zip(weights, states)]
        while len(terms) > 1:
            terms = [sum(terms[i : i + 2]) for i in range(0, len(terms), 2)]
        ys[pl.ds(t, SEGMENTS, stride=seg), :] = terms[0] + skip * g
        return states

    first = tuple(starts[pl.ds(n, SEGMENTS, stride=modes), :] for n in range(modes))
    lax.fori_loop(0, seg, step, first, unroll=8)
    filtered = ys[...].astype(jnp.bfloat16).astype(jnp.float32)
    mixer_ref[...] = (first_ref[...] * filtered).astype(jnp.bfloat16)


def short_part(features, halo, short_filter, decay_rate):
    _, tokens, channels = features.shape
    modes = decay_rate.shape[0]
    f32 = jnp.float32
    return pl.pallas_call(
        short_kernel,
        grid=(channels // LANES,),
        in_specs=[
            pl.BlockSpec((3, tokens, LANES), lambda c: (0, 0, c)),
            pl.BlockSpec((3, HALO, LANES), lambda c: (0, 0, c)),
            pl.BlockSpec((3, TAPS, LANES), lambda c: (0, 0, c)),
            pl.BlockSpec((modes, LANES), lambda c: (0, c)),
        ],
        out_specs=[
            pl.BlockSpec((tokens, LANES), lambda c: (0, c)),
            pl.BlockSpec((tokens, LANES), lambda c: (0, c)),
            pl.BlockSpec((SEGMENTS, modes, LANES), lambda c: (0, 0, c)),
            pl.BlockSpec((modes, LANES), lambda c: (0, c)),
        ],
        out_shape=[
            jax.ShapeDtypeStruct((tokens, channels), jnp.bfloat16),
            jax.ShapeDtypeStruct((tokens, channels), f32),
            jax.ShapeDtypeStruct((SEGMENTS, modes, channels), f32),
            jax.ShapeDtypeStruct((modes, channels), f32),
        ],
        scratch_shapes=[
            pltpu.VMEM((3, HALO + tokens, LANES), f32),
            pltpu.VMEM((tokens, LANES), f32),
            pltpu.VMEM((modes * SEGMENTS, LANES), f32),
        ],
        compiler_params=pltpu.CompilerParams(vmem_limit_bytes=24 * MIB),
        cost_estimate=pl.CostEstimate(flops=100 * tokens * channels, bytes_accessed=13 * tokens * channels, transcendentals=0),
        name="short_and_end_states",
    )(features, halo, short_filter, decay_rate)


def long_part(gated, first, enter, state, decay_rate, residue, skip_gain):
    tokens, channels = gated.shape
    modes = decay_rate.shape[0]
    f32 = jnp.float32
    by_token = pl.BlockSpec((tokens, LANES), lambda c: (0, c))
    by_mode = pl.BlockSpec((modes, LANES), lambda c: (0, c))
    return pl.pallas_call(
        long_kernel,
        grid=(channels // LANES,),
        in_specs=[
            by_token,
            by_token,
            pl.BlockSpec((SEGMENTS, modes, LANES), lambda c: (0, 0, c)),
            by_mode,
            by_mode,
            by_mode,
            pl.BlockSpec((1, LANES), lambda c: (0, c)),
        ],
        out_specs=by_token,
        out_shape=jax.ShapeDtypeStruct((tokens, channels), jnp.bfloat16),
        scratch_shapes=[
            pltpu.VMEM((tokens, LANES), f32),
            pltpu.VMEM((tokens, LANES), f32),
            pltpu.VMEM((SEGMENTS * modes, LANES), f32),
        ],
        compiler_params=pltpu.CompilerParams(vmem_limit_bytes=24 * MIB),
        cost_estimate=pl.CostEstimate(flops=100 * tokens * channels, bytes_accessed=10 * tokens * channels, transcendentals=0),
        name="modal_filter",
    )(gated, first, enter, state, decay_rate, residue, skip_gain[None])


def entering_states(ends, decay_rate, tokens):
    count = lax.axis_size("ctx")

    def power(k):
        return jnp.exp(-float(k * tokens) * decay_rate)

    near = shifted(ends, "ctx", 1)
    for j in range(2, min(RADIX, count - 1) + 1):
        near = near + power(j - 1) * shifted(ends, "ctx", j)
    state = near
    for m in range(RADIX, count, RADIX):
        state = state + power(m) * shifted(near, "ctx", m)
    return state


def normed_product(place_ref, *refs, pieces, steps):
    x_refs, (gain_ref, w_ref, out_ref, normed_ref, acc) = refs[:pieces], refs[pieces:]
    stream, k = pl.program_id(0), pl.program_id(1)
    per_piece = x_refs[0].shape[1]
    rows = w_ref.shape[0] * w_ref.shape[2]

    @pl.when((stream == 0) & (k == 0))
    def _():
        squares = 0.0
        for x_ref in x_refs:
            as_float = x_ref[...].astype(jnp.float32)
            squares = squares + jnp.sum(as_float * as_float, axis=1, keepdims=True)
        inverse = lax.rsqrt(squares / (pieces * per_piece) + EPSILON)
        for p, x_ref in enumerate(x_refs):
            at = lax.rem(place_ref[0] + p, pieces)
            gain = gain_ref[pl.ds(at, 1), :]
            scaled = (x_ref[...].astype(jnp.float32) * inverse * gain).astype(jnp.bfloat16)
            for part in range(per_piece // rows):
                normed_ref[p * (per_piece // rows) + part] = scaled[:, part * rows : (part + 1) * rows]

    weights = w_ref[:, 0].reshape(rows, w_ref.shape[3])
    term = jnp.dot(normed_ref[k], weights, preferred_element_type=jnp.float32)

    @pl.when(k == 0)
    def _():
        acc[...] = term

    @pl.when(k > 0)
    def _():
        acc[...] += term

    @pl.when(k == steps - 1)
    def _():
        out_ref[0] = acc[...].astype(jnp.bfloat16)


def product_only(place_ref, x_ref, w_ref, out_ref, acc, *, steps):
    k = pl.program_id(1)
    rows = w_ref.shape[0] * w_ref.shape[2]
    weights = w_ref[:, 0].reshape(rows, w_ref.shape[3])
    term = jnp.dot(x_ref[0], weights, preferred_element_type=jnp.float32)

    @pl.when(k == 0)
    def _():
        acc[...] = term

    @pl.when(k > 0)
    def _():
        acc[...] += term

    @pl.when(k == steps - 1)
    def _():
        out_ref[0] = acc[...].astype(jnp.bfloat16)


def weight_group(weights, pieces):
    shards, _, rows, _ = weights.shape
    return math.gcd(4, shards // pieces), rows


def project_first(place, xs, gain, weights):
    pieces = len(xs)
    tokens, per_piece = xs[0].shape
    shards, streams, rows, cols = weights.shape
    group, rows = weight_group(weights, pieces)
    steps = shards // group
    each = steps // pieces

    def weight_at(j, k, place):
        return (lax.rem(place[0] + k // each, pieces) * each + lax.rem(k, each), j, 0, 0)

    whole = pl.BlockSpec((tokens, per_piece), lambda j, k, place: (0, 0))
    return pl.pallas_call(
        functools.partial(normed_product, pieces=pieces, steps=steps),
        grid_spec=pltpu.PrefetchScalarGridSpec(
            num_scalar_prefetch=1,
            grid=(streams, steps),
            in_specs=[whole] * pieces
            + [
                pl.BlockSpec((pieces, per_piece), lambda j, k, place: (0, 0)),
                pl.BlockSpec((group, 1, rows, cols), weight_at),
            ],
            out_specs=[
                pl.BlockSpec((1, tokens, cols), lambda j, k, place: (j, 0, 0)),
                pl.BlockSpec((steps, tokens, group * rows), lambda j, k, place: (0, 0, 0)),
            ],
            scratch_shapes=[pltpu.VMEM((tokens, cols), jnp.float32)],
        ),
        out_shape=[
            jax.ShapeDtypeStruct((streams, tokens, cols), jnp.bfloat16),
            jax.ShapeDtypeStruct((steps, tokens, group * rows), jnp.bfloat16),
        ],
        compiler_params=pltpu.CompilerParams(vmem_limit_bytes=48 * MIB),
        cost_estimate=pl.CostEstimate(flops=2 * tokens * shards * rows * cols * streams, bytes_accessed=weights.size * 2, transcendentals=0),
        name="norm_keys_values",
    )(place, *xs, gain.reshape(pieces, per_piece), weights)


def project_rest(place, normed, weights, pieces):
    steps, tokens, _ = normed.shape
    shards, streams, rows, cols = weights.shape
    group, rows = weight_group(weights, pieces)
    each = steps // pieces

    def weight_at(j, k, place):
        return (lax.rem(place[0] + k // each, pieces) * each + lax.rem(k, each), j, 0, 0)

    return pl.pallas_call(
        functools.partial(product_only, steps=steps),
        grid_spec=pltpu.PrefetchScalarGridSpec(
            num_scalar_prefetch=1,
            grid=(streams, steps),
            in_specs=[
                pl.BlockSpec((1, tokens, group * rows), lambda j, k, place: (k, 0, 0)),
                pl.BlockSpec((group, 1, rows, cols), weight_at),
            ],
            out_specs=pl.BlockSpec((1, tokens, cols), lambda j, k, place: (j, 0, 0)),
            scratch_shapes=[pltpu.VMEM((tokens, cols), jnp.float32)],
        ),
        out_shape=jax.ShapeDtypeStruct((streams, tokens, cols), jnp.bfloat16),
        compiler_params=pltpu.CompilerParams(vmem_limit_bytes=32 * MIB),
        cost_estimate=pl.CostEstimate(flops=2 * tokens * shards * rows * cols * streams, bytes_accessed=weights.size * 2, transcendentals=0),
        name="project_queries",
    )(place, normed, weights)


def attend_kernel(position_ref, q_ref, *refs):
    kv_refs, out_ref = refs[:-1], refs[-1]
    tokens = q_ref.shape[1]
    tile = math.gcd(tokens, 256)
    contract = (((1,), (1,)), ((), ()))
    for r in range(tokens // tile):
        query = q_ref[0, r * tile : (r + 1) * tile]
        scores = []
        for lag, ref in enumerate(kv_refs):
            keys = (r + 1) * tile if lag == 0 else tokens
            s = lax.dot_general(query, ref[0, :keys], contract, preferred_element_type=jnp.float32) * (1.0 / math.sqrt(HD))
            if lag == 0:
                row = r * tile + lax.broadcasted_iota(jnp.int32, s.shape, 0)
                s = jnp.where(row >= lax.broadcasted_iota(jnp.int32, s.shape, 1), s, -jnp.inf)
            else:
                s = jnp.where(position_ref[0] >= lag, s, -jnp.inf)
            scores.append(s)
        peak = functools.reduce(jnp.maximum, [jnp.max(s, axis=1, keepdims=True) for s in scores])
        total, output = 0.0, 0.0
        for s, ref in zip(scores, kv_refs):
            expo = jnp.exp(s - peak)
            total = total + jnp.sum(expo, axis=1, keepdims=True)
            output = output + jnp.dot(expo.astype(jnp.bfloat16), ref[1, : s.shape[1]], preferred_element_type=jnp.float32)
        out_ref[r * tile : (r + 1) * tile] = (output / total).astype(jnp.bfloat16)


def attend(position, query, blocks):
    _, tokens, cols = query.shape
    pair = pl.BlockSpec((2, tokens, HD), lambda h, position: (0, 0, h))
    return pl.pallas_call(
        attend_kernel,
        grid_spec=pltpu.PrefetchScalarGridSpec(
            num_scalar_prefetch=1,
            grid=(cols // HD,),
            in_specs=[pl.BlockSpec((1, tokens, HD), lambda h, position: (0, 0, h))] + [pair] * len(blocks),
            out_specs=pl.BlockSpec((tokens, HD), lambda h, position: (0, h)),
        ),
        out_shape=jax.ShapeDtypeStruct((tokens, cols), jnp.bfloat16),
        compiler_params=pltpu.CompilerParams(vmem_limit_bytes=32 * MIB),
        cost_estimate=pl.CostEstimate(flops=4 * tokens * tokens * 3 * cols, bytes_accessed=16 * tokens * cols, transcendentals=0),
        name="windowed_attention",
    )(position, query, *blocks)


def on_device(features, short_filter, decay_rate, residue, skip_gain, norm_gain, qkv_weight):
    streams = features.transpose(1, 0, 2)
    weights = qkv_weight.transpose(1, 0, 2)
    tokens = streams.shape[1]
    pieces = lax.axis_size("tp")
    key_value_rows = lax.all_gather(weights[1:], "ctx")
    halo = shifted(streams[:, tokens - HALO :], "ctx", 1)
    query_shard, halo = lax.optimization_barrier((weights[:1], halo))
    query_rows = lax.all_gather(query_shard, "ctx")
    gated, first, enter, ends = short_part(streams, halo, short_filter, decay_rate)
    state = entering_states(ends, decay_rate, tokens)
    mixer = long_part(gated, first, enter, state, decay_rate, residue, skip_gain)
    parts = [mixer]
    for step in range(1, pieces):
        parts.append(lax.ppermute(mixer, "tp", [(s, (s - step) % pieces) for s in range(pieces)]))
    place = lax.axis_index("tp").astype(jnp.int32).reshape(1)
    key_value, normed = project_first(place, parts, norm_gain, key_value_rows)
    blocks = [key_value] + [shifted(key_value, "ctx", lag) for lag in range(1, WINDOW)]
    query = project_rest(place, normed, query_rows, pieces)
    position = lax.axis_index("ctx").astype(jnp.int32).reshape(1)
    return (mixer, attend(position, query, blocks))


def solution(mesh):
    placed = (
        P("ctx", None, "tp"),
        P(None, None, "tp"),
        P(None, "tp"),
        P(None, "tp"),
        P("tp"),
        P(),
        P("ctx", None, "tp"),
    )
    return jax.shard_map(
        on_device,
        mesh=mesh,
        in_specs=placed,
        out_specs=(P("ctx", "tp"), P("ctx", "tp")),
        check_vma=False,
    )
```

time: 960 us -> 308 us (0.32)
  other arithmetic: 451 us -> 0.16 us
  matrix products: 131 us -> 0 us
  Pallas kernels: 0 us -> 76 us
  blocking collectives: 53.4 us -> 0 us
  waiting for transfers between devices: 226 us -> 175 us
  local copies, waits for them, and re-layouts: 63.9 us -> 15.8 us
  starting transfers between devices: 11.8 us -> 26.5 us
    add x19 -> x2, other arithmetic: 415 us -> 0.16 us  [the longest x1 0.08 us: entering_states(): near = near + power(j - 1) * shifted(ends, 'ctx', j)]
    dot_general x11 -> x0, matrix products: 131 us -> none  [the longest x1 56.1 us: channel_conv(): entering = jnp.einsum('cnkb,cnb->cnk', carry, block_ends, precision=PRECISE)]
    all_gather x2, waiting for transfers between devices: 189 us -> 92.9 us  [the longest x1 80.1 us: on_device(): query_rows = lax.all_gather(query_shard, 'ctx')]
    pallas_call x0 -> x5, Pallas kernels: none -> 76 us  [the longest x1 20.1 us: short_part(): pl.pallas_call(short_kernel, grid=(channels // LANES,), in_specs=[pl.Bloc...]
    all_to_all x1 -> x0, blocking collectives: 53.4 us -> none  [on_device(): lax.all_to_all(filtered, 'ctx', split_axis=1, concat_axis=0, tiled=True)]
    ppermute x3 -> x11, waiting for transfers between devices: 36.6 us -> 81.6 us  [the longest x1 41.7 us: on_device(): lax.ppermute(mixer, 'tp', [(s, (s - step) % pieces) for s in range(pieces)])]
    select_n x1 -> x0, local copies, waits for them, and re-layouts: 26.3 us -> none  [channel_conv(): jnp.where(spacing[None, None] >= 0, jnp.exp(-rate_cols[:, :, None, None]...]
    ppermute x3 -> x11, starting transfers between devices: 6 us -> 26.5 us  [the longest x10 25.7 us: shifted(): lax.ppermute(value, axis, [(source, source + steps) for source in range(c...]
  transfers between devices with their start and end apart: 6 -> 13, of which waited for: 5 -> 12; matrix products, arithmetic and copies ran while one was open for 46% -> 1% of each run, Pallas kernels for 0% -> 20%
where the time goes in v1:
time: 308 us; the launch traced here: 307 us
  waiting for transfers between devices  175 us (57%)
  Pallas kernels  76 us (25%)
  starting transfers between devices  26.5 us (9%)
  local copies, waits for them, and re-layouts  15.8 us (5%)
  between operations  14.2 us (5%)
    all_gather x1, waiting for transfers between devices, on_device(): query_rows = lax.all_gather(query_shard, 'ctx')  80.1 us
    ppermute x1, waiting for transfers between devices, on_device(): lax.ppermute(mixer, 'tp', [(s, (s - step) % pieces) for s in range(pieces)])  41.7 us
    ppermute x10, waiting for transfers between devices, shifted(): lax.ppermute(value, axis, [(source, source + steps) for source in range(c...  39.9 us
    ppermute x10, starting transfers between devices, shifted(): lax.ppermute(value, axis, [(source, source + steps) for source in range(c...  25.7 us
    pallas_call x1, Pallas kernels, short_part(): pl.pallas_call(short_kernel, grid=(channels // LANES,), in_specs=[pl.Bloc...  20.1 us
    pallas_call x1, Pallas kernels, project_first(): pl.pallas_call(functools.partial(normed_product, pieces=pieces, steps=ste...  18.4 us
    pallas_call x1, Pallas kernels, long_part(): pl.pallas_call(long_kernel, grid=(channels // LANES,), in_specs=[by_token...  17.1 us
    pallas_call x1, Pallas kernels, attend(): pl.pallas_call(attend_kernel, grid_spec=pltpu.PrefetchScalarGridSpec(num_...  14.4 us
  transfers between devices with their start and end apart: 13, of which 12 were waited for; matrix products, arithmetic and copies ran while one was open for 1% of the time, Pallas kernels for 20%

profile of v1, /device:TPU:16, one launch (start us, length us, event | category | flops | bytes accessed | tf_op | source)
XLA Modules:
  0.0 307.3 jit_solution(18424405792380306925)
XLA Ops:
  7.2 0.0 all-gather.5.cloned.1.call-start
  7.2 0.0 copy-start.1
  7.2 0.0 copy-start.3
  7.2 2.3 slice.14
  9.5 0.0 all-gather.5.cloned.1.call-update
  9.6 0.0 all-gather.7.cloned.1.call-start
  9.6 0.9 slice.13
  10.6 1.9 collective-permute-start
  12.5 1.9 slice.12
  14.4 4.1 %collective-permute-done.halo_ref = bf16[3,16,2048]{2,1,0:T(8,128)(2,1)S(1)} collective-permute-done((bf16[3,16,2048]{2,1,0:T(8,128)(2,1)S(1)}, bf16[3,16,2048]{2,1,0:T(8,128)(2,1)S(1)}, u32[]{:S(2)}, u32[]{:S(2)}) %collective-permute-start) | collective-permute-done | bytes 196640 | tf_op jit(solution)/shard_map/ppermute | solution.py:24
  18.5 0.0 all-gather.7.cloned.1.call-update
  18.5 0.0 copy-done.1
  18.5 0.0 copy-done.3
  18.5 0.0 copy-start
  18.5 3.4 %copy-done = bf16[512,3,2048]{2,0,1:T(8,128)(2,1)S(1)} copy-done((bf16[512,3,2048]{2,0,1:T(8,128)(2,1)S(1)}, bf16[512,3,2048]{2,0,1:T(8,128)(2,1)}, u32[]{:S(2)}) %copy-start) | copy-done | bytes 6291480
  22.0 0.0 copy-start.4
  22.0 0.0 copy-start.5
  22.0 20.1 %short_and_end_states.1 = (bf16[512,2048]{1,0:T(8,128)(2,1)S(1)}, f32[512,2048]{1,0:T(8,128)S(1)}, f32[8,16,2048]{2,1,0:T(8,128)S(1)}, f32[16,2048]{1,0:T(8,128)S(1)}) custom-call(bf16[3,512,2048]{2,1,0:T(8,128)(2,1)S(1)} %bitcast.8, bf16[3,16,2048]{2,1,0:T(8,128)(2,1)S(1)} %collective-permute-done.halo_ref, f32[3,7,2048]{2,1,0:T(8,128)S(1)} %copy-done.3, ...), custom_call_target="tpu_custom_call" | custom-call | flops 104857600 | bytes 13631488 | tf_op jit(solution)/shard_map/short_and_end_states/pallas_call | solution.py:100
  42.1 1.9 collective-permute-start.1
  44.0 2.3 collective-permute-start.2
  46.4 4.4 %collective-permute-start.3 = (f32[16,2048]{1,0:T(8,128)S(1)}, f32[16,2048]{1,0:T(8,128)S(1)}, u32[]{:S(2)}, u32[]{:S(2)}) collective-permute-start(f32[16,2048]{1,0:T(8,128)S(1)} %get-tuple-element.14), channel_id=1, source_target_pairs={{0,6},{2,8},{4,10},{6,12},{8,14},{10,16},{12,18},{14,20},{16,22},{... | collective-permute-start | bytes 393224 | tf_op jit(solution)/shard_map/ppermute | solution.py:24
  50.8 1.9 collective-permute-start.4
  52.7 1.7 collective-permute-done.1
  54.5 3.5 %collective-permute-done.2 = f32[16,2048]{1,0:T(8,128)S(1)} collective-permute-done((f32[16,2048]{1,0:T(8,128)S(1)}, f32[16,2048]{1,0:T(8,128)S(1)}, u32[]{:S(2)}, u32[]{:S(2)}) %collective-permute-start.2) | collective-permute-done | bytes 131104 | tf_op jit(solution)/shard_map/ppermute | solution.py:24
  57.9 0.3 collective-permute-done.3
  58.3 1.9 collective-permute-done.4
  60.1 0.1 multiply_add_fusion.1
  60.2 2.9 collective-permute-start.5
  63.1 1.3 collective-permute-start.6
  64.4 0.7 collective-permute-start.7
  65.1 2.0 collective-permute-done.5
  67.1 4.7 %collective-permute-done.6 = f32[16,2048]{1,0:T(8,128)S(1)} collective-permute-done((f32[16,2048]{1,0:T(8,128)S(1)}, f32[16,2048]{1,0:T(8,128)S(1)}, u32[]{:S(2)}, u32[]{:S(2)}) %collective-permute-start.6) | collective-permute-done | bytes 131104 | tf_op jit(solution)/shard_map/ppermute | solution.py:24
  71.8 0.0 collective-permute-done.7
  71.8 0.1 multiply_add_fusion.state_ref
  71.9 0.0 copy-done.4
  71.9 0.0 copy-done.5
  71.9 0.0 copy-start.8
  71.9 17.1 %modal_filter.1.refs_0_ = bf16[512,2048]{1,0:T(8,128)(2,1)} custom-call(bf16[512,2048]{1,0:T(8,128)(2,1)S(1)} %get-tuple-element.11.gated_ref, f32[512,2048]{1,0:T(8,128)S(1)} %get-tuple-element.12.first_ref, f32[8,16,2048]{2,1,0:T(8,128)S(1)} %get-tuple-element.13.enter_ref, f32[16,2048]{1,0:T(8,128)S(1)} %multiply_add_fusion.state_ref, ...), custom_call_target="tpu_custom_call" | custom-call | flops 104857600 | bytes 10485760 | tf_op jit(solution)/shard_map/modal_filter/pallas_call | solution.py:138
  89.1 0.8 collective-permute-start.8
  89.9 0.0 copy-done.8
  89.9 41.7 %collective-permute-done.8.refs_1_ = bf16[512,2048]{1,0:T(8,128)(2,1)S(1)} collective-permute-done((bf16[512,2048]{1,0:T(8,128)(2,1)}, bf16[512,2048]{1,0:T(8,128)(2,1)S(1)}, u32[]{:S(2)}, u32[]{:S(2)}) %collective-permute-start.8) | collective-permute-done | bytes 2097184 | tf_op jit(solution)/shard_map/ppermute | solution.py:362
  131.6 0.0 copy-start.9
  131.6 12.8 %all-gather.5.cloned.1.call-done = bf16[32,256,1024]{2,1,0:T(8,128)(2,1)} async-done(((bf16[2,256,1024]{2,1,0:T(8,128)(2,1)}), bf16[32,256,1024]{2,1,0:T(8,128)(2,1)}) %all-gather.5.cloned.1.call-update) | async-done | bytes 16777232 | tf_op jit(solution)/shard_map/all_gather | solution.py:353
  144.4 0.0 copy-done.9
  144.4 0.0 copy-start.2
  144.4 1.6 copy-done.2
  146.0 18.4 %norm_keys_values.1 = (bf16[2,512,1024]{2,1,0:T(8,128)(2,1)S(1)}, bf16[4,512,1024]{2,1,0:T(8,128)(2,1)}) custom-call(s32[1]{0:T(128)} %bitcast.4.place_ref, bf16[512,2048]{1,0:T(8,128)(2,1)S(1)} %copy-done.2, bf16[512,2048]{1,0:T(8,128)(2,1)} %copy-done.9, f32[2,2048]{1,0:T(2,128)S(1)} %reshape.15.refs_2_, bf16[16,2,256,1024]{3,2,1,0:T(8,128)(2,1)} %bitcast.13), custom_call_target="tpu_custom_call" | custom-call | flops 8589934592 | bytes 16777216 | tf_op jit(solution)/shard_map/norm_keys_values/pallas_call | solution.py:250
  164.4 6.4 %collective-permute-start.10 = (bf16[2,512,1024]{2,1,0:T(8,128)(2,1)S(1)}, bf16[2,512,1024]{2,1,0:T(8,128)(2,1)}, u32[]{:S(2)}, u32[]{:S(2)}) collective-permute-start(bf16[2,512,1024]{2,1,0:T(8,128)(2,1)S(1)} %get-tuple-element.17.refs_0_), channel_id=1, source_target_pairs={{0,4},{2,6},{4,8},{6,10},{8,12},{10,14},{12,16},{14,18},{16,20},{1... | collective-permute-start | bytes 6291464 | tf_op jit(solution)/shard_map/ppermute | solution.py:24
  170.8 1.9 collective-permute-start.9
  172.7 80.1 %all-gather.7.cloned.1.call-done = bf16[16,256,1024]{2,1,0:T(8,128)(2,1)} async-done(((bf16[1,256,1024]{2,1,0:T(8,128)(2,1)}), bf16[16,256,1024]{2,1,0:T(8,128)(2,1)}) %all-gather.7.cloned.1.call-update) | async-done | bytes 8388624 | tf_op jit(solution)/shard_map/all_gather | solution.py:356
  252.8 0.0 copy-start.6
  252.8 3.4 %copy-done.6 = bf16[16,256,1024]{2,1,0:T(8,128)(2,1)S(1)} copy-done((bf16[16,256,1024]{2,1,0:T(8,128)(2,1)S(1)}, bf16[16,256,1024]{2,1,0:T(8,128)(2,1)}, u32[]{:S(2)}) %copy-start.6) | copy-done | bytes 8388632
  256.2 0.0 copy-start.7
  256.2 2.2 copy-done.7
  258.4 5.9 %project_queries.1.q_ref = bf16[1,512,1024]{2,1,0:T(8,128)(2,1)S(1)} custom-call(s32[1]{0:T(128)} %bitcast.4.place_ref, bf16[4,512,1024]{2,1,0:T(8,128)(2,1)S(1)} %copy-done.7, bf16[16,1,256,1024]{3,2,1,0:T(8,128)(2,1)S(1)} %bitcast.10), custom_call_target="tpu_custom_call" | custom-call | flops 4294967296 | bytes 8388608 | tf_op jit(solution)/shard_map/project_queries/pallas_call | solution.py:285
  264.3 1.2 collective-permute-done.10.refs_2_
  265.5 20.5 %collective-permute-done.9.refs_1_ = bf16[2,512,1024]{2,1,0:T(8,128)(2,1)} collective-permute-done((bf16[2,512,1024]{2,1,0:T(8,128)(2,1)S(1)}, bf16[2,512,1024]{2,1,0:T(8,128)(2,1)}, u32[]{:S(2)}, u32[]{:S(2)}) %collective-permute-start.9) | collective-permute-done | bytes 2097184 | tf_op jit(solution)/shard_map/ppermute | solution.py:24
  286.0 14.4 %windowed_attention.1 = bf16[512,1024]{1,0:T(8,128)(2,1)} custom-call(s32[1]{0:T(128)} %bitcast.3.position_ref, bf16[1,512,1024]{2,1,0:T(8,128)(2,1)S(1)} %project_queries.1.q_ref, bf16[2,512,1024]{2,1,0:T(8,128)(2,1)S(1)} %get-tuple-element.17.refs_0_, bf16[2,512,1024]{2,1,0:T(8,128)(2,1)} %collective-permute-done.9.refs_1_, ...), custom_call_target="tpu_custom_call" | custom-call | flops 3221225472 | bytes 8388608 | tf_op jit(solution)/shard_map/windowed_attention/pallas_call | solution.py:333
  (1 shorter events, 0.0 us)
Async XLA Ops:
  7.2 137.2 %all-gather.5.cloned.1.call-start = ((), (), s32[]{:S(2)}) async-start(), calls=%async_computation | async-start | bytes 17825792 | tf_op jit(solution)/shard_map/all_gather | solution.py:353
  7.2 11.3 %copy-start.1 = (f32[16,2048]{1,0:T(8,128)S(1)}, f32[16,2048]{1,0:T(8,128)}, u32[]{:S(2)}) copy-start(f32[16,2048]{1,0:T(8,128)} %decay_ref.3) | copy-start | bytes 393220
  7.2 11.3 %copy-start.3 = (f32[3,7,2048]{2,1,0:T(8,128)S(1)}, f32[3,7,2048]{2,1,0:T(8,128)}, u32[]{:S(2)}) copy-start(f32[3,7,2048]{2,1,0:T(8,128)} %taps_ref.1) | copy-start | bytes 516100
  9.6 243.2 %all-gather.7.cloned.1.call-start = ((), (), s32[]{:S(2)}) async-start(), calls=%async_computation.1 | async-start | bytes 8912896 | tf_op jit(solution)/shard_map/all_gather | solution.py:356
  10.6 7.9 %collective-permute-start = (bf16[3,16,2048]{2,1,0:T(8,128)(2,1)S(1)}, bf16[3,16,2048]{2,1,0:T(8,128)(2,1)S(1)}, u32[]{:S(2)}, u32[]{:S(2)}) collective-permute-start(bf16[3,16,2048]{2,1,0:T(8,128)(2,1)S(1)} %slice.13), channel_id=1, source_target_pairs={{0,2},{2,4},{4,6},{6,8},{8,10},{10,12},{12,14},{14,16},{16,18},{18... | collective-permute-start | bytes 589832 | tf_op jit(solution)/shard_map/ppermute | solution.py:24
  18.5 3.5 %copy-start = (bf16[512,3,2048]{2,0,1:T(8,128)(2,1)S(1)}, bf16[512,3,2048]{2,0,1:T(8,128)(2,1)}, u32[]{:S(2)}) copy-start(bf16[512,3,2048]{2,0,1:T(8,128)(2,1)} %param.7) | copy-start | bytes 18874372
  22.0 50.0 %copy-start.4 = (f32[16,2048]{1,0:T(8,128)S(1)}, f32[16,2048]{1,0:T(8,128)}, u32[]{:S(2)}) copy-start(f32[16,2048]{1,0:T(8,128)} %residue_ref.1) | copy-start | bytes 393220
  22.0 50.0 %copy-start.5 = (f32[2048]{0:T(1024)S(1)}, f32[2048]{0:T(1024)}, u32[]{:S(2)}) copy-start(f32[2048]{0:T(1024)} %param.11) | copy-start | bytes 24580
  42.1 12.3 %collective-permute-start.1 = (f32[16,2048]{1,0:T(8,128)S(1)}, f32[16,2048]{1,0:T(8,128)S(1)}, u32[]{:S(2)}, u32[]{:S(2)}) collective-permute-start(f32[16,2048]{1,0:T(8,128)S(1)} %get-tuple-element.14), channel_id=1, source_target_pairs={{0,2},{2,4},{4,6},{6,8},{8,10},{10,12},{12,14},{14,16},{16,18},{18... | collective-permute-start | bytes 393224 | tf_op jit(solution)/shard_map/ppermute | solution.py:24
  44.0 13.9 %collective-permute-start.2 = (f32[16,2048]{1,0:T(8,128)S(1)}, f32[16,2048]{1,0:T(8,128)S(1)}, u32[]{:S(2)}, u32[]{:S(2)}) collective-permute-start(f32[16,2048]{1,0:T(8,128)S(1)} %get-tuple-element.14), channel_id=1, source_target_pairs={{0,4},{2,6},{4,8},{6,10},{8,12},{10,14},{12,16},{14,18},{16,20},{1... | collective-permute-start | bytes 393224 | tf_op jit(solution)/shard_map/ppermute | solution.py:24
  46.4 11.9 %collective-permute-start.3 = (f32[16,2048]{1,0:T(8,128)S(1)}, f32[16,2048]{1,0:T(8,128)S(1)}, u32[]{:S(2)}, u32[]{:S(2)}) collective-permute-start(f32[16,2048]{1,0:T(8,128)S(1)} %get-tuple-element.14), channel_id=1, source_target_pairs={{0,6},{2,8},{4,10},{6,12},{8,14},{10,16},{12,18},{14,20},{16,22},{... | collective-permute-start | bytes 393224 | tf_op jit(solution)/shard_map/ppermute | solution.py:24
  50.8 9.3 %collective-permute-start.4 = (f32[16,2048]{1,0:T(8,128)S(1)}, f32[16,2048]{1,0:T(8,128)S(1)}, u32[]{:S(2)}, u32[]{:S(2)}) collective-permute-start(f32[16,2048]{1,0:T(8,128)S(1)} %get-tuple-element.14), channel_id=1, source_target_pairs={{0,8},{2,10},{4,12},{6,14},{8,16},{10,18},{12,20},{14,22},{16,24},... | collective-permute-start | bytes 393224 | tf_op jit(solution)/shard_map/ppermute | solution.py:24
  60.2 6.9 %collective-permute-start.5 = (f32[16,2048]{1,0:T(8,128)S(1)}, f32[16,2048]{1,0:T(8,128)S(1)}, u32[]{:S(2)}, u32[]{:S(2)}) collective-permute-start(f32[16,2048]{1,0:T(8,128)S(1)} %multiply_add_fusion.1), channel_id=1, source_target_pairs={{0,8},{2,10},{4,12},{6,14},{8,16},{10,18},{12,20},{14,22},{16,24},... | collective-permute-start | bytes 393224 | tf_op jit(solution)/shard_map/ppermute | solution.py:24
  63.1 8.7 %collective-permute-start.6 = (f32[16,2048]{1,0:T(8,128)S(1)}, f32[16,2048]{1,0:T(8,128)S(1)}, u32[]{:S(2)}, u32[]{:S(2)}) collective-permute-start(f32[16,2048]{1,0:T(8,128)S(1)} %multiply_add_fusion.1), channel_id=1, source_target_pairs={{0,16},{2,18},{4,20},{6,22},{8,24},{10,26},{12,28},{14,30},{1,17},... | collective-permute-start | bytes 393224 | tf_op jit(solution)/shard_map/ppermute | solution.py:24
  64.4 7.4 %collective-permute-start.7 = (f32[16,2048]{1,0:T(8,128)S(1)}, f32[16,2048]{1,0:T(8,128)S(1)}, u32[]{:S(2)}, u32[]{:S(2)}) collective-permute-start(f32[16,2048]{1,0:T(8,128)S(1)} %multiply_add_fusion.1), channel_id=1, source_target_pairs={{0,24},{2,26},{4,28},{6,30},{1,25},{3,27},{5,29},{7,31}} | collective-permute-start | bytes 393224 | tf_op jit(solution)/shard_map/ppermute | solution.py:24
  71.9 18.0 %copy-start.8 = (f32[4096]{0:T(1024)S(1)}, f32[4096]{0:T(1024)}, u32[]{:S(2)}) copy-start(f32[4096]{0:T(1024)} %param.12) | copy-start | bytes 49156
  89.1 42.6 %collective-permute-start.8 = (bf16[512,2048]{1,0:T(8,128)(2,1)}, bf16[512,2048]{1,0:T(8,128)(2,1)S(1)}, u32[]{:S(2)}, u32[]{:S(2)}) collective-permute-start(bf16[512,2048]{1,0:T(8,128)(2,1)} %modal_filter.1.refs_0_), channel_id=1, source_target_pairs={{0,1},{1,0},{2,3},{3,2},{4,5},{5,4},{6,7},{7,6},{8,9},{9,8},{10,11... | collective-permute-start | bytes 6291464 | tf_op jit(solution)/shard_map/ppermute | solution.py:362
  131.6 12.8 %copy-start.9 = (bf16[512,2048]{1,0:T(8,128)(2,1)}, bf16[512,2048]{1,0:T(8,128)(2,1)S(1)}, u32[]{:S(2)}) copy-start(bf16[512,2048]{1,0:T(8,128)(2,1)S(1)} %collective-permute-done.8.refs_1_) | copy-start | bytes 6291460
  144.4 1.6 copy-start.2
  164.4 101.1 %collective-permute-start.10 = (bf16[2,512,1024]{2,1,0:T(8,128)(2,1)S(1)}, bf16[2,512,1024]{2,1,0:T(8,128)(2,1)}, u32[]{:S(2)}, u32[]{:S(2)}) collective-permute-start(bf16[2,512,1024]{2,1,0:T(8,128)(2,1)S(1)} %get-tuple-element.17.refs_0_), channel_id=1, source_target_pairs={{0,4},{2,6},{4,8},{6,10},{8,12},{10,14},{12,16},{14,18},{16,20},{1... | collective-permute-start | bytes 6291464 | tf_op jit(solution)/shard_map/ppermute | solution.py:24
  170.8 115.2 %collective-permute-start.9 = (bf16[2,512,1024]{2,1,0:T(8,128)(2,1)S(1)}, bf16[2,512,1024]{2,1,0:T(8,128)(2,1)}, u32[]{:S(2)}, u32[]{:S(2)}) collective-permute-start(bf16[2,512,1024]{2,1,0:T(8,128)(2,1)S(1)} %get-tuple-element.17.refs_0_), channel_id=1, source_target_pairs={{0,2},{2,4},{4,6},{6,8},{8,10},{10,12},{12,14},{14,16},{16,18},{18... | collective-permute-start | bytes 6291464 | tf_op jit(solution)/shard_map/ppermute | solution.py:24
  252.8 3.4 %copy-start.6 = (bf16[16,256,1024]{2,1,0:T(8,128)(2,1)S(1)}, bf16[16,256,1024]{2,1,0:T(8,128)(2,1)}, u32[]{:S(2)}) copy-start(bf16[16,256,1024]{2,1,0:T(8,128)(2,1)} %all-gather.7.cloned.1.call-done) | copy-start | bytes 25165828
  256.2 2.2 copy-start.7
Sparse Core Ops, SparseCore 0:
  10.7 133.6 all-gather.4
  146.6 106.1 all-gather.6

commit v2 on v1

--- a/solution.py
+++ b/solution.py
@@ -16,6 +16,7 @@
 SEGMENTS = 8
 HALO = 16
 RADIX = 4
+HALVES = 2
 MIB = 1 << 20
 
 
@@ -129,25 +130,27 @@
     )(features, halo, short_filter, decay_rate)
 
 
-def long_part(gated, first, enter, state, decay_rate, residue, skip_gain):
+def long_part(gated, first, enter, state, decay_rate, residue, skip_gain, half):
     tokens, channels = gated.shape
+    channels = channels // HALVES
+    ahead = half * (channels // LANES)
     modes = decay_rate.shape[0]
     f32 = jnp.float32
-    by_token = pl.BlockSpec((tokens, LANES), lambda c: (0, c))
-    by_mode = pl.BlockSpec((modes, LANES), lambda c: (0, c))
+    by_token = pl.BlockSpec((tokens, LANES), lambda c: (0, c + ahead))
+    by_mode = pl.BlockSpec((modes, LANES), lambda c: (0, c + ahead))
     return pl.pallas_call(
         long_kernel,
         grid=(channels // LANES,),
         in_specs=[
             by_token,
             by_token,
-            pl.BlockSpec((SEGMENTS, modes, LANES), lambda c: (0, 0, c)),
+            pl.BlockSpec((SEGMENTS, modes, LANES), lambda c: (0, 0, c + ahead)),
             by_mode,
             by_mode,
             by_mode,
-            pl.BlockSpec((1, LANES), lambda c: (0, c)),
-        ],
-        out_specs=by_token,
+            pl.BlockSpec((1, LANES), lambda c: (0, c + ahead)),
+        ],
+        out_specs=pl.BlockSpec((tokens, LANES), lambda c: (0, c)),
         out_shape=jax.ShapeDtypeStruct((tokens, channels), jnp.bfloat16),
         scratch_shapes=[
             pltpu.VMEM((tokens, LANES), f32),
@@ -175,134 +178,109 @@
     return state
 
 
-def normed_product(place_ref, *refs, pieces, steps):
-    x_refs, (gain_ref, w_ref, out_ref, normed_ref, acc) = refs[:pieces], refs[pieces:]
-    stream, k = pl.program_id(0), pl.program_id(1)
-    per_piece = x_refs[0].shape[1]
-    rows = w_ref.shape[0] * w_ref.shape[2]
-
-    @pl.when((stream == 0) & (k == 0))
-    def _():
-        squares = 0.0
-        for x_ref in x_refs:
-            as_float = x_ref[...].astype(jnp.float32)
-            squares = squares + jnp.sum(as_float * as_float, axis=1, keepdims=True)
-        inverse = lax.rsqrt(squares / (pieces * per_piece) + EPSILON)
-        for p, x_ref in enumerate(x_refs):
-            at = lax.rem(place_ref[0] + p, pieces)
-            gain = gain_ref[pl.ds(at, 1), :]
-            scaled = (x_ref[...].astype(jnp.float32) * inverse * gain).astype(jnp.bfloat16)
-            for part in range(per_piece // rows):
-                normed_ref[p * (per_piece // rows) + part] = scaled[:, part * rows : (part + 1) * rows]
-
-    weights = w_ref[:, 0].reshape(rows, w_ref.shape[3])
-    term = jnp.dot(normed_ref[k], weights, preferred_element_type=jnp.float32)
-
-    @pl.when(k == 0)
-    def _():
-        acc[...] = term
-
-    @pl.when(k > 0)
-    def _():
-        acc[...] += term
-
-    @pl.when(k == steps - 1)
-    def _():
-        out_ref[0] = acc[...].astype(jnp.bfloat16)
-
-
-def product_only(place_ref, x_ref, w_ref, out_ref, acc, *, steps):
-    k = pl.program_id(1)
-    rows = w_ref.shape[0] * w_ref.shape[2]
-    weights = w_ref[:, 0].reshape(rows, w_ref.shape[3])
-    term = jnp.dot(x_ref[0], weights, preferred_element_type=jnp.float32)
-
-    @pl.when(k == 0)
-    def _():
-        acc[...] = term
-
-    @pl.when(k > 0)
-    def _():
-        acc[...] += term
-
-    @pl.when(k == steps - 1)
-    def _():
-        out_ref[0] = acc[...].astype(jnp.bfloat16)
-
-
-def weight_group(weights, pieces):
-    shards, _, rows, _ = weights.shape
-    return math.gcd(4, shards // pieces), rows
-
-
-def project_first(place, xs, gain, weights):
-    pieces = len(xs)
-    tokens, per_piece = xs[0].shape
-    shards, streams, rows, cols = weights.shape
-    group, rows = weight_group(weights, pieces)
-    steps = shards // group
-    each = steps // pieces
-
-    def weight_at(j, k, place):
-        return (lax.rem(place[0] + k // each, pieces) * each + lax.rem(k, each), j, 0, 0)
-
-    whole = pl.BlockSpec((tokens, per_piece), lambda j, k, place: (0, 0))
-    return pl.pallas_call(
-        functools.partial(normed_product, pieces=pieces, steps=steps),
+def norm_kernel(place_ref, *refs, pieces):
+    x_refs, (gain_ref, out_ref) = refs[:-2], refs[-2:]
+    split = len(x_refs) // pieces
+    width = x_refs[0].shape[1]
+    rows = out_ref.shape[2]
+    squares = 0.0
+    for x_ref in x_refs:
+        as_float = x_ref[...].astype(jnp.float32)
+        squares = squares + jnp.sum(as_float * as_float, axis=1, keepdims=True)
+    inverse = lax.rsqrt(squares / (len(x_refs) * width) + EPSILON)
+    each = width // rows
+    for p, x_ref in enumerate(x_refs):
+        at = lax.rem(place_ref[0] + p // split, pieces) * split + p % split
+        gain = gain_ref[pl.ds(at, 1), :]
+        scaled = (x_ref[...].astype(jnp.float32) * inverse * gain).astype(jnp.bfloat16)
+        for part in range(each):
+            out_ref[p * each + part] = scaled[:, part * rows : (part + 1) * rows]
+
+
+def norm_part(place, xs, gain, pieces, rows):
+    tokens, width = xs[0].shape
+    tile = math.gcd(tokens, 128)
+    steps = len(xs) * width // rows
+    return pl.pallas_call(
+        functools.partial(norm_kernel, pieces=pieces),
         grid_spec=pltpu.PrefetchScalarGridSpec(
             num_scalar_prefetch=1,
-            grid=(streams, steps),
-            in_specs=[whole] * pieces
-            + [
-                pl.BlockSpec((pieces, per_piece), lambda j, k, place: (0, 0)),
-                pl.BlockSpec((group, 1, rows, cols), weight_at),
-            ],
-            out_specs=[
-                pl.BlockSpec((1, tokens, cols), lambda j, k, place: (j, 0, 0)),
-                pl.BlockSpec((steps, tokens, group * rows), lambda j, k, place: (0, 0, 0)),
-            ],
-            scratch_shapes=[pltpu.VMEM((tokens, cols), jnp.float32)],
+            grid=(tokens // tile,),
+            in_specs=[pl.BlockSpec((tile, width), lambda t, place: (t, 0))] * len(xs)
+            + [pl.BlockSpec((len(xs), width), lambda t, place: (0, 0))],
+            out_specs=pl.BlockSpec((steps, tile, rows), lambda t, place: (0, t, 0)),
         ),
-        out_shape=[
-            jax.ShapeDtypeStruct((streams, tokens, cols), jnp.bfloat16),
-            jax.ShapeDtypeStruct((steps, tokens, group * rows), jnp.bfloat16),
-        ],
-        compiler_params=pltpu.CompilerParams(vmem_limit_bytes=48 * MIB),
-        cost_estimate=pl.CostEstimate(flops=2 * tokens * shards * rows * cols * streams, bytes_accessed=weights.size * 2, transcendentals=0),
-        name="norm_keys_values",
-    )(place, *xs, gain.reshape(pieces, per_piece), weights)
-
-
-def project_rest(place, normed, weights, pieces):
-    steps, tokens, _ = normed.shape
-    shards, streams, rows, cols = weights.shape
-    group, rows = weight_group(weights, pieces)
+        out_shape=jax.ShapeDtypeStruct((steps, tokens, rows), jnp.bfloat16),
+        compiler_params=pltpu.CompilerParams(vmem_limit_bytes=32 * MIB),
+        cost_estimate=pl.CostEstimate(flops=8 * tokens * width * len(xs), bytes_accessed=4 * tokens * width * len(xs), transcendentals=0),
+        name="norm",
+    )(place, *xs, gain.reshape(len(xs), width))
+
+
+def product_kernel(place_ref, x_ref, *refs, steps):
+    w_refs, (out_ref, acc) = refs[:-2], refs[-2:]
+    k = pl.program_id(0)
+    for i, w_ref in enumerate(w_refs):
+        weights = w_ref[:, 0].reshape(w_ref.shape[0] * w_ref.shape[2], w_ref.shape[3])
+        term = jnp.dot(x_ref[0], weights, preferred_element_type=jnp.float32)
+
+        @pl.when(k == 0)
+        def _():
+            acc[i] = term
+
+        @pl.when((k > 0) & (k < steps - 1))
+        def _():
+            acc[i] += term
+
+        @pl.when(k == steps - 1)
+        def _():
+            out_ref[i] = (acc[i] + term).astype(jnp.bfloat16)
+
+
+def project(place, normed, weights, pieces, group, streams, half, halves):
+    steps, tokens, depth = normed.shape
+    _, _, rows, cols = weights.shape
+    cols = cols // halves
     each = steps // pieces
 
-    def weight_at(j, k, place):
-        return (lax.rem(place[0] + k // each, pieces) * each + lax.rem(k, each), j, 0, 0)
-
-    return pl.pallas_call(
-        functools.partial(product_only, steps=steps),
+    def weight_at(stream):
+        return lambda k, place: (lax.rem(place[0] + k // each, pieces) * each + lax.rem(k, each), stream, 0, half)
+
+    return pl.pallas_call(
+        functools.partial(product_kernel, steps=steps),
         grid_spec=pltpu.PrefetchScalarGridSpec(
             num_scalar_prefetch=1,
-            grid=(streams, steps),
-            in_specs=[
-                pl.BlockSpec((1, tokens, group * rows), lambda j, k, place: (k, 0, 0)),
-                pl.BlockSpec((group, 1, rows, cols), weight_at),
-            ],
-            out_specs=pl.BlockSpec((1, tokens, cols), lambda j, k, place: (j, 0, 0)),
-            scratch_shapes=[pltpu.VMEM((tokens, cols), jnp.float32)],
+            grid=(steps,),
+            in_specs=[pl.BlockSpec((1, tokens, depth), lambda k, place: (k, 0, 0))]
+            + [pl.BlockSpec((group, 1, rows, cols), weight_at(stream)) for stream in streams],
+            out_specs=pl.BlockSpec((len(streams), tokens, cols), lambda k, place: (0, 0, 0)),
+            scratch_shapes=[pltpu.VMEM((len(streams), tokens, cols), jnp.float32)],
         ),
-        out_shape=jax.ShapeDtypeStruct((streams, tokens, cols), jnp.bfloat16),
+        out_shape=jax.ShapeDtypeStruct((len(streams), tokens, cols), jnp.bfloat16),
         compiler_params=pltpu.CompilerParams(vmem_limit_bytes=32 * MIB),
-        cost_estimate=pl.CostEstimate(flops=2 * tokens * shards * rows * cols * streams, bytes_accessed=weights.size * 2, transcendentals=0),
-        name="project_queries",
-    )(place, normed, weights)
+        cost_estimate=pl.CostEstimate(
+            flops=2 * steps * tokens * depth * cols * len(streams),
+            bytes_accessed=2 * steps * depth * (tokens + cols * len(streams)),
+            transcendentals=0,
+        ),
+        name="project",
+    )(place, normed, *[weights] * len(streams))
 
 
 def attend_kernel(position_ref, q_ref, *refs):
-    kv_refs, out_ref = refs[:-1], refs[-1]
+    own_ref, near_ref, even_ref, odd_ref = refs[:4]
+    out_ref, far = refs[-2:]
+    even = lax.rem(position_ref[0], 2) == 0
+
+    @pl.when(even)
+    def _():
+        far[...] = even_ref[...]
+
+    @pl.when(jnp.logical_not(even))
+    def _():
+        far[...] = odd_ref[...]
+
+    kv_refs = (own_ref, near_ref, far)
     tokens = q_ref.shape[1]
     tile = math.gcd(tokens, 256)
     contract = (((1,), (1,)), ((), ()))
@@ -327,22 +305,37 @@
         out_ref[r * tile : (r + 1) * tile] = (output / total).astype(jnp.bfloat16)
 
 
-def attend(position, query, blocks):
+def attend(position, query, blocks, half, before):
     _, tokens, cols = query.shape
+    heads = cols // HD // HALVES
+    ahead = half * heads
     pair = pl.BlockSpec((2, tokens, HD), lambda h, position: (0, 0, h))
+    extra = [] if before is None else [before]
     return pl.pallas_call(
         attend_kernel,
         grid_spec=pltpu.PrefetchScalarGridSpec(
             num_scalar_prefetch=1,
-            grid=(cols // HD,),
-            in_specs=[pl.BlockSpec((1, tokens, HD), lambda h, position: (0, 0, h))] + [pair] * len(blocks),
-            out_specs=pl.BlockSpec((tokens, HD), lambda h, position: (0, h)),
+            grid=(heads,),
+            in_specs=[pl.BlockSpec((1, tokens, HD), lambda h, position: (0, 0, h + ahead))]
+            + [pair] * len(blocks)
+            + [pl.BlockSpec(memory_space=pl.ANY)] * len(extra),
+            out_specs=pl.BlockSpec((tokens, HD), lambda h, position: (0, h + ahead)),
+            scratch_shapes=[pltpu.VMEM((2, tokens, HD), jnp.bfloat16)],
         ),
         out_shape=jax.ShapeDtypeStruct((tokens, cols), jnp.bfloat16),
+        input_output_aliases={2 + len(blocks): 0} if extra else {},
         compiler_params=pltpu.CompilerParams(vmem_limit_bytes=32 * MIB),
-        cost_estimate=pl.CostEstimate(flops=4 * tokens * tokens * 3 * cols, bytes_accessed=16 * tokens * cols, transcendentals=0),
+        cost_estimate=pl.CostEstimate(flops=4 * tokens * tokens * 3 * cols // HALVES, bytes_accessed=16 * tokens * cols // HALVES, transcendentals=0),
         name="windowed_attention",
-    )(position, query, *blocks)
+    )(position, query, *blocks, *extra)
+
+
+def window_blocks(own):
+    count = lax.axis_size("ctx")
+    near = shifted(own, "ctx", 1)
+    even = lax.ppermute(own, "ctx", [(s, s + 2) for s in range(0, count - 2, 2)])
+    odd = lax.ppermute(near, "ctx", [(s, s + 1) for s in range(0, count - 1, 2)])
+    return (own, near, even, odd)
 
 
 def on_device(features, short_filter, decay_rate, residue, skip_gain, norm_gain, qkv_weight):
@@ -350,22 +343,31 @@
     weights = qkv_weight.transpose(1, 0, 2)
     tokens = streams.shape[1]
     pieces = lax.axis_size("tp")
-    key_value_rows = lax.all_gather(weights[1:], "ctx")
+    rows = lax.all_gather(weights, "ctx")
     halo = shifted(streams[:, tokens - HALO :], "ctx", 1)
-    query_shard, halo = lax.optimization_barrier((weights[:1], halo))
-    query_rows = lax.all_gather(query_shard, "ctx")
     gated, first, enter, ends = short_part(streams, halo, short_filter, decay_rate)
     state = entering_states(ends, decay_rate, tokens)
-    mixer = long_part(gated, first, enter, state, decay_rate, residue, skip_gain)
-    parts = [mixer]
-    for step in range(1, pieces):
-        parts.append(lax.ppermute(mixer, "tp", [(s, (s - step) % pieces) for s in range(pieces)]))
+    own = []
+    others = [[] for _ in range(1, pieces)]
+    for half in range(HALVES):
+        own.append(long_part(gated, first, enter, state, decay_rate, residue, skip_gain, half))
+        for step in range(1, pieces):
+            source = [(s, (s - step) % pieces) for s in range(pieces)]
+            others[step - 1].append(lax.ppermute(own[-1], "tp", source))
+    parts = own + [part for group in others for part in group]
     place = lax.axis_index("tp").astype(jnp.int32).reshape(1)
-    key_value, normed = project_first(place, parts, norm_gain, key_value_rows)
-    blocks = [key_value] + [shifted(key_value, "ctx", lag) for lag in range(1, WINDOW)]
-    query = project_rest(place, normed, query_rows, pieces)
+    group = math.gcd(4, rows.shape[0] // len(parts))
+    normed = norm_part(place, parts, norm_gain, pieces, group * rows.shape[2])
+    windows = []
+    for half in range(HALVES):
+        pair = project(place, normed, rows, pieces, group, (1, 2), half, HALVES)
+        windows.append(window_blocks(pair))
+    query = project(place, normed, rows, pieces, group, (0,), 0, 1)
     position = lax.axis_index("ctx").astype(jnp.int32).reshape(1)
-    return (mixer, attend(position, query, blocks))
+    attended = None
+    for half in range(HALVES):
+        attended = attend(position, query, windows[half], half, attended)
+    return (jnp.concatenate(own, axis=1), attended)
 
 
 def solution(mesh):

time: 308 us -> 243 us (0.79)
  waiting for transfers between devices: 175 us -> 83.8 us
  starting transfers between devices: 26.5 us -> 48.2 us
  Pallas kernels: 76 us -> 81.7 us
  local copies, waits for them, and re-layouts: 15.8 us -> 12.2 us
    all_gather x2 -> x1, waiting for transfers between devices: 92.9 us -> 1.08 us  [on_device(): rows = lax.all_gather(weights, 'ctx')]
    ppermute x1 -> x6, starting transfers between devices: 0.82 us -> 20.6 us  [the longest x2 13.9 us: window_blocks(): lax.ppermute(near, 'ctx', [(s, s + 1) for s in range(0, count - 1, 2)])]
    slice x2 -> x0, local copies, waits for them, and re-layouts: 4.2 us -> none  [the longest x1 2.31 us: on_device(): key_value_rows = lax.all_gather(weights[1:], 'ctx')]
    pallas_call x2 -> x4, Pallas kernels: 24.3 us -> 28.4 us  [the longest x3 24.7 us: project(): pl.pallas_call(functools.partial(product_kernel, steps=steps), grid_spec=...]
    pallas_call x1 -> x2, Pallas kernels: 14.4 us -> 16.2 us  [attend(): pl.pallas_call(attend_kernel, grid_spec=pltpu.PrefetchScalarGridSpec(num_...]
    unnamed x20 -> x18, local copies, waits for them, and re-layouts: 10.6 us -> 11.2 us
    ppermute x1 -> x6, waiting for transfers between devices: 41.7 us -> 41.2 us  [the longest x2 41.2 us: on_device(): others[step - 1].append(lax.ppermute(own[-1], 'tp', source))]
    pallas_call x1 -> x2, Pallas kernels: 17.1 us -> 16.9 us  [long_part(): pl.pallas_call(long_kernel, grid=(channels // LANES,), in_specs=[by_token...]
  transfers between devices with their start and end apart: 13 -> 17, of which waited for: 12 -> 11; matrix products, arithmetic and copies ran while one was open for 1% -> 1% of each run, Pallas kernels for 20% -> 27%
where the time goes in v2:
time: 243 us; the launch traced here: 242 us
  waiting for transfers between devices  83.8 us (34%)
  Pallas kernels  81.7 us (34%)
  starting transfers between devices  48.2 us (20%)
  between operations  14.3 us (6%)
  local copies, waits for them, and re-layouts  12.2 us (5%)
    ppermute x2, waiting for transfers between devices, on_device(): others[step - 1].append(lax.ppermute(own[-1], 'tp', source))  41.2 us
    ppermute x10, waiting for transfers between devices, shifted(): lax.ppermute(value, axis, [(source, source + steps) for source in range(c...  40.9 us
    ppermute x10, starting transfers between devices, shifted(): lax.ppermute(value, axis, [(source, source + steps) for source in range(c...  27.5 us
    pallas_call x3, Pallas kernels, project(): pl.pallas_call(functools.partial(product_kernel, steps=steps), grid_spec=...  24.7 us
    pallas_call x1, Pallas kernels, short_part(): pl.pallas_call(short_kernel, grid=(channels // LANES,), in_specs=[pl.Bloc...  20.1 us
    pallas_call x2, Pallas kernels, long_part(): pl.pallas_call(long_kernel, grid=(channels // LANES,), in_specs=[by_token...  16.9 us
    pallas_call x2, Pallas kernels, attend(): pl.pallas_call(attend_kernel, grid_spec=pltpu.PrefetchScalarGridSpec(num_...  16.2 us
    ppermute x2, starting transfers between devices, window_blocks(): lax.ppermute(near, 'ctx', [(s, s + 1) for s in range(0, count - 1, 2)])  13.9 us
  transfers between devices with their start and end apart: 17, of which 11 were waited for; matrix products, arithmetic and copies ran while one was open for 1% of the time, Pallas kernels for 27%

profile of v2, /device:TPU:16, one launch (start us, length us, event | category | flops | bytes accessed | tf_op | source)
XLA Modules:
  0.0 241.9 jit_solution(13683969626716555727)
XLA Ops:
  7.2 0.0 all-gather.3.cloned.1.call-start
  7.2 0.7 all-gather.3.cloned.1.call-update
  7.9 0.0 copy-start.5
  7.9 0.0 copy-start.7
  7.9 1.0 slice.4
  8.9 1.9 collective-permute-start
  10.8 6.0 %collective-permute-done.halo_ref = bf16[3,16,2048]{2,1,0:T(8,128)(2,1)S(1)} collective-permute-done((bf16[3,16,2048]{2,1,0:T(8,128)(2,1)S(1)}, bf16[3,16,2048]{2,1,0:T(8,128)(2,1)S(1)}, u32[]{:S(2)}, u32[]{:S(2)}) %collective-permute-start) | collective-permute-done | bytes 196640 | tf_op jit(solution)/shard_map/ppermute | solution.py:25
  16.8 0.0 copy-start.3
  16.8 3.8 %copy-done.3 = bf16[512,3,2048]{2,0,1:T(8,128)(2,1)S(1)} copy-done((bf16[512,3,2048]{2,0,1:T(8,128)(2,1)S(1)}, bf16[512,3,2048]{2,0,1:T(8,128)(2,1)}, u32[]{:S(2)}) %copy-start.3) | copy-done | bytes 6291480
  20.6 0.0 copy-start.4
  20.6 0.9 copy-done.4
  21.5 0.0 copy-start.6
  21.5 0.9 copy-done.6
  22.4 20.1 %short_and_end_states.1 = (bf16[512,2048]{1,0:T(8,128)(2,1)S(1)}, f32[512,2048]{1,0:T(8,128)S(1)}, f32[8,16,2048]{2,1,0:T(8,128)S(1)}, f32[16,2048]{1,0:T(8,128)S(1)}) custom-call(bf16[3,512,2048]{2,1,0:T(8,128)(2,1)S(1)} %bitcast.7, bf16[3,16,2048]{2,1,0:T(8,128)(2,1)S(1)} %collective-permute-done.halo_ref, f32[3,7,2048]{2,1,0:T(8,128)S(1)} %copy-done.6, ...), custom_call_target="tpu_custom_call" | custom-call | flops 104857600 | bytes 13631488 | tf_op jit(solution)/shard_map/short_and_end_states/pallas_call | solution.py:101
  42.5 3.4 %collective-permute-start.4 = (f32[16,2048]{1,0:T(8,128)S(1)}, f32[16,2048]{1,0:T(8,128)S(1)}, u32[]{:S(2)}, u32[]{:S(2)}) collective-permute-start(f32[16,2048]{1,0:T(8,128)S(1)} %get-tuple-element.9), channel_id=1, source_target_pairs={{0,8},{2,10},{4,12},{6,14},{8,16},{10,18},{12,20},{14,22},{16,24},... | collective-permute-start | bytes 393224 | tf_op jit(solution)/shard_map/ppermute | solution.py:25
  45.9 1.9 collective-permute-start.3
  47.9 2.6 %collective-permute-start.2 = (f32[16,2048]{1,0:T(8,128)S(1)}, f32[16,2048]{1,0:T(8,128)S(1)}, u32[]{:S(2)}, u32[]{:S(2)}) collective-permute-start(f32[16,2048]{1,0:T(8,128)S(1)} %get-tuple-element.9), channel_id=1, source_target_pairs={{0,4},{2,6},{4,8},{6,10},{8,12},{10,14},{12,16},{14,18},{16,20},{1... | collective-permute-start | bytes 393224 | tf_op jit(solution)/shard_map/ppermute | solution.py:25
  50.5 1.9 collective-permute-start.1
  52.5 0.4 collective-permute-done.4
  52.9 2.6 %collective-permute-done.3 = f32[16,2048]{1,0:T(8,128)S(1)} collective-permute-done((f32[16,2048]{1,0:T(8,128)S(1)}, f32[16,2048]{1,0:T(8,128)S(1)}, u32[]{:S(2)}, u32[]{:S(2)}) %collective-permute-start.3) | collective-permute-done | bytes 131104 | tf_op jit(solution)/shard_map/ppermute | solution.py:25
  55.5 9.0 %collective-permute-done.2 = f32[16,2048]{1,0:T(8,128)S(1)} collective-permute-done((f32[16,2048]{1,0:T(8,128)S(1)}, f32[16,2048]{1,0:T(8,128)S(1)}, u32[]{:S(2)}, u32[]{:S(2)}) %collective-permute-start.2) | collective-permute-done | bytes 131104 | tf_op jit(solution)/shard_map/ppermute | solution.py:25
  64.5 2.5 %collective-permute-done.1 = f32[16,2048]{1,0:T(8,128)S(1)} collective-permute-done((f32[16,2048]{1,0:T(8,128)S(1)}, f32[16,2048]{1,0:T(8,128)S(1)}, u32[]{:S(2)}, u32[]{:S(2)}) %collective-permute-start.1) | collective-permute-done | bytes 131104 | tf_op jit(solution)/shard_map/ppermute | solution.py:25
  67.0 0.1 multiply_add_fusion.1
  67.1 0.7 collective-permute-start.7
  67.8 1.3 collective-permute-start.6
  69.0 2.5 %collective-permute-start.5 = (f32[16,2048]{1,0:T(8,128)S(1)}, f32[16,2048]{1,0:T(8,128)S(1)}, u32[]{:S(2)}, u32[]{:S(2)}) collective-permute-start(f32[16,2048]{1,0:T(8,128)S(1)} %multiply_add_fusion.1), channel_id=1, source_target_pairs={{0,8},{2,10},{4,12},{6,14},{8,16},{10,18},{12,20},{14,22},{16,24},... | collective-permute-start | bytes 393224 | tf_op jit(solution)/shard_map/ppermute | solution.py:25
  71.6 0.0 collective-permute-done.7
  71.6 11.8 %collective-permute-done.6 = f32[16,2048]{1,0:T(8,128)S(1)} collective-permute-done((f32[16,2048]{1,0:T(8,128)S(1)}, f32[16,2048]{1,0:T(8,128)S(1)}, u32[]{:S(2)}, u32[]{:S(2)}) %collective-permute-start.6) | collective-permute-done | bytes 131104 | tf_op jit(solution)/shard_map/ppermute | solution.py:25
  83.4 3.0 %collective-permute-done.5 = f32[16,2048]{1,0:T(8,128)S(1)} collective-permute-done((f32[16,2048]{1,0:T(8,128)S(1)}, f32[16,2048]{1,0:T(8,128)S(1)}, u32[]{:S(2)}, u32[]{:S(2)}) %collective-permute-start.5) | collective-permute-done | bytes 131104 | tf_op jit(solution)/shard_map/ppermute | solution.py:25
  86.4 0.1 multiply_add_fusion.state_ref
  86.5 0.0 copy-done.5
  86.5 0.0 copy-done.7
  86.5 8.5 %modal_filter.3.refs_1_ = bf16[512,1024]{1,0:T(8,128)(2,1)S(1)} custom-call(bf16[512,2048]{1,0:T(8,128)(2,1)S(1)} %get-tuple-element.6.gated_ref, f32[512,2048]{1,0:T(8,128)S(1)} %get-tuple-element.7.first_ref, f32[8,16,2048]{2,1,0:T(8,128)S(1)} %get-tuple-element.8.enter_ref, f32[16,2048]{1,0:T(8,128)S(1)} %multiply_add_fusion.state_ref, ...), custom_call_target="tpu_custom_call" | custom-call | flops 52428800 | bytes 5242880 | tf_op jit(solution)/shard_map/modal_filter/pallas_call | solution.py:141
  95.0 0.0 copy-start.8
  95.0 8.5 %modal_filter.2.refs_0_ = bf16[512,1024]{1,0:T(8,128)(2,1)S(1)} custom-call(bf16[512,2048]{1,0:T(8,128)(2,1)S(1)} %get-tuple-element.6.gated_ref, f32[512,2048]{1,0:T(8,128)S(1)} %get-tuple-element.7.first_ref, f32[8,16,2048]{2,1,0:T(8,128)S(1)} %get-tuple-element.8.enter_ref, f32[16,2048]{1,0:T(8,128)S(1)} %multiply_add_fusion.state_ref, ...), custom_call_target="tpu_custom_call" | custom-call | flops 52428800 | bytes 5242880 | tf_op jit(solution)/shard_map/modal_filter/pallas_call | solution.py:141
  103.5 1.6 collective-permute-start.8
  105.0 0.5 collective-permute-start.9
  105.5 0.0 copy-done.8
  105.6 24.1 %collective-permute-done.8.refs_2_ = bf16[512,1024]{1,0:T(8,128)(2,1)S(1)} collective-permute-done((bf16[512,1024]{1,0:T(8,128)(2,1)S(1)}, bf16[512,1024]{1,0:T(8,128)(2,1)S(1)}, u32[]{:S(2)}, u32[]{:S(2)}) %collective-permute-start.8) | collective-permute-done | bytes 1048608 | tf_op jit(solution)/shard_map/ppermute | solution.py:356
  129.6 17.1 %collective-permute-done.9.refs_3_ = bf16[512,1024]{1,0:T(8,128)(2,1)} collective-permute-done((bf16[512,1024]{1,0:T(8,128)(2,1)S(1)}, bf16[512,1024]{1,0:T(8,128)(2,1)}, u32[]{:S(2)}, u32[]{:S(2)}) %collective-permute-start.9) | collective-permute-done | bytes 1048608 | tf_op jit(solution)/shard_map/ppermute | solution.py:356
  146.8 3.7 %norm.1.x_ref = bf16[4,512,1024]{2,1,0:T(8,128)(2,1)S(1)} custom-call(s32[1]{0:T(128)} %bitcast.3.place_ref, bf16[512,1024]{1,0:T(8,128)(2,1)S(1)} %modal_filter.2.refs_0_, bf16[512,1024]{1,0:T(8,128)(2,1)S(1)} %modal_filter.3.refs_1_, bf16[512,1024]{1,0:T(8,128)(2,1)S(1)} %collective-permute-done.8.refs_2_, ...), custom_call_target="tpu_custom_call" | custom-call | flops 16777216 | bytes 8388608 | tf_op jit(solution)/shard_map/norm/pallas_call | solution.py:204
  150.5 0.0 copy-start
  150.5 2.0 copy-done
  152.4 1.1 all-gather.3.cloned.1.call-done
  153.5 2.2 copy-done.1
  155.7 8.1 %project.5.refs_0_ = bf16[2,512,512]{2,1,0:T(8,128)(2,1)S(1)} custom-call(s32[1]{0:T(128)} %bitcast.3.place_ref, bf16[4,512,1024]{2,1,0:T(8,128)(2,1)S(1)} %copy-done.1, bf16[16,3,256,1024]{3,2,1,0:T(8,128)(2,1)} %bitcast.10, bf16[16,3,256,1024]{3,2,1,0:T(8,128)(2,1)} %bitcast.11), custom_call_target="tpu_custom_call" | custom-call | flops 4294967296 | bytes 12582912 | tf_op jit(solution)/shard_map/project/pallas_call | solution.py:249
  163.8 2.2 collective-permute-start.13
  166.0 9.1 %project.4.refs_0_ = bf16[2,512,512]{2,1,0:T(8,128)(2,1)} custom-call(s32[1]{0:T(128)} %bitcast.3.place_ref, bf16[4,512,1024]{2,1,0:T(8,128)(2,1)S(1)} %copy-done.1, bf16[16,3,256,1024]{3,2,1,0:T(8,128)(2,1)} %bitcast.12, bf16[16,3,256,1024]{3,2,1,0:T(8,128)(2,1)} %bitcast.13), custom_call_target="tpu_custom_call" | custom-call | flops 4294967296 | bytes 12582912 | tf_op jit(solution)/shard_map/project/pallas_call | solution.py:249
  175.0 9.1 %collective-permute-start.10 = (bf16[2,512,512]{2,1,0:T(8,128)(2,1)}, bf16[2,512,512]{2,1,0:T(8,128)(2,1)}, u32[]{:S(2)}, u32[]{:S(2)}) collective-permute-start(bf16[2,512,512]{2,1,0:T(8,128)(2,1)} %project.4.refs_0_), channel_id=1, source_target_pairs={{0,2},{2,4},{4,6},{6,8},{8,10},{10,12},{12,14},{14,16},{16,18},{18... | collective-permute-start | bytes 3145736 | tf_op jit(solution)/shard_map/ppermute | solution.py:25
  184.2 2.1 collective-permute-start.14
  186.2 0.0 collective-permute-done.13.refs_1_
  186.3 2.7 %collective-permute-start.15 = (bf16[2,512,512]{2,1,0:T(8,128)(2,1)}, bf16[2,512,512]{2,1,0:T(8,128)(2,1)}, u32[]{:S(2)}, u32[]{:S(2)}) collective-permute-start(bf16[2,512,512]{2,1,0:T(8,128)(2,1)} %collective-permute-done.13.refs_1_), channel_id=1, source_target_pairs={{0,2},{4,6},{8,10},{12,14},{16,18},{20,22},{24,26},{28,30},{1,3},{... | collective-permute-start | bytes 3145736 | tf_op jit(solution)/shard_map/ppermute | solution.py:337
  189.0 2.6 %collective-permute-start.11 = (bf16[2,512,512]{2,1,0:T(8,128)(2,1)}, bf16[2,512,512]{2,1,0:T(8,128)(2,1)}, u32[]{:S(2)}, u32[]{:S(2)}) collective-permute-start(bf16[2,512,512]{2,1,0:T(8,128)(2,1)} %project.4.refs_0_), channel_id=1, source_target_pairs={{0,4},{4,8},{8,12},{12,16},{16,20},{20,24},{24,28},{1,5},{5,9},{9,... | collective-permute-start | bytes 3145736 | tf_op jit(solution)/shard_map/ppermute | solution.py:336
  191.5 5.6 %collective-permute-done.10.refs_1_ = bf16[2,512,512]{2,1,0:T(8,128)(2,1)} collective-permute-done((bf16[2,512,512]{2,1,0:T(8,128)(2,1)}, bf16[2,512,512]{2,1,0:T(8,128)(2,1)}, u32[]{:S(2)}, u32[]{:S(2)}) %collective-permute-start.10) | collective-permute-done | bytes 1048608 | tf_op jit(solution)/shard_map/ppermute | solution.py:25
  197.1 11.2 %collective-permute-start.12 = (bf16[2,512,512]{2,1,0:T(8,128)(2,1)}, bf16[2,512,512]{2,1,0:T(8,128)(2,1)}, u32[]{:S(2)}, u32[]{:S(2)}) collective-permute-start(bf16[2,512,512]{2,1,0:T(8,128)(2,1)} %collective-permute-done.10.refs_1_), channel_id=1, source_target_pairs={{0,2},{4,6},{8,10},{12,14},{16,18},{20,22},{24,26},{28,30},{1,3},{... | collective-permute-start | bytes 3145736 | tf_op jit(solution)/shard_map/ppermute | solution.py:337
  208.3 1.5 pad_maximum_fusion
  209.8 1.4 copy-done.2
  211.2 7.6 %project.3.q_ref = bf16[1,512,1024]{2,1,0:T(8,128)(2,1)S(1)} custom-call(s32[1]{0:T(128)} %bitcast.3.place_ref, bf16[4,512,1024]{2,1,0:T(8,128)(2,1)S(1)} %copy-done.2, bf16[16,3,256,1024]{3,2,1,0:T(8,128)(2,1)} %bitcast.14), custom_call_target="tpu_custom_call" | custom-call | flops 4294967296 | bytes 12582912 | tf_op jit(solution)/shard_map/project/pallas_call | solution.py:249
  218.8 0.0 collective-permute-done.14.refs_2_
  218.8 0.0 collective-permute-done.15.refs_3_
  218.8 8.1 %windowed_attention.2.refs_4_ = bf16[512,1024]{1,0:T(8,128)(2,1)} custom-call(s32[1]{0:T(128)} %bitcast.2.position_ref, bf16[1,512,1024]{2,1,0:T(8,128)(2,1)S(1)} %project.3.q_ref, bf16[2,512,512]{2,1,0:T(8,128)(2,1)S(1)} %project.5.refs_0_, bf16[2,512,512]{2,1,0:T(8,128)(2,1)} %collective-permute-done.13.refs_1_, ...), custom_call_target="tpu_custom_call" | custom-call | flops 1610612736 | bytes 4194304 | tf_op jit(solution)/shard_map/windowed_attention/pallas_call | solution.py:314
  226.9 0.0 collective-permute-done.11.refs_2_
  226.9 0.0 collective-permute-done.12.refs_3_
  226.9 8.1 %windowed_attention.3 = bf16[512,1024]{1,0:T(8,128)(2,1)} custom-call(s32[1]{0:T(128)} %bitcast.2.position_ref, bf16[1,512,1024]{2,1,0:T(8,128)(2,1)S(1)} %project.3.q_ref, bf16[2,512,512]{2,1,0:T(8,128)(2,1)} %project.4.refs_0_, bf16[2,512,512]{2,1,0:T(8,128)(2,1)} %collective-permute-done.10.refs_1_, ...), custom_call_target="tpu_custom_call", output_to_operand_aliasing={{}: (6, {})} | custom-call | flops 1610612736 | bytes 4194304 | tf_op jit(solution)/shard_map/windowed_attention/pallas_call | solution.py:314
  (3 shorter events, 0.0 us)
Async XLA Ops:
  7.2 146.4 %all-gather.3.cloned.1.call-start = ((), (), s32[]{:S(2)}) async-start(), calls=%async_computation | async-start | bytes 26738688 | tf_op jit(solution)/shard_map/all_gather | solution.py:346
  7.9 78.6 %copy-start.5 = (f32[16,2048]{1,0:T(8,128)S(1)}, f32[16,2048]{1,0:T(8,128)}, u32[]{:S(2)}) copy-start(f32[16,2048]{1,0:T(8,128)} %residue_ref.3) | copy-start | bytes 393220
  7.9 78.6 %copy-start.7 = (f32[2048]{0:T(1024)S(1)}, f32[2048]{0:T(1024)}, u32[]{:S(2)}) copy-start(f32[2048]{0:T(1024)} %param.11) | copy-start | bytes 24580
  8.9 7.9 %collective-permute-start = (bf16[3,16,2048]{2,1,0:T(8,128)(2,1)S(1)}, bf16[3,16,2048]{2,1,0:T(8,128)(2,1)S(1)}, u32[]{:S(2)}, u32[]{:S(2)}) collective-permute-start(bf16[3,16,2048]{2,1,0:T(8,128)(2,1)S(1)} %slice.4), channel_id=1, source_target_pairs={{0,2},{2,4},{4,6},{6,8},{8,10},{10,12},{12,14},{14,16},{16,18},{18... | collective-permute-start | bytes 589832 | tf_op jit(solution)/shard_map/ppermute | solution.py:25
  16.8 3.8 %copy-start.3 = (bf16[512,3,2048]{2,0,1:T(8,128)(2,1)S(1)}, bf16[512,3,2048]{2,0,1:T(8,128)(2,1)}, u32[]{:S(2)}) copy-start(bf16[512,3,2048]{2,0,1:T(8,128)(2,1)} %param.7) | copy-start | bytes 18874372
  20.6 0.9 copy-start.4
  21.5 0.9 copy-start.6
  42.5 10.3 %collective-permute-start.4 = (f32[16,2048]{1,0:T(8,128)S(1)}, f32[16,2048]{1,0:T(8,128)S(1)}, u32[]{:S(2)}, u32[]{:S(2)}) collective-permute-start(f32[16,2048]{1,0:T(8,128)S(1)} %get-tuple-element.9), channel_id=1, source_target_pairs={{0,8},{2,10},{4,12},{6,14},{8,16},{10,18},{12,20},{14,22},{16,24},... | collective-permute-start | bytes 393224 | tf_op jit(solution)/shard_map/ppermute | solution.py:25
  45.9 9.6 %collective-permute-start.3 = (f32[16,2048]{1,0:T(8,128)S(1)}, f32[16,2048]{1,0:T(8,128)S(1)}, u32[]{:S(2)}, u32[]{:S(2)}) collective-permute-start(f32[16,2048]{1,0:T(8,128)S(1)} %get-tuple-element.9), channel_id=1, source_target_pairs={{0,6},{2,8},{4,10},{6,12},{8,14},{10,16},{12,18},{14,20},{16,22},{... | collective-permute-start | bytes 393224 | tf_op jit(solution)/shard_map/ppermute | solution.py:25
  47.9 16.7 %collective-permute-start.2 = (f32[16,2048]{1,0:T(8,128)S(1)}, f32[16,2048]{1,0:T(8,128)S(1)}, u32[]{:S(2)}, u32[]{:S(2)}) collective-permute-start(f32[16,2048]{1,0:T(8,128)S(1)} %get-tuple-element.9), channel_id=1, source_target_pairs={{0,4},{2,6},{4,8},{6,10},{8,12},{10,14},{12,16},{14,18},{16,20},{1... | collective-permute-start | bytes 393224 | tf_op jit(solution)/shard_map/ppermute | solution.py:25
  50.5 16.5 %collective-permute-start.1 = (f32[16,2048]{1,0:T(8,128)S(1)}, f32[16,2048]{1,0:T(8,128)S(1)}, u32[]{:S(2)}, u32[]{:S(2)}) collective-permute-start(f32[16,2048]{1,0:T(8,128)S(1)} %get-tuple-element.9), channel_id=1, source_target_pairs={{0,2},{2,4},{4,6},{6,8},{8,10},{10,12},{12,14},{14,16},{16,18},{18... | collective-permute-start | bytes 393224 | tf_op jit(solution)/shard_map/ppermute | solution.py:25
  67.1 4.5 %collective-permute-start.7 = (f32[16,2048]{1,0:T(8,128)S(1)}, f32[16,2048]{1,0:T(8,128)S(1)}, u32[]{:S(2)}, u32[]{:S(2)}) collective-permute-start(f32[16,2048]{1,0:T(8,128)S(1)} %multiply_add_fusion.1), channel_id=1, source_target_pairs={{0,24},{2,26},{4,28},{6,30},{1,25},{3,27},{5,29},{7,31}} | collective-permute-start | bytes 393224 | tf_op jit(solution)/shard_map/ppermute | solution.py:25
  67.8 15.6 %collective-permute-start.6 = (f32[16,2048]{1,0:T(8,128)S(1)}, f32[16,2048]{1,0:T(8,128)S(1)}, u32[]{:S(2)}, u32[]{:S(2)}) collective-permute-start(f32[16,2048]{1,0:T(8,128)S(1)} %multiply_add_fusion.1), channel_id=1, source_target_pairs={{0,16},{2,18},{4,20},{6,22},{8,24},{10,26},{12,28},{14,30},{1,17},... | collective-permute-start | bytes 393224 | tf_op jit(solution)/shard_map/ppermute | solution.py:25
  69.0 17.3 %collective-permute-start.5 = (f32[16,2048]{1,0:T(8,128)S(1)}, f32[16,2048]{1,0:T(8,128)S(1)}, u32[]{:S(2)}, u32[]{:S(2)}) collective-permute-start(f32[16,2048]{1,0:T(8,128)S(1)} %multiply_add_fusion.1), channel_id=1, source_target_pairs={{0,8},{2,10},{4,12},{6,14},{8,16},{10,18},{12,20},{14,22},{16,24},... | collective-permute-start | bytes 393224 | tf_op jit(solution)/shard_map/ppermute | solution.py:25
  95.0 10.6 %copy-start.8 = (f32[4096]{0:T(1024)S(1)}, f32[4096]{0:T(1024)}, u32[]{:S(2)}) copy-start(f32[4096]{0:T(1024)} %param.12) | copy-start | bytes 49156
  103.5 26.2 %collective-permute-start.8 = (bf16[512,1024]{1,0:T(8,128)(2,1)S(1)}, bf16[512,1024]{1,0:T(8,128)(2,1)S(1)}, u32[]{:S(2)}, u32[]{:S(2)}) collective-permute-start(bf16[512,1024]{1,0:T(8,128)(2,1)S(1)} %modal_filter.2.refs_0_), channel_id=1, source_target_pairs={{0,1},{1,0},{2,3},{3,2},{4,5},{5,4},{6,7},{7,6},{8,9},{9,8},{10,11... | collective-permute-start | bytes 3145736 | tf_op jit(solution)/shard_map/ppermute | solution.py:356
  105.0 41.7 %collective-permute-start.9 = (bf16[512,1024]{1,0:T(8,128)(2,1)S(1)}, bf16[512,1024]{1,0:T(8,128)(2,1)}, u32[]{:S(2)}, u32[]{:S(2)}) collective-permute-start(bf16[512,1024]{1,0:T(8,128)(2,1)S(1)} %modal_filter.3.refs_1_), channel_id=1, source_target_pairs={{0,1},{1,0},{2,3},{3,2},{4,5},{5,4},{6,7},{7,6},{8,9},{9,8},{10,11... | collective-permute-start | bytes 3145736 | tf_op jit(solution)/shard_map/ppermute | solution.py:356
  150.5 2.0 copy-start
  153.5 2.2 copy-start.1
  163.8 22.5 %collective-permute-start.13 = (bf16[2,512,512]{2,1,0:T(8,128)(2,1)S(1)}, bf16[2,512,512]{2,1,0:T(8,128)(2,1)}, u32[]{:S(2)}, u32[]{:S(2)}) collective-permute-start(bf16[2,512,512]{2,1,0:T(8,128)(2,1)S(1)} %project.5.refs_0_), channel_id=1, source_target_pairs={{0,2},{2,4},{4,6},{6,8},{8,10},{10,12},{12,14},{14,16},{16,18},{18... | collective-permute-start | bytes 3145736 | tf_op jit(solution)/shard_map/ppermute | solution.py:25
  175.0 22.0 %collective-permute-start.10 = (bf16[2,512,512]{2,1,0:T(8,128)(2,1)}, bf16[2,512,512]{2,1,0:T(8,128)(2,1)}, u32[]{:S(2)}, u32[]{:S(2)}) collective-permute-start(bf16[2,512,512]{2,1,0:T(8,128)(2,1)} %project.4.refs_0_), channel_id=1, source_target_pairs={{0,2},{2,4},{4,6},{6,8},{8,10},{10,12},{12,14},{14,16},{16,18},{18... | collective-permute-start | bytes 3145736 | tf_op jit(solution)/shard_map/ppermute | solution.py:25
  184.2 34.6 %collective-permute-start.14 = (bf16[2,512,512]{2,1,0:T(8,128)(2,1)S(1)}, bf16[2,512,512]{2,1,0:T(8,128)(2,1)}, u32[]{:S(2)}, u32[]{:S(2)}) collective-permute-start(bf16[2,512,512]{2,1,0:T(8,128)(2,1)S(1)} %project.5.refs_0_), channel_id=1, source_target_pairs={{0,4},{4,8},{8,12},{12,16},{16,20},{20,24},{24,28},{1,5},{5,9},{9,... | collective-permute-start | bytes 3145736 | tf_op jit(solution)/shard_map/ppermute | solution.py:336
  186.3 32.5 %collective-permute-start.15 = (bf16[2,512,512]{2,1,0:T(8,128)(2,1)}, bf16[2,512,512]{2,1,0:T(8,128)(2,1)}, u32[]{:S(2)}, u32[]{:S(2)}) collective-permute-start(bf16[2,512,512]{2,1,0:T(8,128)(2,1)} %collective-permute-done.13.refs_1_), channel_id=1, source_target_pairs={{0,2},{4,6},{8,10},{12,14},{16,18},{20,22},{24,26},{28,30},{1,3},{... | collective-permute-start | bytes 3145736 | tf_op jit(solution)/shard_map/ppermute | solution.py:337
  189.0 38.0 %collective-permute-start.11 = (bf16[2,512,512]{2,1,0:T(8,128)(2,1)}, bf16[2,512,512]{2,1,0:T(8,128)(2,1)}, u32[]{:S(2)}, u32[]{:S(2)}) collective-permute-start(bf16[2,512,512]{2,1,0:T(8,128)(2,1)} %project.4.refs_0_), channel_id=1, source_target_pairs={{0,4},{4,8},{8,12},{12,16},{16,20},{20,24},{24,28},{1,5},{5,9},{9,... | collective-permute-start | bytes 3145736 | tf_op jit(solution)/shard_map/ppermute | solution.py:336
  197.1 29.9 %collective-permute-start.12 = (bf16[2,512,512]{2,1,0:T(8,128)(2,1)}, bf16[2,512,512]{2,1,0:T(8,128)(2,1)}, u32[]{:S(2)}, u32[]{:S(2)}) collective-permute-start(bf16[2,512,512]{2,1,0:T(8,128)(2,1)} %collective-permute-done.10.refs_1_), channel_id=1, source_target_pairs={{0,2},{4,6},{8,10},{12,14},{16,18},{20,22},{24,26},{28,30},{1,3},{... | collective-permute-start | bytes 3145736 | tf_op jit(solution)/shard_map/ppermute | solution.py:337
  208.3 2.9 %copy-start.2 = (bf16[4,512,1024]{2,1,0:T(8,128)(2,1)S(1)}, bf16[4,512,1024]{2,1,0:T(8,128)(2,1)}, u32[]{:S(2)}) copy-start(bf16[4,512,1024]{2,1,0:T(8,128)(2,1)} %copy-done) | copy-start | bytes 12582916
Sparse Core Ops, SparseCore 0:
  9.6 143.8 all-gather.2

commit v3 on v2

--- a/solution.py
+++ b/solution.py
@@ -169,12 +169,17 @@
     def power(k):
         return jnp.exp(-float(k * tokens) * decay_rate)
 
-    near = shifted(ends, "ctx", 1)
+    def from_before(value, steps):
+        return shifted(value, "ctx", steps).astype(jnp.float32)
+
+    sent = ends.astype(jnp.bfloat16)
+    near = from_before(sent, 1)
     for j in range(2, min(RADIX, count - 1) + 1):
-        near = near + power(j - 1) * shifted(ends, "ctx", j)
+        near = near + power(j - 1) * from_before(sent, j)
     state = near
+    sent = near.astype(jnp.bfloat16)
     for m in range(RADIX, count, RADIX):
-        state = state + power(m) * shifted(near, "ctx", m)
+        state = state + power(m) * from_before(sent, m)
     return state
 
 
@@ -194,7 +199,7 @@
         gain = gain_ref[pl.ds(at, 1), :]
         scaled = (x_ref[...].astype(jnp.float32) * inverse * gain).astype(jnp.bfloat16)
         for part in range(each):
-            out_ref[p * each + part] = scaled[:, part * rows : (part + 1) * rows]
+            out_ref[at * each + part] = scaled[:, part * rows : (part + 1) * rows]
 
 
 def norm_part(place, xs, gain, pieces, rows):
@@ -217,125 +222,190 @@
     )(place, *xs, gain.reshape(len(xs), width))
 
 
-def product_kernel(place_ref, x_ref, *refs, steps):
-    w_refs, (out_ref, acc) = refs[:-2], refs[-2:]
-    k = pl.program_id(0)
-    for i, w_ref in enumerate(w_refs):
-        weights = w_ref[:, 0].reshape(w_ref.shape[0] * w_ref.shape[2], w_ref.shape[3])
-        term = jnp.dot(x_ref[0], weights, preferred_element_type=jnp.float32)
-
-        @pl.when(k == 0)
-        def _():
-            acc[i] = term
-
-        @pl.when((k > 0) & (k < steps - 1))
-        def _():
-            acc[i] += term
-
-        @pl.when(k == steps - 1)
-        def _():
-            out_ref[i] = (acc[i] + term).astype(jnp.bfloat16)
-
-
-def project(place, normed, weights, pieces, group, streams, half, halves):
-    steps, tokens, depth = normed.shape
-    _, _, rows, cols = weights.shape
-    cols = cols // halves
-    each = steps // pieces
-
-    def weight_at(stream):
-        return lambda k, place: (lax.rem(place[0] + k // each, pieces) * each + lax.rem(k, each), stream, 0, half)
-
-    return pl.pallas_call(
-        functools.partial(product_kernel, steps=steps),
-        grid_spec=pltpu.PrefetchScalarGridSpec(
-            num_scalar_prefetch=1,
-            grid=(steps,),
-            in_specs=[pl.BlockSpec((1, tokens, depth), lambda k, place: (k, 0, 0))]
-            + [pl.BlockSpec((group, 1, rows, cols), weight_at(stream)) for stream in streams],
-            out_specs=pl.BlockSpec((len(streams), tokens, cols), lambda k, place: (0, 0, 0)),
-            scratch_shapes=[pltpu.VMEM((len(streams), tokens, cols), jnp.float32)],
-        ),
-        out_shape=jax.ShapeDtypeStruct((len(streams), tokens, cols), jnp.bfloat16),
-        compiler_params=pltpu.CompilerParams(vmem_limit_bytes=32 * MIB),
-        cost_estimate=pl.CostEstimate(
-            flops=2 * steps * tokens * depth * cols * len(streams),
-            bytes_accessed=2 * steps * depth * (tokens + cols * len(streams)),
-            transcendentals=0,
-        ),
-        name="project",
-    )(place, normed, *[weights] * len(streams))
-
-
-def attend_kernel(position_ref, q_ref, *refs):
-    own_ref, near_ref, even_ref, odd_ref = refs[:4]
-    out_ref, far = refs[-2:]
-    even = lax.rem(position_ref[0], 2) == 0
-
-    @pl.when(even)
-    def _():
-        far[...] = even_ref[...]
-
-    @pl.when(jnp.logical_not(even))
-    def _():
-        far[...] = odd_ref[...]
-
-    kv_refs = (own_ref, near_ref, far)
-    tokens = q_ref.shape[1]
+def head_attention(query, pairs, position, tokens):
     tile = math.gcd(tokens, 256)
     contract = (((1,), (1,)), ((), ()))
+    outputs = []
     for r in range(tokens // tile):
-        query = q_ref[0, r * tile : (r + 1) * tile]
+        rows = query[r * tile : (r + 1) * tile]
         scores = []
-        for lag, ref in enumerate(kv_refs):
-            keys = (r + 1) * tile if lag == 0 else tokens
-            s = lax.dot_general(query, ref[0, :keys], contract, preferred_element_type=jnp.float32) * (1.0 / math.sqrt(HD))
+        for lag, (keys, _) in enumerate(pairs):
+            if lag == 0:
+                keys = keys[: (r + 1) * tile]
+            s = lax.dot_general(rows, keys, contract, preferred_element_type=jnp.float32) * (1.0 / math.sqrt(HD))
             if lag == 0:
                 row = r * tile + lax.broadcasted_iota(jnp.int32, s.shape, 0)
                 s = jnp.where(row >= lax.broadcasted_iota(jnp.int32, s.shape, 1), s, -jnp.inf)
             else:
-                s = jnp.where(position_ref[0] >= lag, s, -jnp.inf)
+                s = jnp.where(position >= lag, s, -jnp.inf)
             scores.append(s)
         peak = functools.reduce(jnp.maximum, [jnp.max(s, axis=1, keepdims=True) for s in scores])
         total, output = 0.0, 0.0
-        for s, ref in zip(scores, kv_refs):
+        for s, (_, values) in zip(scores, pairs):
             expo = jnp.exp(s - peak)
             total = total + jnp.sum(expo, axis=1, keepdims=True)
-            output = output + jnp.dot(expo.astype(jnp.bfloat16), ref[1, : s.shape[1]], preferred_element_type=jnp.float32)
-        out_ref[r * tile : (r + 1) * tile] = (output / total).astype(jnp.bfloat16)
-
-
-def attend(position, query, blocks, half, before):
-    _, tokens, cols = query.shape
-    heads = cols // HD // HALVES
-    ahead = half * heads
-    pair = pl.BlockSpec((2, tokens, HD), lambda h, position: (0, 0, h))
-    extra = [] if before is None else [before]
-    return pl.pallas_call(
-        attend_kernel,
-        grid_spec=pltpu.PrefetchScalarGridSpec(
-            num_scalar_prefetch=1,
-            grid=(heads,),
-            in_specs=[pl.BlockSpec((1, tokens, HD), lambda h, position: (0, 0, h + ahead))]
-            + [pair] * len(blocks)
-            + [pl.BlockSpec(memory_space=pl.ANY)] * len(extra),
-            out_specs=pl.BlockSpec((tokens, HD), lambda h, position: (0, h + ahead)),
-            scratch_shapes=[pltpu.VMEM((2, tokens, HD), jnp.bfloat16)],
+            output = output + jnp.dot(expo.astype(jnp.bfloat16), values[: s.shape[1]], preferred_element_type=jnp.float32)
+        outputs.append((output / total).astype(jnp.bfloat16))
+    return outputs
+
+
+def attention_kernel(
+    normed_ref, rows_ref, out_ref, w_kv, w_q, own, near, far, query, load_sem, near_send, near_recv, far_send, far_recv, relay_send
+):
+    count = lax.axis_size("ctx")
+    me = lax.axis_index("ctx")
+    even = lax.rem(me, 2) == 0
+    chunks, _, tokens, width = own.shape
+    steps, _, depth = normed_ref.shape
+    group = rows_ref.shape[0] // steps
+    has_next, has_before = me < count - 1, me >= 1
+    sends_far = even & (me < count - 2)
+    gets_far = me >= 2
+    relays = even & (me >= 2)
+
+    def load(c, stream):
+        source = rows_ref.at[:, stream, :, c * width : (c + 1) * width]
+        target = w_q.at[c] if stream == 0 else w_kv.at[c, stream - 1]
+        return pltpu.make_async_copy(source, target, load_sem.at[c, stream])
+
+    def wait_load(c, stream):
+        target = w_q.at[c] if stream == 0 else w_kv.at[c, stream - 1]
+        pltpu.make_async_copy(target, target, load_sem.at[c, stream]).wait()
+
+    def remote(source, target, send, recv, device):
+        return pltpu.make_async_remote_copy(
+            src_ref=source,
+            dst_ref=target,
+            send_sem=send,
+            recv_sem=recv,
+            device_id={"ctx": device},
+            device_id_type=pl.DeviceIdType.MESH,
+        )
+
+    def send_near(c):
+        return remote(own.at[c], near.at[c], near_send.at[c], near_recv.at[c], me + 1)
+
+    def send_far(c):
+        return remote(own.at[c], far.at[c], far_send.at[c], far_recv.at[c], me + 2)
+
+    def send_relay(c):
+        return remote(near.at[c], far.at[c], relay_send.at[c], far_recv.at[c], me + 1)
+
+    for c in range(chunks):
+        for stream in (1, 2):
+            load(c, stream).start()
+    for c in range(chunks):
+        load(c, 0).start()
+
+    barrier = pltpu.get_barrier_semaphore()
+    for there, step in ((has_next, 1), (has_before, -1), (sends_far, 2), (relays, -2)):
+
+        @pl.when(there)
+        def _():
+            pl.semaphore_signal(barrier, inc=1, device_id={"ctx": me + step}, device_id_type=pl.DeviceIdType.MESH)
+
+    greeted = [jnp.where(there, 1, 0) for there in (has_next, has_before, sends_far, relays)]
+    pl.semaphore_wait(barrier, sum(greeted))
+
+    @pl.when(jnp.logical_not(has_before))
+    def _():
+        near[...] = jnp.zeros_like(near)
+
+    @pl.when(jnp.logical_not(gets_far))
+    def _():
+        far[...] = jnp.zeros_like(far)
+
+    def product(weights):
+        total = 0.0
+        for k in range(steps):
+            part = weights[k * group : (k + 1) * group].reshape(depth, width)
+            total = total + jnp.dot(normed_ref[k], part, preferred_element_type=jnp.float32)
+        return total.astype(jnp.bfloat16)
+
+    @pl.loop(0, chunks)
+    def _(c):
+        for i in range(2):
+            wait_load(c, i + 1)
+            own[c, i] = product(w_kv.at[c, i])
+
+        @pl.when(has_next)
+        def _():
+            send_near(c).start()
+
+        @pl.when(sends_far)
+        def _():
+            send_far(c).start()
+
+    @pl.loop(0, chunks)
+    def _(c):
+        wait_load(c, 0)
+        query[c] = product(w_q.at[c])
+
+    @pl.loop(0, chunks)
+    def _(c):
+        @pl.when(has_before)
+        def _():
+            send_near(c).wait_recv()
+
+        @pl.when(relays)
+        def _():
+            send_relay(c).start()
+
+        @pl.when(gets_far)
+        def _():
+            send_far(c).wait_recv()
+
+        for head in range(width // HD):
+            cols = slice(head * HD, (head + 1) * HD)
+            pairs = [(ref[c, 0, :, cols], ref[c, 1, :, cols]) for ref in (own, near, far)]
+            outputs = head_attention(query[c, :, cols], pairs, me, tokens)
+            tile = tokens // len(outputs)
+            for r, value in enumerate(outputs):
+                out_ref[c, r * tile : (r + 1) * tile, cols] = value
+
+    @pl.loop(0, chunks)
+    def _(c):
+        @pl.when(has_next)
+        def _():
+            send_near(c).wait_send()
+
+        @pl.when(sends_far)
+        def _():
+            send_far(c).wait_send()
+
+        @pl.when(relays)
+        def _():
+            send_relay(c).wait_send()
+
+
+def attention_part(normed, rows):
+    steps, tokens, depth = normed.shape
+    shards, _, per_shard, cols = rows.shape
+    width = min(cols, 2 * HD)
+    chunks = cols // width
+    bf16 = jnp.bfloat16
+    out = pl.pallas_call(
+        attention_kernel,
+        in_specs=[pl.BlockSpec(memory_space=pltpu.VMEM), pl.BlockSpec(memory_space=pl.ANY)],
+        out_specs=pl.BlockSpec(memory_space=pltpu.VMEM),
+        out_shape=jax.ShapeDtypeStruct((chunks, tokens, width), bf16),
+        scratch_shapes=[
+            pltpu.VMEM((chunks, 2, shards, per_shard, width), bf16),
+            pltpu.VMEM((chunks, shards, per_shard, width), bf16),
+            pltpu.VMEM((chunks, 2, tokens, width), bf16),
+            pltpu.VMEM((chunks, 2, tokens, width), bf16),
+            pltpu.VMEM((chunks, 2, tokens, width), bf16),
+            pltpu.VMEM((chunks, tokens, width), bf16),
+            pltpu.SemaphoreType.DMA((chunks, 3)),
+        ]
+        + [pltpu.SemaphoreType.DMA((chunks,))] * 5,
+        compiler_params=pltpu.CompilerParams(vmem_limit_bytes=52 * MIB, collective_id=0, has_side_effects=True),
+        cost_estimate=pl.CostEstimate(
+            flops=2 * tokens * shards * per_shard * cols * 3, bytes_accessed=rows.size * 2, transcendentals=0
         ),
-        out_shape=jax.ShapeDtypeStruct((tokens, cols), jnp.bfloat16),
-        input_output_aliases={2 + len(blocks): 0} if extra else {},
-        compiler_params=pltpu.CompilerParams(vmem_limit_bytes=32 * MIB),
-        cost_estimate=pl.CostEstimate(flops=4 * tokens * tokens * 3 * cols // HALVES, bytes_accessed=16 * tokens * cols // HALVES, transcendentals=0),
-        name="windowed_attention",
-    )(position, query, *blocks, *extra)
-
-
-def window_blocks(own):
-    count = lax.axis_size("ctx")
-    near = shifted(own, "ctx", 1)
-    even = lax.ppermute(own, "ctx", [(s, s + 2) for s in range(0, count - 2, 2)])
-    odd = lax.ppermute(near, "ctx", [(s, s + 1) for s in range(0, count - 1, 2)])
-    return (own, near, even, odd)
+        name="projections_and_attention",
+    )(normed, rows)
+    return out.transpose(1, 0, 2).reshape(tokens, cols)
 
 
 def on_device(features, short_filter, decay_rate, residue, skip_gain, norm_gain, qkv_weight):
@@ -358,16 +428,7 @@
     place = lax.axis_index("tp").astype(jnp.int32).reshape(1)
     group = math.gcd(4, rows.shape[0] // len(parts))
     normed = norm_part(place, parts, norm_gain, pieces, group * rows.shape[2])
-    windows = []
-    for half in range(HALVES):
-        pair = project(place, normed, rows, pieces, group, (1, 2), half, HALVES)
-        windows.append(window_blocks(pair))
-    query = project(place, normed, rows, pieces, group, (0,), 0, 1)
-    position = lax.axis_index("ctx").astype(jnp.int32).reshape(1)
-    attended = None
-    for half in range(HALVES):
-        attended = attend(position, query, windows[half], half, attended)
-    return (jnp.concatenate(own, axis=1), attended)
+    return (jnp.concatenate(own, axis=1), attention_part(normed, rows))
 
 
 def solution(mesh):

time: 243 us -> 219 us (0.901); the launches traced: 242 us -> 215 us
  starting transfers between devices: 48.2 us -> 18.8 us
  Pallas kernels: 81.7 us -> 101 us
  waiting for transfers between devices: 83.8 us -> 68.5 us
    ppermute x10 -> x8, waiting for transfers between devices: 40.9 us -> 19 us  [shifted(): lax.ppermute(value, axis, [(source, source + steps) for source in range(c...]
    pallas_call x5 -> x1, Pallas kernels: 41 us -> 60.7 us  [attention_part(): pl.pallas_call(attention_kernel, in_specs=[pl.BlockSpec(memory_space=pltp...]
    ppermute x4 -> x0, starting transfers between devices: 18.5 us -> none  [the longest x2 13.9 us: window_blocks(): lax.ppermute(near, 'ctx', [(s, s + 1) for s in range(0, count - 1, 2)])]
    ppermute x10 -> x8, starting transfers between devices: 27.5 us -> 16.7 us  [shifted(): lax.ppermute(value, axis, [(source, source + steps) for source in range(c...]
    all_gather x1, waiting for transfers between devices: 1.08 us -> 6.73 us  [on_device(): rows = lax.all_gather(weights, 'ctx')]
    unnamed x18 -> x15, local copies, waits for them, and re-layouts: 11.2 us -> 8.89 us
  transfers between devices with their start and end apart: 17 -> 11, of which waited for: 11 -> 9; matrix products, arithmetic and copies ran while one was open for 1% -> 1% of each run, Pallas kernels for 27% -> 19%
where the time goes in v3:
time: 219 us; the launch traced here: 215 us
  Pallas kernels  101 us (46%)
  waiting for transfers between devices  68.5 us (31%)
  starting transfers between devices  18.8 us (9%)
  between operations  14.2 us (6%)
  local copies, waits for them, and re-layouts  10.4 us (5%)
    pallas_call x1, Pallas kernels, attention_part(): pl.pallas_call(attention_kernel, in_specs=[pl.BlockSpec(memory_space=pltp...  60.7 us
    ppermute x2, waiting for transfers between devices, on_device(): others[step - 1].append(lax.ppermute(own[-1], 'tp', source))  42.1 us
    pallas_call x1, Pallas kernels, short_part(): pl.pallas_call(short_kernel, grid=(channels // LANES,), in_specs=[pl.Bloc...  20.1 us
    ppermute x8, waiting for transfers between devices, shifted(): lax.ppermute(value, axis, [(source, source + steps) for source in range(c...  19 us
    pallas_call x2, Pallas kernels, long_part(): pl.pallas_call(long_kernel, grid=(channels // LANES,), in_specs=[by_token...  16.9 us
    ppermute x8, starting transfers between devices, shifted(): lax.ppermute(value, axis, [(source, source + steps) for source in range(c...  16.7 us
    unnamed x15, local copies, waits for them, and re-layouts  8.89 us
    all_gather x1, waiting for transfers between devices, on_device(): rows = lax.all_gather(weights, 'ctx')  6.73 us
  transfers between devices with their start and end apart: 11, of which 9 were waited for; matrix products, arithmetic and copies ran while one was open for 1% of the time, Pallas kernels for 19%

profile of v3, /device:TPU:16, one launch (start us, length us, event | category | flops | bytes accessed | tf_op | source)
XLA Modules:
  0.0 215.2 jit_solution(10783035060693422858)
XLA Ops:
  7.2 0.0 all-gather.3.cloned.1.call-start
  7.2 0.7 all-gather.3.cloned.1.call-update
  7.9 0.0 copy-start.3
  7.9 0.0 copy-start.5
  7.9 1.0 slice.4
  8.9 1.9 collective-permute-start
  10.8 6.0 %collective-permute-done.halo_ref = bf16[3,16,2048]{2,1,0:T(8,128)(2,1)S(1)} collective-permute-done((bf16[3,16,2048]{2,1,0:T(8,128)(2,1)S(1)}, bf16[3,16,2048]{2,1,0:T(8,128)(2,1)S(1)}, u32[]{:S(2)}, u32[]{:S(2)}) %collective-permute-start) | collective-permute-done | bytes 196640 | tf_op jit(solution)/shard_map/ppermute | solution.py:25
  16.8 0.0 copy-start
  16.8 3.8 %copy-done = bf16[512,3,2048]{2,0,1:T(8,128)(2,1)S(1)} copy-done((bf16[512,3,2048]{2,0,1:T(8,128)(2,1)S(1)}, bf16[512,3,2048]{2,0,1:T(8,128)(2,1)}, u32[]{:S(2)}) %copy-start) | copy-done | bytes 6291480
  20.6 0.0 copy-start.2
  20.6 0.9 copy-done.2
  21.5 0.0 copy-start.4
  21.5 0.9 copy-done.4
  22.4 20.1 %short_and_end_states.1 = (bf16[512,2048]{1,0:T(8,128)(2,1)S(1)}, f32[512,2048]{1,0:T(8,128)S(1)}, f32[8,16,2048]{2,1,0:T(8,128)S(1)}, f32[16,2048]{1,0:T(8,128)S(1)}) custom-call(bf16[3,512,2048]{2,1,0:T(8,128)(2,1)S(1)} %bitcast.8, bf16[3,16,2048]{2,1,0:T(8,128)(2,1)S(1)} %collective-permute-done.halo_ref, f32[3,7,2048]{2,1,0:T(8,128)S(1)} %copy-done.4, ...), custom_call_target="tpu_custom_call" | custom-call | flops 104857600 | bytes 13631488 | tf_op jit(solution)/shard_map/short_and_end_states/pallas_call | solution.py:101
  42.6 1.9 collective-permute-start.1
  44.5 2.5 %collective-permute-start.2 = (bf16[16,2048]{1,0:T(8,128)(2,1)S(1)}, bf16[16,2048]{1,0:T(8,128)(2,1)S(1)}, u32[]{:S(2)}, u32[]{:S(2)}) collective-permute-start(bf16[16,2048]{1,0:T(8,128)(2,1)S(1)} %convert_element_type.27), channel_id=1, source_target_pairs={{0,4},{2,6},{4,8},{6,10},{8,12},{10,14},{12,16},{14,18},{16,20},{1... | collective-permute-start | bytes 196616 | tf_op jit(solution)/shard_map/ppermute | solution.py:25
  47.0 4.4 %collective-permute-start.3 = (bf16[16,2048]{1,0:T(8,128)(2,1)S(1)}, bf16[16,2048]{1,0:T(8,128)(2,1)S(1)}, u32[]{:S(2)}, u32[]{:S(2)}) collective-permute-start(bf16[16,2048]{1,0:T(8,128)(2,1)S(1)} %convert_element_type.27), channel_id=1, source_target_pairs={{0,6},{2,8},{4,10},{6,12},{8,14},{10,16},{12,18},{14,20},{16,22},{... | collective-permute-start | bytes 196616 | tf_op jit(solution)/shard_map/ppermute | solution.py:25
  51.4 1.9 collective-permute-start.4
  53.4 0.0 collective-permute-done.1
  53.4 0.2 collective-permute-done.2
  53.5 1.0 collective-permute-done.3
  54.5 4.7 %collective-permute-done.4 = bf16[16,2048]{1,0:T(8,128)(2,1)S(1)} collective-permute-done((bf16[16,2048]{1,0:T(8,128)(2,1)S(1)}, bf16[16,2048]{1,0:T(8,128)(2,1)S(1)}, u32[]{:S(2)}, u32[]{:S(2)}) %collective-permute-start.4) | collective-permute-done | bytes 65568 | tf_op jit(solution)/shard_map/ppermute | solution.py:25
  59.2 0.1 fusion
  59.3 2.1 collective-permute-start.5
  61.4 1.3 collective-permute-start.6
  62.7 0.7 collective-permute-start.7
  63.4 5.0 %collective-permute-done.5 = bf16[16,2048]{1,0:T(8,128)(2,1)S(1)} collective-permute-done((bf16[16,2048]{1,0:T(8,128)(2,1)S(1)}, bf16[16,2048]{1,0:T(8,128)(2,1)S(1)}, u32[]{:S(2)}, u32[]{:S(2)}) %collective-permute-start.5) | collective-permute-done | bytes 65568 | tf_op jit(solution)/shard_map/ppermute | solution.py:25
  68.4 2.1 collective-permute-done.6
  70.5 0.0 collective-permute-done.7
  70.5 0.2 multiply_add_fusion.state_ref
  70.7 0.0 copy-done.3
  70.7 0.0 copy-done.5
  70.7 8.5 %modal_filter.2.refs_0_ = bf16[512,1024]{1,0:T(8,128)(2,1)S(1)} custom-call(bf16[512,2048]{1,0:T(8,128)(2,1)S(1)} %get-tuple-element.6.gated_ref, f32[512,2048]{1,0:T(8,128)S(1)} %get-tuple-element.7.first_ref, f32[8,16,2048]{2,1,0:T(8,128)S(1)} %get-tuple-element.8.enter_ref, f32[16,2048]{1,0:T(8,128)S(1)} %multiply_add_fusion.state_ref, ...), custom_call_target="tpu_custom_call" | custom-call | flops 52428800 | bytes 5242880 | tf_op jit(solution)/shard_map/modal_filter/pallas_call | solution.py:141
  79.2 0.0 copy-start.6
  79.2 8.5 %modal_filter.3.refs_1_ = bf16[512,1024]{1,0:T(8,128)(2,1)S(1)} custom-call(bf16[512,2048]{1,0:T(8,128)(2,1)S(1)} %get-tuple-element.6.gated_ref, f32[512,2048]{1,0:T(8,128)S(1)} %get-tuple-element.7.first_ref, f32[8,16,2048]{2,1,0:T(8,128)S(1)} %get-tuple-element.8.enter_ref, f32[16,2048]{1,0:T(8,128)S(1)} %multiply_add_fusion.state_ref, ...), custom_call_target="tpu_custom_call" | custom-call | flops 52428800 | bytes 5242880 | tf_op jit(solution)/shard_map/modal_filter/pallas_call | solution.py:141
  87.7 1.6 collective-permute-start.8
  89.2 0.5 collective-permute-start.9
  89.8 0.0 copy-done.6
  89.8 1.5 pad_maximum_fusion
  91.3 22.5 %collective-permute-done.8.refs_2_ = bf16[512,1024]{1,0:T(8,128)(2,1)S(1)} collective-permute-done((bf16[512,1024]{1,0:T(8,128)(2,1)S(1)}, bf16[512,1024]{1,0:T(8,128)(2,1)S(1)}, u32[]{:S(2)}, u32[]{:S(2)}) %collective-permute-start.8) | collective-permute-done | bytes 1048608 | tf_op jit(solution)/shard_map/ppermute | solution.py:426
  113.8 19.6 %collective-permute-done.9.refs_3_ = bf16[512,1024]{1,0:T(8,128)(2,1)} collective-permute-done((bf16[512,1024]{1,0:T(8,128)(2,1)S(1)}, bf16[512,1024]{1,0:T(8,128)(2,1)}, u32[]{:S(2)}, u32[]{:S(2)}) %collective-permute-start.9) | collective-permute-done | bytes 1048608 | tf_op jit(solution)/shard_map/ppermute | solution.py:426
  133.4 3.7 %norm.1.normed_ref = bf16[4,512,1024]{2,1,0:T(8,128)(2,1)S(1)} custom-call(s32[1]{0:T(128)} %bitcast.2.place_ref, bf16[512,1024]{1,0:T(8,128)(2,1)S(1)} %modal_filter.2.refs_0_, bf16[512,1024]{1,0:T(8,128)(2,1)S(1)} %modal_filter.3.refs_1_, bf16[512,1024]{1,0:T(8,128)(2,1)S(1)} %collective-permute-done.8.refs_2_, ...), custom_call_target="tpu_custom_call" | custom-call | flops 16777216 | bytes 8388608 | tf_op jit(solution)/shard_map/norm/pallas_call | solution.py:209
  137.1 0.0 copy-start.1
  137.1 2.0 copy-done.1
  139.1 6.7 %all-gather.3.cloned.1.call-done = bf16[48,256,1024]{2,1,0:T(8,128)(2,1)} async-done(((bf16[3,256,1024]{2,1,0:T(8,128)(2,1)}), bf16[48,256,1024]{2,1,0:T(8,128)(2,1)}) %all-gather.3.cloned.1.call-update) | async-done | bytes 25165840 | tf_op jit(solution)/shard_map/all_gather | solution.py:416
  145.8 60.7 %projections_and_attention.1 = bf16[4,512,256]{2,1,0:T(8,128)(2,1)S(1)} custom-call(bf16[4,512,1024]{2,1,0:T(8,128)(2,1)} %copy-done.1, bf16[16,3,256,1024]{3,2,1,0:T(8,128)(2,1)} %bitcast.14), custom_call_target="tpu_custom_call" | custom-call | flops 12884901888 | bytes 25165824 | tf_op jit(solution)/shard_map/projections_and_attention/pallas_call | solution.py:387
  206.5 0.5 copy.11
  207.0 1.3 copy.12
  (2 shorter events, 0.0 us)
Async XLA Ops:
  7.2 138.6 %all-gather.3.cloned.1.call-start = ((), (), s32[]{:S(2)}) async-start(), calls=%async_computation | async-start | bytes 26738688 | tf_op jit(solution)/shard_map/all_gather | solution.py:416
  7.9 62.8 %copy-start.3 = (f32[16,2048]{1,0:T(8,128)S(1)}, f32[16,2048]{1,0:T(8,128)}, u32[]{:S(2)}) copy-start(f32[16,2048]{1,0:T(8,128)} %residue_ref.3) | copy-start | bytes 393220
  7.9 62.8 %copy-start.5 = (f32[2048]{0:T(1024)S(1)}, f32[2048]{0:T(1024)}, u32[]{:S(2)}) copy-start(f32[2048]{0:T(1024)} %param.11) | copy-start | bytes 24580
  8.9 7.9 %collective-permute-start = (bf16[3,16,2048]{2,1,0:T(8,128)(2,1)S(1)}, bf16[3,16,2048]{2,1,0:T(8,128)(2,1)S(1)}, u32[]{:S(2)}, u32[]{:S(2)}) collective-permute-start(bf16[3,16,2048]{2,1,0:T(8,128)(2,1)S(1)} %slice.4), channel_id=1, source_target_pairs={{0,2},{2,4},{4,6},{6,8},{8,10},{10,12},{12,14},{14,16},{16,18},{18... | collective-permute-start | bytes 589832 | tf_op jit(solution)/shard_map/ppermute | solution.py:25
  16.8 3.8 %copy-start = (bf16[512,3,2048]{2,0,1:T(8,128)(2,1)S(1)}, bf16[512,3,2048]{2,0,1:T(8,128)(2,1)}, u32[]{:S(2)}) copy-start(bf16[512,3,2048]{2,0,1:T(8,128)(2,1)} %param.7) | copy-start | bytes 18874372
  20.6 0.9 copy-start.2
  21.5 0.9 copy-start.4
  42.6 10.8 %collective-permute-start.1 = (bf16[16,2048]{1,0:T(8,128)(2,1)S(1)}, bf16[16,2048]{1,0:T(8,128)(2,1)S(1)}, u32[]{:S(2)}, u32[]{:S(2)}) collective-permute-start(bf16[16,2048]{1,0:T(8,128)(2,1)S(1)} %convert_element_type.27), channel_id=1, source_target_pairs={{0,2},{2,4},{4,6},{6,8},{8,10},{10,12},{12,14},{14,16},{16,18},{18... | collective-permute-start | bytes 196616 | tf_op jit(solution)/shard_map/ppermute | solution.py:25
  44.5 9.0 %collective-permute-start.2 = (bf16[16,2048]{1,0:T(8,128)(2,1)S(1)}, bf16[16,2048]{1,0:T(8,128)(2,1)S(1)}, u32[]{:S(2)}, u32[]{:S(2)}) collective-permute-start(bf16[16,2048]{1,0:T(8,128)(2,1)S(1)} %convert_element_type.27), channel_id=1, source_target_pairs={{0,4},{2,6},{4,8},{6,10},{8,12},{10,14},{12,16},{14,18},{16,20},{1... | collective-permute-start | bytes 196616 | tf_op jit(solution)/shard_map/ppermute | solution.py:25
  47.0 7.5 %collective-permute-start.3 = (bf16[16,2048]{1,0:T(8,128)(2,1)S(1)}, bf16[16,2048]{1,0:T(8,128)(2,1)S(1)}, u32[]{:S(2)}, u32[]{:S(2)}) collective-permute-start(bf16[16,2048]{1,0:T(8,128)(2,1)S(1)} %convert_element_type.27), channel_id=1, source_target_pairs={{0,6},{2,8},{4,10},{6,12},{8,14},{10,16},{12,18},{14,20},{16,22},{... | collective-permute-start | bytes 196616 | tf_op jit(solution)/shard_map/ppermute | solution.py:25
  51.4 7.8 %collective-permute-start.4 = (bf16[16,2048]{1,0:T(8,128)(2,1)S(1)}, bf16[16,2048]{1,0:T(8,128)(2,1)S(1)}, u32[]{:S(2)}, u32[]{:S(2)}) collective-permute-start(bf16[16,2048]{1,0:T(8,128)(2,1)S(1)} %convert_element_type.27), channel_id=1, source_target_pairs={{0,8},{2,10},{4,12},{6,14},{8,16},{10,18},{12,20},{14,22},{16,24},... | collective-permute-start | bytes 196616 | tf_op jit(solution)/shard_map/ppermute | solution.py:25
  59.3 9.1 %collective-permute-start.5 = (bf16[16,2048]{1,0:T(8,128)(2,1)S(1)}, bf16[16,2048]{1,0:T(8,128)(2,1)S(1)}, u32[]{:S(2)}, u32[]{:S(2)}) collective-permute-start(bf16[16,2048]{1,0:T(8,128)(2,1)S(1)} %fusion), channel_id=1, source_target_pairs={{0,8},{2,10},{4,12},{6,14},{8,16},{10,18},{12,20},{14,22},{16,24},... | collective-permute-start | bytes 196616 | tf_op jit(solution)/shard_map/ppermute | solution.py:25
  61.4 9.1 %collective-permute-start.6 = (bf16[16,2048]{1,0:T(8,128)(2,1)S(1)}, bf16[16,2048]{1,0:T(8,128)(2,1)S(1)}, u32[]{:S(2)}, u32[]{:S(2)}) collective-permute-start(bf16[16,2048]{1,0:T(8,128)(2,1)S(1)} %fusion), channel_id=1, source_target_pairs={{0,16},{2,18},{4,20},{6,22},{8,24},{10,26},{12,28},{14,30},{1,17},... | collective-permute-start | bytes 196616 | tf_op jit(solution)/shard_map/ppermute | solution.py:25
  62.7 7.8 %collective-permute-start.7 = (bf16[16,2048]{1,0:T(8,128)(2,1)S(1)}, bf16[16,2048]{1,0:T(8,128)(2,1)S(1)}, u32[]{:S(2)}, u32[]{:S(2)}) collective-permute-start(bf16[16,2048]{1,0:T(8,128)(2,1)S(1)} %fusion), channel_id=1, source_target_pairs={{0,24},{2,26},{4,28},{6,30},{1,25},{3,27},{5,29},{7,31}} | collective-permute-start | bytes 196616 | tf_op jit(solution)/shard_map/ppermute | solution.py:25
  79.2 10.6 %copy-start.6 = (f32[4096]{0:T(1024)S(1)}, f32[4096]{0:T(1024)}, u32[]{:S(2)}) copy-start(f32[4096]{0:T(1024)} %param.12) | copy-start | bytes 49156
  87.7 26.2 %collective-permute-start.8 = (bf16[512,1024]{1,0:T(8,128)(2,1)S(1)}, bf16[512,1024]{1,0:T(8,128)(2,1)S(1)}, u32[]{:S(2)}, u32[]{:S(2)}) collective-permute-start(bf16[512,1024]{1,0:T(8,128)(2,1)S(1)} %modal_filter.2.refs_0_), channel_id=1, source_target_pairs={{0,1},{1,0},{2,3},{3,2},{4,5},{5,4},{6,7},{7,6},{8,9},{9,8},{10,11... | collective-permute-start | bytes 3145736 | tf_op jit(solution)/shard_map/ppermute | solution.py:426
  89.2 44.2 %collective-permute-start.9 = (bf16[512,1024]{1,0:T(8,128)(2,1)S(1)}, bf16[512,1024]{1,0:T(8,128)(2,1)}, u32[]{:S(2)}, u32[]{:S(2)}) collective-permute-start(bf16[512,1024]{1,0:T(8,128)(2,1)S(1)} %modal_filter.3.refs_1_), channel_id=1, source_target_pairs={{0,1},{1,0},{2,3},{3,2},{4,5},{5,4},{6,7},{7,6},{8,9},{9,8},{10,11... | collective-permute-start | bytes 3145736 | tf_op jit(solution)/shard_map/ppermute | solution.py:426
  137.1 2.0 copy-start.1
Sparse Core Ops, SparseCore 0:
  9.6 136.1 all-gather.2

commit v4 on v3

--- a/solution.py
+++ b/solution.py
@@ -222,35 +222,32 @@
     )(place, *xs, gain.reshape(len(xs), width))
 
 
-def head_attention(query, pairs, position, tokens):
-    tile = math.gcd(tokens, 256)
+def partial_attention(query, first_row, blocks, position):
     contract = (((1,), (1,)), ((), ()))
-    outputs = []
-    for r in range(tokens // tile):
-        rows = query[r * tile : (r + 1) * tile]
-        scores = []
-        for lag, (keys, _) in enumerate(pairs):
-            if lag == 0:
-                keys = keys[: (r + 1) * tile]
-            s = lax.dot_general(rows, keys, contract, preferred_element_type=jnp.float32) * (1.0 / math.sqrt(HD))
-            if lag == 0:
-                row = r * tile + lax.broadcasted_iota(jnp.int32, s.shape, 0)
-                s = jnp.where(row >= lax.broadcasted_iota(jnp.int32, s.shape, 1), s, -jnp.inf)
-            else:
-                s = jnp.where(position >= lag, s, -jnp.inf)
-            scores.append(s)
-        peak = functools.reduce(jnp.maximum, [jnp.max(s, axis=1, keepdims=True) for s in scores])
-        total, output = 0.0, 0.0
-        for s, (_, values) in zip(scores, pairs):
-            expo = jnp.exp(s - peak)
-            total = total + jnp.sum(expo, axis=1, keepdims=True)
-            output = output + jnp.dot(expo.astype(jnp.bfloat16), values[: s.shape[1]], preferred_element_type=jnp.float32)
-        outputs.append((output / total).astype(jnp.bfloat16))
-    return outputs
+    scores = []
+    for lag, keys, _ in blocks:
+        s = lax.dot_general(query, keys, contract, preferred_element_type=jnp.float32) * (1.0 / math.sqrt(HD))
+        if lag == 0:
+            row = first_row + lax.broadcasted_iota(jnp.int32, s.shape, 0)
+            s = jnp.where(row >= lax.broadcasted_iota(jnp.int32, s.shape, 1), s, -jnp.inf)
+        else:
+            s = jnp.where(position >= lag, s, -jnp.inf)
+        scores.append(s)
+    peak = functools.reduce(jnp.maximum, [jnp.max(s, axis=1, keepdims=True) for s in scores])
+    return scores, peak
+
+
+def weigh(scores, peak, blocks):
+    total, output = 0.0, 0.0
+    for s, (_, _, values) in zip(scores, blocks):
+        expo = jnp.exp(s - peak)
+        total = total + jnp.sum(expo, axis=1, keepdims=True)
+        output = output + jnp.dot(expo.astype(jnp.bfloat16), values, preferred_element_type=jnp.float32)
+    return total, output
 
 
 def attention_kernel(
-    normed_ref, rows_ref, out_ref, w_kv, w_q, own, near, far, query, load_sem, near_send, near_recv, far_send, far_recv, relay_send
+    normed_ref, rows_ref, out_ref, w_kv, w_q, own, near, far, query, load_sem, near_send, near_recv, far_send, far_recv, relay_send, peaks, totals, outputs
 ):
     count = lax.axis_size("ctx")
     me = lax.axis_index("ctx")
@@ -264,7 +261,7 @@
     relays = even & (me >= 2)
 
     def load(c, stream):
-        source = rows_ref.at[:, stream, :, c * width : (c + 1) * width]
+        source = rows_ref.at[:, stream, :, pl.ds(pl.multiple_of(c * width, width), width)]
         target = w_q.at[c] if stream == 0 else w_kv.at[c, stream - 1]
         return pltpu.make_async_copy(source, target, load_sem.at[c, stream])
 
@@ -291,11 +288,8 @@
     def send_relay(c):
         return remote(near.at[c], far.at[c], relay_send.at[c], far_recv.at[c], me + 1)
 
-    for c in range(chunks):
-        for stream in (1, 2):
-            load(c, stream).start()
-    for c in range(chunks):
-        load(c, 0).start()
+    for stream in (1, 2):
+        load(0, stream).start()
 
     barrier = pltpu.get_barrier_semaphore()
     for there, step in ((has_next, 1), (has_before, -1), (sends_far, 2), (relays, -2)):
@@ -324,6 +318,12 @@
 
     @pl.loop(0, chunks)
     def _(c):
+        @pl.when(c < chunks - 1)
+        def _():
+            for stream in (1, 2):
+                load(c + 1, stream).start()
+
+        load(c, 0).start()
         for i in range(2):
             wait_load(c, i + 1)
             own[c, i] = product(w_kv.at[c, i])
@@ -351,17 +351,30 @@
         def _():
             send_relay(c).start()
 
+        tile = math.gcd(tokens, 256)
+        tiles = [(head * HD, r * tile) for head in range(width // HD) for r in range(tokens // tile)]
+
+        def block(ref, lag, col, keys):
+            return lag, ref[c, 0, :keys, col : col + HD], ref[c, 1, :keys, col : col + HD]
+
+        for at, (col, row) in enumerate(tiles):
+            blocks = [block(own, 0, col, row + tile), block(near, 1, col, tokens)]
+            scores, peak = partial_attention(query[c, row : row + tile, col : col + HD], row, blocks, me)
+            total, output = weigh(scores, peak, blocks)
+            peaks[at], totals[at], outputs[at] = peak, total, output
+
         @pl.when(gets_far)
         def _():
             send_far(c).wait_recv()
 
-        for head in range(width // HD):
-            cols = slice(head * HD, (head + 1) * HD)
-            pairs = [(ref[c, 0, :, cols], ref[c, 1, :, cols]) for ref in (own, near, far)]
-            outputs = head_attention(query[c, :, cols], pairs, me, tokens)
-            tile = tokens // len(outputs)
-            for r, value in enumerate(outputs):
-                out_ref[c, r * tile : (r + 1) * tile, cols] = value
+        for at, (col, row) in enumerate(tiles):
+            blocks = [block(far, 2, col, tokens)]
+            scores, peak = partial_attention(query[c, row : row + tile, col : col + HD], row, blocks, me)
+            both = jnp.maximum(peak, peaks[at])
+            total, output = weigh(scores, both, blocks)
+            scale = jnp.exp(peaks[at] - both)
+            output = (outputs[at] * scale + output) / (totals[at] * scale + total)
+            out_ref[c, row : row + tile, col : col + HD] = output.astype(jnp.bfloat16)
 
     @pl.loop(0, chunks)
     def _(c):
@@ -383,6 +396,8 @@
     shards, _, per_shard, cols = rows.shape
     width = min(cols, 2 * HD)
     chunks = cols // width
+    tile = math.gcd(tokens, 256)
+    tiles = (width // HD) * (tokens // tile)
     bf16 = jnp.bfloat16
     out = pl.pallas_call(
         attention_kernel,
@@ -398,7 +413,9 @@
             pltpu.VMEM((chunks, tokens, width), bf16),
             pltpu.SemaphoreType.DMA((chunks, 3)),
         ]
-        + [pltpu.SemaphoreType.DMA((chunks,))] * 5,
+        + [pltpu.SemaphoreType.DMA((chunks,))] * 5
+        + [pltpu.VMEM((tiles, tile, 1), jnp.float32)] * 2
+        + [pltpu.VMEM((tiles, tile, HD), jnp.float32)],
         compiler_params=pltpu.CompilerParams(vmem_limit_bytes=52 * MIB, collective_id=0, has_side_effects=True),
         cost_estimate=pl.CostEstimate(
             flops=2 * tokens * shards * per_shard * cols * 3, bytes_accessed=rows.size * 2, transcendentals=0

time: 219 us -> 218 us (level)
  no operation moved by 1% of the time
where the time goes in v4:
time: 218 us; the launch traced here: 216 us
  Pallas kernels  102 us (47%)
  waiting for transfers between devices  68.5 us (31%)
  starting transfers between devices  18.8 us (9%)
  between operations  14.2 us (7%)
  local copies, waits for them, and re-layouts  10.4 us (5%)
    pallas_call x1, Pallas kernels, attention_part(): pl.pallas_call(attention_kernel, in_specs=[pl.BlockSpec(memory_space=pltp...  61.3 us
    ppermute x2, waiting for transfers between devices, on_device(): others[step - 1].append(lax.ppermute(own[-1], 'tp', source))  42.1 us
    pallas_call x1, Pallas kernels, short_part(): pl.pallas_call(short_kernel, grid=(channels // LANES,), in_specs=[pl.Bloc...  20.1 us
    ppermute x8, waiting for transfers between devices, shifted(): lax.ppermute(value, axis, [(source, source + steps) for source in range(c...  19 us
    pallas_call x2, Pallas kernels, long_part(): pl.pallas_call(long_kernel, grid=(channels // LANES,), in_specs=[by_token...  16.9 us
    ppermute x8, starting transfers between devices, shifted(): lax.ppermute(value, axis, [(source, source + steps) for source in range(c...  16.7 us
    unnamed x15, local copies, waits for them, and re-layouts  8.89 us
    all_gather x1, waiting for transfers between devices, on_device(): rows = lax.all_gather(weights, 'ctx')  6.73 us
  transfers between devices with their start and end apart: 11, of which 9 were waited for; matrix products, arithmetic and copies ran while one was open for 1% of the time, Pallas kernels for 19%

profile of v4, /device:TPU:16, one launch (start us, length us, event | category | flops | bytes accessed | tf_op | source)
XLA Modules:
  0.0 215.8 jit_solution(1265217123726994461)
XLA Ops:
  7.2 0.0 all-gather.3.cloned.1.call-start
  7.2 0.7 all-gather.3.cloned.1.call-update
  7.9 0.0 copy-start.3
  7.9 0.0 copy-start.5
  7.9 1.0 slice.4
  8.9 1.9 collective-permute-start
  10.8 6.0 %collective-permute-done.halo_ref = bf16[3,16,2048]{2,1,0:T(8,128)(2,1)S(1)} collective-permute-done((bf16[3,16,2048]{2,1,0:T(8,128)(2,1)S(1)}, bf16[3,16,2048]{2,1,0:T(8,128)(2,1)S(1)}, u32[]{:S(2)}, u32[]{:S(2)}) %collective-permute-start) | collective-permute-done | bytes 196640 | tf_op jit(solution)/shard_map/ppermute | solution.py:25
  16.8 0.0 copy-start
  16.8 3.8 %copy-done = bf16[512,3,2048]{2,0,1:T(8,128)(2,1)S(1)} copy-done((bf16[512,3,2048]{2,0,1:T(8,128)(2,1)S(1)}, bf16[512,3,2048]{2,0,1:T(8,128)(2,1)}, u32[]{:S(2)}) %copy-start) | copy-done | bytes 6291480
  20.6 0.0 copy-start.2
  20.6 0.9 copy-done.2
  21.5 0.0 copy-start.4
  21.5 0.9 copy-done.4
  22.4 20.1 %short_and_end_states.1 = (bf16[512,2048]{1,0:T(8,128)(2,1)S(1)}, f32[512,2048]{1,0:T(8,128)S(1)}, f32[8,16,2048]{2,1,0:T(8,128)S(1)}, f32[16,2048]{1,0:T(8,128)S(1)}) custom-call(bf16[3,512,2048]{2,1,0:T(8,128)(2,1)S(1)} %bitcast.8, bf16[3,16,2048]{2,1,0:T(8,128)(2,1)S(1)} %collective-permute-done.halo_ref, f32[3,7,2048]{2,1,0:T(8,128)S(1)} %copy-done.4, ...), custom_call_target="tpu_custom_call" | custom-call | flops 104857600 | bytes 13631488 | tf_op jit(solution)/shard_map/short_and_end_states/pallas_call | solution.py:101
  42.6 1.9 collective-permute-start.1
  44.5 2.5 %collective-permute-start.2 = (bf16[16,2048]{1,0:T(8,128)(2,1)S(1)}, bf16[16,2048]{1,0:T(8,128)(2,1)S(1)}, u32[]{:S(2)}, u32[]{:S(2)}) collective-permute-start(bf16[16,2048]{1,0:T(8,128)(2,1)S(1)} %convert_element_type.27), channel_id=1, source_target_pairs={{0,4},{2,6},{4,8},{6,10},{8,12},{10,14},{12,16},{14,18},{16,20},{1... | collective-permute-start | bytes 196616 | tf_op jit(solution)/shard_map/ppermute | solution.py:25
  47.0 4.4 %collective-permute-start.3 = (bf16[16,2048]{1,0:T(8,128)(2,1)S(1)}, bf16[16,2048]{1,0:T(8,128)(2,1)S(1)}, u32[]{:S(2)}, u32[]{:S(2)}) collective-permute-start(bf16[16,2048]{1,0:T(8,128)(2,1)S(1)} %convert_element_type.27), channel_id=1, source_target_pairs={{0,6},{2,8},{4,10},{6,12},{8,14},{10,16},{12,18},{14,20},{16,22},{... | collective-permute-start | bytes 196616 | tf_op jit(solution)/shard_map/ppermute | solution.py:25
  51.4 1.9 collective-permute-start.4
  53.4 0.0 collective-permute-done.1
  53.4 0.2 collective-permute-done.2
  53.5 1.0 collective-permute-done.3
  54.5 4.7 %collective-permute-done.4 = bf16[16,2048]{1,0:T(8,128)(2,1)S(1)} collective-permute-done((bf16[16,2048]{1,0:T(8,128)(2,1)S(1)}, bf16[16,2048]{1,0:T(8,128)(2,1)S(1)}, u32[]{:S(2)}, u32[]{:S(2)}) %collective-permute-start.4) | collective-permute-done | bytes 65568 | tf_op jit(solution)/shard_map/ppermute | solution.py:25
  59.2 0.1 fusion
  59.3 2.1 collective-permute-start.5
  61.4 1.3 collective-permute-start.6
  62.7 0.7 collective-permute-start.7
  63.4 5.0 %collective-permute-done.5 = bf16[16,2048]{1,0:T(8,128)(2,1)S(1)} collective-permute-done((bf16[16,2048]{1,0:T(8,128)(2,1)S(1)}, bf16[16,2048]{1,0:T(8,128)(2,1)S(1)}, u32[]{:S(2)}, u32[]{:S(2)}) %collective-permute-start.5) | collective-permute-done | bytes 65568 | tf_op jit(solution)/shard_map/ppermute | solution.py:25
  68.4 2.1 collective-permute-done.6
  70.5 0.0 collective-permute-done.7
  70.5 0.2 multiply_add_fusion.state_ref
  70.7 0.0 copy-done.3
  70.7 0.0 copy-done.5
  70.7 8.5 %modal_filter.2.refs_0_ = bf16[512,1024]{1,0:T(8,128)(2,1)S(1)} custom-call(bf16[512,2048]{1,0:T(8,128)(2,1)S(1)} %get-tuple-element.6.gated_ref, f32[512,2048]{1,0:T(8,128)S(1)} %get-tuple-element.7.first_ref, f32[8,16,2048]{2,1,0:T(8,128)S(1)} %get-tuple-element.8.enter_ref, f32[16,2048]{1,0:T(8,128)S(1)} %multiply_add_fusion.state_ref, ...), custom_call_target="tpu_custom_call" | custom-call | flops 52428800 | bytes 5242880 | tf_op jit(solution)/shard_map/modal_filter/pallas_call | solution.py:141
  79.2 0.0 copy-start.6
  79.2 8.5 %modal_filter.3.refs_1_ = bf16[512,1024]{1,0:T(8,128)(2,1)S(1)} custom-call(bf16[512,2048]{1,0:T(8,128)(2,1)S(1)} %get-tuple-element.6.gated_ref, f32[512,2048]{1,0:T(8,128)S(1)} %get-tuple-element.7.first_ref, f32[8,16,2048]{2,1,0:T(8,128)S(1)} %get-tuple-element.8.enter_ref, f32[16,2048]{1,0:T(8,128)S(1)} %multiply_add_fusion.state_ref, ...), custom_call_target="tpu_custom_call" | custom-call | flops 52428800 | bytes 5242880 | tf_op jit(solution)/shard_map/modal_filter/pallas_call | solution.py:141
  87.7 1.6 collective-permute-start.8
  89.2 0.5 collective-permute-start.9
  89.8 0.0 copy-done.6
  89.8 1.5 pad_maximum_fusion
  91.3 22.5 %collective-permute-done.8.refs_2_ = bf16[512,1024]{1,0:T(8,128)(2,1)S(1)} collective-permute-done((bf16[512,1024]{1,0:T(8,128)(2,1)S(1)}, bf16[512,1024]{1,0:T(8,128)(2,1)S(1)}, u32[]{:S(2)}, u32[]{:S(2)}) %collective-permute-start.8) | collective-permute-done | bytes 1048608 | tf_op jit(solution)/shard_map/ppermute | solution.py:443
  113.8 19.6 %collective-permute-done.9.refs_3_ = bf16[512,1024]{1,0:T(8,128)(2,1)} collective-permute-done((bf16[512,1024]{1,0:T(8,128)(2,1)S(1)}, bf16[512,1024]{1,0:T(8,128)(2,1)}, u32[]{:S(2)}, u32[]{:S(2)}) %collective-permute-start.9) | collective-permute-done | bytes 1048608 | tf_op jit(solution)/shard_map/ppermute | solution.py:443
  133.4 3.7 %norm.1.normed_ref = bf16[4,512,1024]{2,1,0:T(8,128)(2,1)S(1)} custom-call(s32[1]{0:T(128)} %bitcast.2.place_ref, bf16[512,1024]{1,0:T(8,128)(2,1)S(1)} %modal_filter.2.refs_0_, bf16[512,1024]{1,0:T(8,128)(2,1)S(1)} %modal_filter.3.refs_1_, bf16[512,1024]{1,0:T(8,128)(2,1)S(1)} %collective-permute-done.8.refs_2_, ...), custom_call_target="tpu_custom_call" | custom-call | flops 16777216 | bytes 8388608 | tf_op jit(solution)/shard_map/norm/pallas_call | solution.py:209
  137.1 0.0 copy-start.1
  137.1 2.0 copy-done.1
  139.1 6.7 %all-gather.3.cloned.1.call-done = bf16[48,256,1024]{2,1,0:T(8,128)(2,1)} async-done(((bf16[3,256,1024]{2,1,0:T(8,128)(2,1)}), bf16[48,256,1024]{2,1,0:T(8,128)(2,1)}) %all-gather.3.cloned.1.call-update) | async-done | bytes 25165840 | tf_op jit(solution)/shard_map/all_gather | solution.py:433
  145.8 61.3 %projections_and_attention.1 = bf16[4,512,256]{2,1,0:T(8,128)(2,1)S(1)} custom-call(bf16[4,512,1024]{2,1,0:T(8,128)(2,1)} %copy-done.1, bf16[16,3,256,1024]{3,2,1,0:T(8,128)(2,1)} %bitcast.14), custom_call_target="tpu_custom_call" | custom-call | flops 12884901888 | bytes 25165824 | tf_op jit(solution)/shard_map/projections_and_attention/pallas_call | solution.py:402
  207.1 0.5 copy.11
  207.6 1.3 copy.12
  (2 shorter events, 0.0 us)
Async XLA Ops:
  7.2 138.6 %all-gather.3.cloned.1.call-start = ((), (), s32[]{:S(2)}) async-start(), calls=%async_computation | async-start | bytes 26738688 | tf_op jit(solution)/shard_map/all_gather | solution.py:433
  7.9 62.8 %copy-start.3 = (f32[16,2048]{1,0:T(8,128)S(1)}, f32[16,2048]{1,0:T(8,128)}, u32[]{:S(2)}) copy-start(f32[16,2048]{1,0:T(8,128)} %residue_ref.3) | copy-start | bytes 393220
  7.9 62.8 %copy-start.5 = (f32[2048]{0:T(1024)S(1)}, f32[2048]{0:T(1024)}, u32[]{:S(2)}) copy-start(f32[2048]{0:T(1024)} %param.11) | copy-start | bytes 24580
  8.9 7.9 %collective-permute-start = (bf16[3,16,2048]{2,1,0:T(8,128)(2,1)S(1)}, bf16[3,16,2048]{2,1,0:T(8,128)(2,1)S(1)}, u32[]{:S(2)}, u32[]{:S(2)}) collective-permute-start(bf16[3,16,2048]{2,1,0:T(8,128)(2,1)S(1)} %slice.4), channel_id=1, source_target_pairs={{0,2},{2,4},{4,6},{6,8},{8,10},{10,12},{12,14},{14,16},{16,18},{18... | collective-permute-start | bytes 589832 | tf_op jit(solution)/shard_map/ppermute | solution.py:25
  16.8 3.8 %copy-start = (bf16[512,3,2048]{2,0,1:T(8,128)(2,1)S(1)}, bf16[512,3,2048]{2,0,1:T(8,128)(2,1)}, u32[]{:S(2)}) copy-start(bf16[512,3,2048]{2,0,1:T(8,128)(2,1)} %param.7) | copy-start | bytes 18874372
  20.6 0.9 copy-start.2
  21.5 0.9 copy-start.4
  42.6 10.8 %collective-permute-start.1 = (bf16[16,2048]{1,0:T(8,128)(2,1)S(1)}, bf16[16,2048]{1,0:T(8,128)(2,1)S(1)}, u32[]{:S(2)}, u32[]{:S(2)}) collective-permute-start(bf16[16,2048]{1,0:T(8,128)(2,1)S(1)} %convert_element_type.27), channel_id=1, source_target_pairs={{0,2},{2,4},{4,6},{6,8},{8,10},{10,12},{12,14},{14,16},{16,18},{18... | collective-permute-start | bytes 196616 | tf_op jit(solution)/shard_map/ppermute | solution.py:25
  44.5 9.0 %collective-permute-start.2 = (bf16[16,2048]{1,0:T(8,128)(2,1)S(1)}, bf16[16,2048]{1,0:T(8,128)(2,1)S(1)}, u32[]{:S(2)}, u32[]{:S(2)}) collective-permute-start(bf16[16,2048]{1,0:T(8,128)(2,1)S(1)} %convert_element_type.27), channel_id=1, source_target_pairs={{0,4},{2,6},{4,8},{6,10},{8,12},{10,14},{12,16},{14,18},{16,20},{1... | collective-permute-start | bytes 196616 | tf_op jit(solution)/shard_map/ppermute | solution.py:25
  47.0 7.5 %collective-permute-start.3 = (bf16[16,2048]{1,0:T(8,128)(2,1)S(1)}, bf16[16,2048]{1,0:T(8,128)(2,1)S(1)}, u32[]{:S(2)}, u32[]{:S(2)}) collective-permute-start(bf16[16,2048]{1,0:T(8,128)(2,1)S(1)} %convert_element_type.27), channel_id=1, source_target_pairs={{0,6},{2,8},{4,10},{6,12},{8,14},{10,16},{12,18},{14,20},{16,22},{... | collective-permute-start | bytes 196616 | tf_op jit(solution)/shard_map/ppermute | solution.py:25
  51.4 7.8 %collective-permute-start.4 = (bf16[16,2048]{1,0:T(8,128)(2,1)S(1)}, bf16[16,2048]{1,0:T(8,128)(2,1)S(1)}, u32[]{:S(2)}, u32[]{:S(2)}) collective-permute-start(bf16[16,2048]{1,0:T(8,128)(2,1)S(1)} %convert_element_type.27), channel_id=1, source_target_pairs={{0,8},{2,10},{4,12},{6,14},{8,16},{10,18},{12,20},{14,22},{16,24},... | collective-permute-start | bytes 196616 | tf_op jit(solution)/shard_map/ppermute | solution.py:25
  59.3 9.1 %collective-permute-start.5 = (bf16[16,2048]{1,0:T(8,128)(2,1)S(1)}, bf16[16,2048]{1,0:T(8,128)(2,1)S(1)}, u32[]{:S(2)}, u32[]{:S(2)}) collective-permute-start(bf16[16,2048]{1,0:T(8,128)(2,1)S(1)} %fusion), channel_id=1, source_target_pairs={{0,8},{2,10},{4,12},{6,14},{8,16},{10,18},{12,20},{14,22},{16,24},... | collective-permute-start | bytes 196616 | tf_op jit(solution)/shard_map/ppermute | solution.py:25
  61.4 9.1 %collective-permute-start.6 = (bf16[16,2048]{1,0:T(8,128)(2,1)S(1)}, bf16[16,2048]{1,0:T(8,128)(2,1)S(1)}, u32[]{:S(2)}, u32[]{:S(2)}) collective-permute-start(bf16[16,2048]{1,0:T(8,128)(2,1)S(1)} %fusion), channel_id=1, source_target_pairs={{0,16},{2,18},{4,20},{6,22},{8,24},{10,26},{12,28},{14,30},{1,17},... | collective-permute-start | bytes 196616 | tf_op jit(solution)/shard_map/ppermute | solution.py:25
  62.7 7.8 %collective-permute-start.7 = (bf16[16,2048]{1,0:T(8,128)(2,1)S(1)}, bf16[16,2048]{1,0:T(8,128)(2,1)S(1)}, u32[]{:S(2)}, u32[]{:S(2)}) collective-permute-start(bf16[16,2048]{1,0:T(8,128)(2,1)S(1)} %fusion), channel_id=1, source_target_pairs={{0,24},{2,26},{4,28},{6,30},{1,25},{3,27},{5,29},{7,31}} | collective-permute-start | bytes 196616 | tf_op jit(solution)/shard_map/ppermute | solution.py:25
  79.2 10.6 %copy-start.6 = (f32[4096]{0:T(1024)S(1)}, f32[4096]{0:T(1024)}, u32[]{:S(2)}) copy-start(f32[4096]{0:T(1024)} %param.12) | copy-start | bytes 49156
  87.7 26.2 %collective-permute-start.8 = (bf16[512,1024]{1,0:T(8,128)(2,1)S(1)}, bf16[512,1024]{1,0:T(8,128)(2,1)S(1)}, u32[]{:S(2)}, u32[]{:S(2)}) collective-permute-start(bf16[512,1024]{1,0:T(8,128)(2,1)S(1)} %modal_filter.2.refs_0_), channel_id=1, source_target_pairs={{0,1},{1,0},{2,3},{3,2},{4,5},{5,4},{6,7},{7,6},{8,9},{9,8},{10,11... | collective-permute-start | bytes 3145736 | tf_op jit(solution)/shard_map/ppermute | solution.py:443
  89.2 44.2 %collective-permute-start.9 = (bf16[512,1024]{1,0:T(8,128)(2,1)S(1)}, bf16[512,1024]{1,0:T(8,128)(2,1)}, u32[]{:S(2)}, u32[]{:S(2)}) collective-permute-start(bf16[512,1024]{1,0:T(8,128)(2,1)S(1)} %modal_filter.3.refs_1_), channel_id=1, source_target_pairs={{0,1},{1,0},{2,3},{3,2},{4,5},{5,4},{6,7},{7,6},{8,9},{9,8},{10,11... | collective-permute-start | bytes 3145736 | tf_op jit(solution)/shard_map/ppermute | solution.py:443
  137.1 2.0 copy-start.1
Sparse Core Ops, SparseCore 0:
  9.6 136.1 all-gather.2

commit v5 on v4

--- a/solution.py
+++ b/solution.py
@@ -169,17 +169,12 @@
     def power(k):
         return jnp.exp(-float(k * tokens) * decay_rate)
 
-    def from_before(value, steps):
-        return shifted(value, "ctx", steps).astype(jnp.float32)
-
-    sent = ends.astype(jnp.bfloat16)
-    near = from_before(sent, 1)
-    for j in range(2, min(RADIX, count - 1) + 1):
-        near = near + power(j - 1) * from_before(sent, j)
-    state = near
-    sent = near.astype(jnp.bfloat16)
-    for m in range(RADIX, count, RADIX):
-        state = state + power(m) * from_before(sent, m)
+    state = shifted(ends, "ctx", 1)
+    step = 1
+    while step < count:
+        sent = state if step < RADIX else state.astype(jnp.bfloat16)
+        state = state + power(step) * shifted(sent, "ctx", step).astype(jnp.float32)
+        step *= 2
     return state
 
 

time: 218 us -> 223 us (1.023)
  waiting for transfers between devices: 68.5 us -> 80.9 us
  starting transfers between devices: 18.8 us -> 14.7 us
    ppermute x8 -> x6, waiting for transfers between devices: 19 us -> 41.9 us  [shifted(): lax.ppermute(value, axis, [(source, source + steps) for source in range(c...]
    all_gather x1, waiting for transfers between devices: 6.73 us -> 0.01 us  [on_device(): rows = lax.all_gather(weights, 'ctx')]
    ppermute x8 -> x6, starting transfers between devices: 16.7 us -> 12.6 us  [shifted(): lax.ppermute(value, axis, [(source, source + steps) for source in range(c...]
    ppermute x2, waiting for transfers between devices: 42.1 us -> 38.3 us  [on_device(): others[step - 1].append(lax.ppermute(own[-1], 'tp', source))]
  transfers between devices with their start and end apart: 11 -> 9, of which waited for: 9 -> 8; matrix products, arithmetic and copies ran while one was open for 1% -> 1% of each run, Pallas kernels for 19% -> 18%
where the time goes in v5:
time: 223 us; the launch traced here: 222 us
  Pallas kernels  99.9 us (45%)
  waiting for transfers between devices  80.9 us (36%)
  starting transfers between devices  14.7 us (7%)
  between operations  14.2 us (6%)
  local copies, waits for them, and re-layouts  10.4 us (5%)
    pallas_call x1, Pallas kernels, attention_part(): pl.pallas_call(attention_kernel, in_specs=[pl.BlockSpec(memory_space=pltp...  59.1 us
    ppermute x6, waiting for transfers between devices, shifted(): lax.ppermute(value, axis, [(source, source + steps) for source in range(c...  41.9 us
    ppermute x2, waiting for transfers between devices, on_device(): others[step - 1].append(lax.ppermute(own[-1], 'tp', source))  38.3 us
    pallas_call x1, Pallas kernels, short_part(): pl.pallas_call(short_kernel, grid=(channels // LANES,), in_specs=[pl.Bloc...  20.1 us
    pallas_call x2, Pallas kernels, long_part(): pl.pallas_call(long_kernel, grid=(channels // LANES,), in_specs=[by_token...  16.9 us
    ppermute x6, starting transfers between devices, shifted(): lax.ppermute(value, axis, [(source, source + steps) for source in range(c...  12.6 us
    unnamed x15, local copies, waits for them, and re-layouts  8.88 us
  transfers between devices with their start and end apart: 9, of which 8 were waited for; matrix products, arithmetic and copies ran while one was open for 1% of the time, Pallas kernels for 18%

profile of v5, /device:TPU:16, one launch (start us, length us, event | category | flops | bytes accessed | tf_op | source)
XLA Modules:
  0.0 221.8 jit_solution(12063437656344062786)
XLA Ops:
  7.2 0.0 all-gather.3.cloned.1.call-start
  7.2 0.7 all-gather.3.cloned.1.call-update
  7.9 0.0 copy-start.3
  7.9 0.0 copy-start.5
  7.9 1.0 slice.4
  8.9 1.9 collective-permute-start
  10.8 6.0 %collective-permute-done.halo_ref = bf16[3,16,2048]{2,1,0:T(8,128)(2,1)S(1)} collective-permute-done((bf16[3,16,2048]{2,1,0:T(8,128)(2,1)S(1)}, bf16[3,16,2048]{2,1,0:T(8,128)(2,1)S(1)}, u32[]{:S(2)}, u32[]{:S(2)}) %collective-permute-start) | collective-permute-done | bytes 196640 | tf_op jit(solution)/shard_map/ppermute | solution.py:25
  16.8 0.0 copy-start
  16.8 3.8 %copy-done = bf16[512,3,2048]{2,0,1:T(8,128)(2,1)S(1)} copy-done((bf16[512,3,2048]{2,0,1:T(8,128)(2,1)S(1)}, bf16[512,3,2048]{2,0,1:T(8,128)(2,1)}, u32[]{:S(2)}) %copy-start) | copy-done | bytes 6291480
  20.6 0.0 copy-start.1
  20.6 0.9 copy-done.1
  21.5 0.0 copy-start.4
  21.5 0.9 copy-done.4
  22.4 20.1 %short_and_end_states.1 = (bf16[512,2048]{1,0:T(8,128)(2,1)S(1)}, f32[512,2048]{1,0:T(8,128)S(1)}, f32[8,16,2048]{2,1,0:T(8,128)S(1)}, f32[16,2048]{1,0:T(8,128)S(1)}) custom-call(bf16[3,512,2048]{2,1,0:T(8,128)(2,1)S(1)} %bitcast.8, bf16[3,16,2048]{2,1,0:T(8,128)(2,1)S(1)} %collective-permute-done.halo_ref, f32[3,7,2048]{2,1,0:T(8,128)S(1)} %copy-done.4, ...), custom_call_target="tpu_custom_call" | custom-call | flops 104857600 | bytes 13631488 | tf_op jit(solution)/shard_map/short_and_end_states/pallas_call | solution.py:101
  42.5 1.9 collective-permute-start.1
  44.5 8.0 %collective-permute-done.1 = f32[16,2048]{1,0:T(8,128)S(1)} collective-permute-done((f32[16,2048]{1,0:T(8,128)S(1)}, f32[16,2048]{1,0:T(8,128)S(1)}, u32[]{:S(2)}, u32[]{:S(2)}) %collective-permute-start.1) | collective-permute-done | bytes 131104 | tf_op jit(solution)/shard_map/ppermute | solution.py:25
  52.5 1.9 collective-permute-start.2
  54.4 8.0 %collective-permute-done.2 = f32[16,2048]{1,0:T(8,128)S(1)} collective-permute-done((f32[16,2048]{1,0:T(8,128)S(1)}, f32[16,2048]{1,0:T(8,128)S(1)}, u32[]{:S(2)}, u32[]{:S(2)}) %collective-permute-start.2) | collective-permute-done | bytes 131104 | tf_op jit(solution)/shard_map/ppermute | solution.py:25
  62.5 1.9 collective-permute-start.3
  64.4 8.8 %collective-permute-done.3 = f32[16,2048]{1,0:T(8,128)S(1)} collective-permute-done((f32[16,2048]{1,0:T(8,128)S(1)}, f32[16,2048]{1,0:T(8,128)S(1)}, u32[]{:S(2)}, u32[]{:S(2)}) %collective-permute-start.3) | collective-permute-done | bytes 131104 | tf_op jit(solution)/shard_map/ppermute | solution.py:25
  73.3 3.6 %collective-permute-start.4 = (bf16[16,2048]{1,0:T(8,128)(2,1)S(1)}, bf16[16,2048]{1,0:T(8,128)(2,1)S(1)}, u32[]{:S(2)}, u32[]{:S(2)}) collective-permute-start(bf16[16,2048]{1,0:T(8,128)(2,1)S(1)} %fusion.1), channel_id=1, source_target_pairs={{0,8},{2,10},{4,12},{6,14},{8,16},{10,18},{12,20},{14,22},{16,24},... | collective-permute-start | bytes 196616 | tf_op jit(solution)/shard_map/ppermute | solution.py:25
  76.9 3.9 %collective-permute-done.4 = bf16[16,2048]{1,0:T(8,128)(2,1)S(1)} collective-permute-done((bf16[16,2048]{1,0:T(8,128)(2,1)S(1)}, bf16[16,2048]{1,0:T(8,128)(2,1)S(1)}, u32[]{:S(2)}, u32[]{:S(2)}) %collective-permute-start.4) | collective-permute-done | bytes 65568 | tf_op jit(solution)/shard_map/ppermute | solution.py:25
  80.8 0.1 fusion
  80.9 1.3 collective-permute-start.5
  82.2 7.1 %collective-permute-done.5 = bf16[16,2048]{1,0:T(8,128)(2,1)S(1)} collective-permute-done((bf16[16,2048]{1,0:T(8,128)(2,1)S(1)}, bf16[16,2048]{1,0:T(8,128)(2,1)S(1)}, u32[]{:S(2)}, u32[]{:S(2)}) %collective-permute-start.5) | collective-permute-done | bytes 65568 | tf_op jit(solution)/shard_map/ppermute | solution.py:25
  89.3 0.1 multiply_add_fusion.state_ref
  89.4 0.0 copy-done.3
  89.4 0.0 copy-done.5
  89.4 8.5 %modal_filter.2.refs_0_ = bf16[512,1024]{1,0:T(8,128)(2,1)S(1)} custom-call(bf16[512,2048]{1,0:T(8,128)(2,1)S(1)} %get-tuple-element.6.gated_ref, f32[512,2048]{1,0:T(8,128)S(1)} %get-tuple-element.7.first_ref, f32[8,16,2048]{2,1,0:T(8,128)S(1)} %get-tuple-element.8.enter_ref, f32[16,2048]{1,0:T(8,128)S(1)} %multiply_add_fusion.state_ref, ...), custom_call_target="tpu_custom_call" | custom-call | flops 52428800 | bytes 5242880 | tf_op jit(solution)/shard_map/modal_filter/pallas_call | solution.py:141
  97.9 0.0 copy-start.6
  97.9 8.5 %modal_filter.3.refs_1_ = bf16[512,1024]{1,0:T(8,128)(2,1)S(1)} custom-call(bf16[512,2048]{1,0:T(8,128)(2,1)S(1)} %get-tuple-element.6.gated_ref, f32[512,2048]{1,0:T(8,128)S(1)} %get-tuple-element.7.first_ref, f32[8,16,2048]{2,1,0:T(8,128)S(1)} %get-tuple-element.8.enter_ref, f32[16,2048]{1,0:T(8,128)S(1)} %multiply_add_fusion.state_ref, ...), custom_call_target="tpu_custom_call" | custom-call | flops 52428800 | bytes 5242880 | tf_op jit(solution)/shard_map/modal_filter/pallas_call | solution.py:141
  106.4 1.5 collective-permute-start.6
  107.9 0.6 collective-permute-start.7
  108.5 0.0 copy-done.6
  108.5 1.5 pad_maximum_fusion
  110.0 22.5 %collective-permute-done.6.refs_2_ = bf16[512,1024]{1,0:T(8,128)(2,1)S(1)} collective-permute-done((bf16[512,1024]{1,0:T(8,128)(2,1)S(1)}, bf16[512,1024]{1,0:T(8,128)(2,1)S(1)}, u32[]{:S(2)}, u32[]{:S(2)}) %collective-permute-start.6) | collective-permute-done | bytes 1048608 | tf_op jit(solution)/shard_map/ppermute | solution.py:438
  132.5 15.8 %collective-permute-done.7.refs_3_ = bf16[512,1024]{1,0:T(8,128)(2,1)} collective-permute-done((bf16[512,1024]{1,0:T(8,128)(2,1)S(1)}, bf16[512,1024]{1,0:T(8,128)(2,1)}, u32[]{:S(2)}, u32[]{:S(2)}) %collective-permute-start.7) | collective-permute-done | bytes 1048608 | tf_op jit(solution)/shard_map/ppermute | solution.py:438
  148.3 3.7 %norm.1.normed_ref = bf16[4,512,1024]{2,1,0:T(8,128)(2,1)S(1)} custom-call(s32[1]{0:T(128)} %bitcast.2.place_ref, bf16[512,1024]{1,0:T(8,128)(2,1)S(1)} %modal_filter.2.refs_0_, bf16[512,1024]{1,0:T(8,128)(2,1)S(1)} %modal_filter.3.refs_1_, bf16[512,1024]{1,0:T(8,128)(2,1)S(1)} %collective-permute-done.6.refs_2_, ...), custom_call_target="tpu_custom_call" | custom-call | flops 16777216 | bytes 8388608 | tf_op jit(solution)/shard_map/norm/pallas_call | solution.py:204
  152.0 0.0 copy-start.2
  152.0 2.0 copy-done.2
  153.9 0.0 all-gather.3.cloned.1.call-done
  153.9 59.1 %projections_and_attention.1 = bf16[4,512,256]{2,1,0:T(8,128)(2,1)S(1)} custom-call(bf16[4,512,1024]{2,1,0:T(8,128)(2,1)} %copy-done.2, bf16[16,3,256,1024]{3,2,1,0:T(8,128)(2,1)} %bitcast.14), custom_call_target="tpu_custom_call" | custom-call | flops 12884901888 | bytes 25165824 | tf_op jit(solution)/shard_map/projections_and_attention/pallas_call | solution.py:397
  213.1 0.5 copy.11
  213.6 1.3 copy.12
  (3 shorter events, 0.1 us)
Async XLA Ops:
  7.2 146.8 %all-gather.3.cloned.1.call-start = ((), (), s32[]{:S(2)}) async-start(), calls=%async_computation | async-start | bytes 26738688 | tf_op jit(solution)/shard_map/all_gather | solution.py:428
  7.9 81.5 %copy-start.3 = (f32[16,2048]{1,0:T(8,128)S(1)}, f32[16,2048]{1,0:T(8,128)}, u32[]{:S(2)}) copy-start(f32[16,2048]{1,0:T(8,128)} %residue_ref.3) | copy-start | bytes 393220
  7.9 81.5 %copy-start.5 = (f32[2048]{0:T(1024)S(1)}, f32[2048]{0:T(1024)}, u32[]{:S(2)}) copy-start(f32[2048]{0:T(1024)} %param.11) | copy-start | bytes 24580
  8.9 7.9 %collective-permute-start = (bf16[3,16,2048]{2,1,0:T(8,128)(2,1)S(1)}, bf16[3,16,2048]{2,1,0:T(8,128)(2,1)S(1)}, u32[]{:S(2)}, u32[]{:S(2)}) collective-permute-start(bf16[3,16,2048]{2,1,0:T(8,128)(2,1)S(1)} %slice.4), channel_id=1, source_target_pairs={{0,2},{2,4},{4,6},{6,8},{8,10},{10,12},{12,14},{14,16},{16,18},{18... | collective-permute-start | bytes 589832 | tf_op jit(solution)/shard_map/ppermute | solution.py:25
  16.8 3.8 %copy-start = (bf16[512,3,2048]{2,0,1:T(8,128)(2,1)S(1)}, bf16[512,3,2048]{2,0,1:T(8,128)(2,1)}, u32[]{:S(2)}) copy-start(bf16[512,3,2048]{2,0,1:T(8,128)(2,1)} %param.7) | copy-start | bytes 18874372
  20.6 0.9 copy-start.1
  21.5 0.9 copy-start.4
  42.5 10.0 %collective-permute-start.1 = (f32[16,2048]{1,0:T(8,128)S(1)}, f32[16,2048]{1,0:T(8,128)S(1)}, u32[]{:S(2)}, u32[]{:S(2)}) collective-permute-start(f32[16,2048]{1,0:T(8,128)S(1)} %get-tuple-element.9), channel_id=1, source_target_pairs={{0,2},{2,4},{4,6},{6,8},{8,10},{10,12},{12,14},{14,16},{16,18},{18... | collective-permute-start | bytes 393224 | tf_op jit(solution)/shard_map/ppermute | solution.py:25
  52.5 10.0 %collective-permute-start.2 = (f32[16,2048]{1,0:T(8,128)S(1)}, f32[16,2048]{1,0:T(8,128)S(1)}, u32[]{:S(2)}, u32[]{:S(2)}) collective-permute-start(f32[16,2048]{1,0:T(8,128)S(1)} %collective-permute-done.1), channel_id=1, source_target_pairs={{0,2},{2,4},{4,6},{6,8},{8,10},{10,12},{12,14},{14,16},{16,18},{18... | collective-permute-start | bytes 393224 | tf_op jit(solution)/shard_map/ppermute | solution.py:25
  62.5 10.7 %collective-permute-start.3 = (f32[16,2048]{1,0:T(8,128)S(1)}, f32[16,2048]{1,0:T(8,128)S(1)}, u32[]{:S(2)}, u32[]{:S(2)}) collective-permute-start(f32[16,2048]{1,0:T(8,128)S(1)} %multiply_add_fusion.3), channel_id=1, source_target_pairs={{0,4},{2,6},{4,8},{6,10},{8,12},{10,14},{12,16},{14,18},{16,20},{1... | collective-permute-start | bytes 393224 | tf_op jit(solution)/shard_map/ppermute | solution.py:25
  73.3 7.5 %collective-permute-start.4 = (bf16[16,2048]{1,0:T(8,128)(2,1)S(1)}, bf16[16,2048]{1,0:T(8,128)(2,1)S(1)}, u32[]{:S(2)}, u32[]{:S(2)}) collective-permute-start(bf16[16,2048]{1,0:T(8,128)(2,1)S(1)} %fusion.1), channel_id=1, source_target_pairs={{0,8},{2,10},{4,12},{6,14},{8,16},{10,18},{12,20},{14,22},{16,24},... | collective-permute-start | bytes 196616 | tf_op jit(solution)/shard_map/ppermute | solution.py:25
  80.9 8.4 %collective-permute-start.5 = (bf16[16,2048]{1,0:T(8,128)(2,1)S(1)}, bf16[16,2048]{1,0:T(8,128)(2,1)S(1)}, u32[]{:S(2)}, u32[]{:S(2)}) collective-permute-start(bf16[16,2048]{1,0:T(8,128)(2,1)S(1)} %fusion), channel_id=1, source_target_pairs={{0,16},{2,18},{4,20},{6,22},{8,24},{10,26},{12,28},{14,30},{1,17},... | collective-permute-start | bytes 196616 | tf_op jit(solution)/shard_map/ppermute | solution.py:25
  97.9 10.6 %copy-start.6 = (f32[4096]{0:T(1024)S(1)}, f32[4096]{0:T(1024)}, u32[]{:S(2)}) copy-start(f32[4096]{0:T(1024)} %param.12) | copy-start | bytes 49156
  106.4 26.2 %collective-permute-start.6 = (bf16[512,1024]{1,0:T(8,128)(2,1)S(1)}, bf16[512,1024]{1,0:T(8,128)(2,1)S(1)}, u32[]{:S(2)}, u32[]{:S(2)}) collective-permute-start(bf16[512,1024]{1,0:T(8,128)(2,1)S(1)} %modal_filter.2.refs_0_), channel_id=1, source_target_pairs={{0,1},{1,0},{2,3},{3,2},{4,5},{5,4},{6,7},{7,6},{8,9},{9,8},{10,11... | collective-permute-start | bytes 3145736 | tf_op jit(solution)/shard_map/ppermute | solution.py:438
  107.9 40.4 %collective-permute-start.7 = (bf16[512,1024]{1,0:T(8,128)(2,1)S(1)}, bf16[512,1024]{1,0:T(8,128)(2,1)}, u32[]{:S(2)}, u32[]{:S(2)}) collective-permute-start(bf16[512,1024]{1,0:T(8,128)(2,1)S(1)} %modal_filter.3.refs_1_), channel_id=1, source_target_pairs={{0,1},{1,0},{2,3},{3,2},{4,5},{5,4},{6,7},{7,6},{8,9},{9,8},{10,11... | collective-permute-start | bytes 3145736 | tf_op jit(solution)/shard_map/ppermute | solution.py:438
  152.0 2.0 copy-start.2
Sparse Core Ops, SparseCore 0:
  9.6 132.6 all-gather.2
